TPU v7x, 32 devices: a whole 2x2x4 slice. The times are simulated.
32 devices in a mesh: space: 16 (over z, x, core), mode: 2 (over y).
Axes of the slice: x: 2, y: 2, z: 4, core: 2. Of those that a mesh axis runs over, the one named last changes fastest.
Arguments:
- eigvecs: bfloat16 [2, 512, 12, 384], P(None, 'space'), may hold values from -0.56640625 to 0.56640625
- solutions: bfloat16 [2, 512, 12, 384], P(None, 'space', None, 'mode'), may hold values from -0.56640625 to 0.56640625
- momenta: int32 [8, 3], replicated, may hold values from -3 to 3
- gammas: int32 [4], replicated, may hold values from 0 to 15
Outputs:
- fields: float32 [12288, 2, 384], P('space', None, 'mode')
- traces: float32 [4, 4, 8, 2], replicated
All inputs are finite; a program needn't handle non-finite values.
Results may differ from a plain program's by a relative error of at most 0.0029.
Values may be sent and summed in bfloat16 or wider, within the bound.
No kernel may reach another device: no remote copies, remote signals or barrier semaphores. Data moves between devices by JAX's collectives and lax.ppermute only.
A program may use at most 128 MiB of HBM per device.

v0:
```python
import math

import jax
import jax.numpy as jnp
import numpy as np
from jax import lax
from jax.sharding import PartitionSpec as P

LATT = 96


def shifted(x, axis, by):
    count = lax.axis_size(axis)
    return lax.ppermute(x, axis, [(i, (i + by) % count) for i in range(count)])


def gamma_table():
    unit = 1j
    first = np.array([[0, 0, 0, unit], [0, 0, unit, 0], [0, -unit, 0, 0], [-unit, 0, 0, 0]])
    second = np.array([[0, 0, 0, -1], [0, 0, 1, 0], [0, 1, 0, 0], [-1, 0, 0, 0]], dtype=complex)
    third = np.array([[0, 0, unit, 0], [0, 0, 0, -unit], [-unit, 0, 0, 0], [0, unit, 0, 0]])
    fourth = np.array([[0, 0, 1, 0], [0, 0, 0, 1], [1, 0, 0, 0], [0, 1, 0, 0]], dtype=complex)
    basis = [first, second, third, fourth]
    table = []
    for number in range(16):
        matrix = np.eye(4, dtype=complex)
        for bit_pos in range(4):
            if number >> bit_pos & 1:
                matrix = matrix @ basis[bit_pos]
        table.append(matrix)
    table = np.stack(table)
    return (table.real.astype(np.float32), table.imag.astype(np.float32))


def select_gammas(gammas):
    table_re, table_im = gamma_table()
    select = (gammas[:, None] == jnp.arange(16, dtype=jnp.int32)[None, :]).astype(jnp.float32)
    count = gammas.shape[0]
    real_part = jnp.dot(
        select, jnp.asarray(table_re).reshape(16, 16), precision=lax.Precision.HIGHEST
    ).reshape(count, 4, 4)
    imag_part = jnp.dot(
        select, jnp.asarray(table_im).reshape(16, 16), precision=lax.Precision.HIGHEST
    ).reshape(count, 4, 4)
    return (real_part, imag_part)


def phases(momenta, first_site, count):
    index = first_site + jnp.arange(count, dtype=jnp.int32)
    coord_x = index // (LATT * LATT)
    coord_y = index // LATT % LATT
    coord_z = index % LATT
    phase_int = (
        momenta[:, 0:1] * coord_x[None, :]
        + momenta[:, 1:2] * coord_y[None, :]
        + momenta[:, 2:3] * coord_z[None, :]
    ) % LATT
    theta = 2.0 * math.pi / LATT * phase_int.astype(jnp.float32)
    return (jnp.cos(theta), jnp.sin(theta))


def left_side(vectors, cosine, sine_part):
    vec_re = vectors[0].astype(jnp.float32)[None]
    vec_im = vectors[1].astype(jnp.float32)[None]
    cosine = cosine[:, :, None, None]
    sine_part = sine_part[:, :, None, None]
    left_re = cosine * vec_re - sine_part * vec_im
    left_im = -(sine_part * vec_re + cosine * vec_im)
    return jnp.stack([left_re, left_im], 1).astype(jnp.bfloat16)


def right_side(vectors, gamma_re, gamma_im):
    count = vectors.shape[1]
    width = vectors.shape[3]
    sol_re = vectors[0].astype(jnp.float32).reshape(count, 4, 3, width)
    sol_im = vectors[1].astype(jnp.float32).reshape(count, 4, 3, width)
    high = lax.Precision.HIGHEST
    rot_re = jnp.einsum("gst,xtcj->gxscj", gamma_re, sol_re, precision=high) - jnp.einsum(
        "gst,xtcj->gxscj", gamma_im, sol_im, precision=high
    )
    rot_im = jnp.einsum("gst,xtcj->gxscj", gamma_re, sol_im, precision=high) + jnp.einsum(
        "gst,xtcj->gxscj", gamma_im, sol_re, precision=high
    )
    groups = gamma_re.shape[0]
    rot_re = rot_re.reshape(groups, count, 12, width)
    rot_im = rot_im.reshape(groups, count, 12, width)
    upper = jnp.stack([rot_re, rot_im], 3)
    lower = jnp.stack([-rot_im, rot_re], 3)
    return jnp.stack([upper, lower], 1).astype(jnp.bfloat16)


def body(eigvecs, solutions, momenta, gammas):
    local_sites = eigvecs.shape[1]
    vec_count = eigvecs.shape[3]
    col_count = solutions.shape[3]
    groups = gammas.shape[0]
    mom_count = momenta.shape[0]
    device = lax.axis_index("space")
    space_count = lax.axis_size("space")
    gamma_re, gamma_im = select_gammas(gammas)
    cosine, sine_part = phases(momenta, device * local_sites, local_sites)
    left = left_side(eigvecs, cosine, sine_part)
    right = right_side(solutions, gamma_re, gamma_im)
    partial_fields = jnp.einsum(
        "paxci,gaxcrj->gpirj", left, right, preferred_element_type=jnp.float32
    )
    partial_fields = partial_fields.reshape(groups * mom_count * vec_count, 2, col_count)
    fields = lax.psum_scatter(partial_fields, "space", scatter_dimension=0, tiled=True)
    own_rows = fields.shape[0]
    spacing = space_count // groups
    own_gamma = device // spacing
    row_index = device * own_rows + jnp.arange(own_rows, dtype=jnp.int32)
    row_mom = row_index % (mom_count * vec_count) // vec_count
    mom_onehot = (row_mom[:, None] == jnp.arange(mom_count, dtype=jnp.int32)[None, :]).astype(
        jnp.float32
    )
    gamma_range = jnp.arange(groups, dtype=jnp.int32)

    def pair_terms(first_rows, second_rows):
        real_sum = jnp.sum(
            first_rows[:, 0] * second_rows[:, 0] + first_rows[:, 1] * second_rows[:, 1], -1
        )
        imag_sum = jnp.sum(
            first_rows[:, 1] * second_rows[:, 0] - first_rows[:, 0] * second_rows[:, 1], -1
        )
        return jnp.dot(
            mom_onehot.T, jnp.stack([real_sum, imag_sum], 1), precision=lax.Precision.HIGHEST
        )

    def place(row_gamma, col_gamma, values):
        row_hot = (gamma_range == row_gamma).astype(jnp.float32)
        col_hot = (gamma_range == col_gamma).astype(jnp.float32)
        return row_hot[:, None, None, None] * col_hot[None, :, None, None] * values[None, None]

    total = place(own_gamma, own_gamma, pair_terms(fields, fields))
    last_shift = groups - 1
    for step in range(1, last_shift + 1):
        other = shifted(fields.astype(jnp.bfloat16), "space", step * spacing).astype(fields.dtype)
        values = pair_terms(fields, other)
        other_gamma = (own_gamma - step) % groups
        total = total + place(own_gamma, other_gamma, values)
    traces = lax.psum(total, ("space", "mode")) / float(vec_count * vec_count)
    return (fields, traces)


def solution(mesh):
    return jax.shard_map(
        body,
        mesh=mesh,
        in_specs=(P(None, "space", None, None), P(None, "space", None, "mode"), P(), P()),
        out_specs=(P("space", None, "mode"), P()),
        check_vma=False,
    )
```

profile of v0, /device:TPU:0, one launch (start us, length us, event | category | flops | bytes accessed | tf_op | source)
XLA Modules:
  0.0 375.1 jit_solution(10506076556761638614)
XLA Ops:
  7.3 0.8 slice_bitcast_fusion.2
  8.1 1.2 bitcast_convert_fusion.1
  9.3 1.1 fusion.63
  10.4 0.2 convolution_bitcast_fusion.2
  10.6 0.3 convolution_bitcast_fusion.1
  10.9 1.1 fusion.10
  11.9 1.0 fusion.14
  13.0 1.5 convert_bitcast_fusion
  14.5 0.1 copy.22
  14.6 0.1 copy.25
  14.8 1.3 fusion.4
  16.1 0.1 copy.17
  16.3 2.2 maximum_bitcast_fusion.4
  18.6 2.0 subtract_convert_fusion
  20.7 9.7 %convolution_bitcast_fusion = f32[4,8,384,2,192]{2,4,1,3,0:T(8,128)S(1)} fusion(bf16[8,1,32,12,384]{4,2,3,1,0:T(8,128)(2,1)S(1)} %get-tuple-element.15, bf16[8,1,32,12,384]{4,2,3,1,0:T(8,128)(2,1)S(1)} %get-tuple-element.14, bf16[4,1,32,12,2,192]{5,2,3,1,4,0:T(8,128)(2,1)} %get-tuple-element.21, bf16[4,1,32,12,2,192]{5,2,3,1,4,0:T(8,128)(2,1)} %get-tuple-element.20), kind=kOutput, calls=%fused_computation | convolution fusion | flops 7261913088 | bytes 25952256 | tf_op jit(solution)/shard_map/paxci,gaxcrj->gpirj/dot_general | solution.py:104
  30.4 22.8 %copy.28 = f32[4,8,384,2,192]{2,1,0,4,3:T(8,128)} copy(f32[4,8,384,2,192]{2,4,1,3,0:T(8,128)S(1)} %convolution_bitcast_fusion) | data formatting | bytes 37748736 | tf_op jit(solution)/shard_map/paxci,gaxcrj->gpirj/transpose | solution.py:104
  53.1 19.5 %reshape.469 = f32[12288,2,192]{0,2,1:T(8,128)} reshape(f32[4,8,384,2,192]{2,1,0,4,3:T(8,128)} %copy.28) | data formatting | bytes 37748736 | tf_op jit(solution)/shard_map/reshape | solution.py:107
  72.7 197.8 %reduce-scatter.2.cloned.1.call-done = f32[768,2,192]{0,2,1:T(8,128)} async-done(((f32[12288,2,192]{0,2,1:T(8,128)}), f32[768,2,192]{0,2,1:T(8,128)}) %reduce-scatter.2.cloned.1.call-update) | async-done | bytes 1179664 | tf_op jit(solution)/shard_map/reduce_scatter | solution.py:108
  270.5 1.3 convert_element_type.73
  271.8 0.2 collective-permute-start
  272.0 1.6 collective-permute-start.1
  273.6 2.7 collective-permute-start.2
  276.4 13.6 %collective-permute-done = bf16[768,2,192]{0,2,1:T(8,128)(2,1)S(1)} collective-permute-done((bf16[768,2,192]{0,2,1:T(8,128)(2,1)S(1)}, bf16[768,2,192]{0,2,1:T(8,128)(2,1)S(1)}, u32[]{:S(2)}, u32[]{:S(2)}) %collective-permute-start) | collective-permute-done | bytes 589856 | tf_op jit(solution)/shard_map/ppermute | solution.py:14
  290.1 24.2 %collective-permute-done.1 = bf16[768,2,192]{0,2,1:T(8,128)(2,1)S(1)} collective-permute-done((bf16[768,2,192]{0,2,1:T(8,128)(2,1)S(1)}, bf16[768,2,192]{0,2,1:T(8,128)(2,1)S(1)}, u32[]{:S(2)}, u32[]{:S(2)}) %collective-permute-start.1) | collective-permute-done | bytes 589856 | tf_op jit(solution)/shard_map/ppermute | solution.py:14
  314.4 0.6 add_reduce_fusion.2
  315.2 0.3 fusion.9
  315.5 0.3 fusion.8
  315.8 0.3 fusion.7
  316.2 0.3 fusion.6
  316.5 0.1 multiply_add_fusion
  316.7 51.0 %psum.7 = f32[4,4,8,2]{2,3,1,0:T(2,128)S(1)} all-reduce(f32[4,4,8,2]{2,3,1,0:T(2,128)S(1)} %multiply_add_fusion), channel_id=1, replica_groups=mesh['space'=16,'mode'=2] {'space','mode'}, use_global_device_ids=true, to_apply=%region_9.10 | all-reduce | flops 256 | bytes 2048 | tf_op jit(solution)/shard_map/psum | solution.py:142
  367.7 0.6 broadcast_multiply_fusion
  (29 shorter events, 0.6 us)
Async XLA Ops:
  7.2 3.2 copy-start.3
  7.2 3.4 copy-start.2
  7.2 3.2 copy-start.1
  7.2 263.3 %reduce-scatter.2.cloned.1.call-start = ((), (), s32[]{:S(2)}) async-start(), calls=%async_computation.1 | async-start | bytes 20054016 | tf_op jit(solution)/shard_map/reduce_scatter | solution.py:108
  271.8 18.2 %collective-permute-start = (bf16[768,2,192]{0,2,1:T(8,128)(2,1)S(1)}, bf16[768,2,192]{0,2,1:T(8,128)(2,1)S(1)}, u32[]{:S(2)}, u32[]{:S(2)}) collective-permute-start(bf16[768,2,192]{0,2,1:T(8,128)(2,1)S(1)} %convert_element_type.73), channel_id=1, source_target_pairs={{0,8},{2,10},{4,12},{6,14},{8,16},{10,18},{12,20},{14,22},{16,24},... | collective-permute-start | bytes 1769480 | tf_op jit(solution)/shard_map/ppermute | solution.py:14
  272.0 42.2 %collective-permute-start.1 = (bf16[768,2,192]{0,2,1:T(8,128)(2,1)S(1)}, bf16[768,2,192]{0,2,1:T(8,128)(2,1)S(1)}, u32[]{:S(2)}, u32[]{:S(2)}) collective-permute-start(bf16[768,2,192]{0,2,1:T(8,128)(2,1)S(1)} %convert_element_type.73), channel_id=1, source_target_pairs={{0,16},{2,18},{4,20},{6,22},{8,24},{10,26},{12,28},{14,30},{16,0},... | collective-permute-start | bytes 1769480 | tf_op jit(solution)/shard_map/ppermute | solution.py:14
  273.6 40.7 %collective-permute-start.2 = (bf16[768,2,192]{0,2,1:T(8,128)(2,1)S(1)}, bf16[768,2,192]{0,2,1:T(8,128)(2,1)S(1)}, u32[]{:S(2)}, u32[]{:S(2)}) collective-permute-start(bf16[768,2,192]{0,2,1:T(8,128)(2,1)S(1)} %convert_element_type.73), channel_id=1, source_target_pairs={{0,24},{2,26},{4,28},{6,30},{8,0},{10,2},{12,4},{14,6},{16,8},{18,... | collective-permute-start | bytes 1769480 | tf_op jit(solution)/shard_map/ppermute | solution.py:14
  276.4 38.0 %copy-start = (f32[768,2,192]{0,2,1:T(8,128)S(1)}, f32[768,2,192]{0,2,1:T(8,128)}, u32[]{:S(2)}) copy-start(f32[768,2,192]{0,2,1:T(8,128)} %reduce-scatter.2.cloned.1.call-done) | copy-start | bytes 3538948
Sparse Core Ops, SparseCore 0:
  72.8 197.6 reduce-scatter.1
where the time goes:
time: 376 us; the launch traced here: 375 us
  waiting for transfers between devices  236 us (63%)
  blocking collectives  51 us (14%)
  local copies, waits for them, and re-layouts  44.6 us (12%)
  matrix products  16.5 us (4%)
  between operations  14.3 us (4%)
  other arithmetic  8.65 us (2%)
  starting transfers between devices  4.53 us (1%)
    reduce_scatter x1, waiting for transfers between devices, body(): lax.psum_scatter(partial_fields, 'space', scatter_dimension=0, tiled=True)  198 us
    psum x1, blocking collectives, body(): traces = lax.psum(total, ('space', 'mode')) / float(vec_count * vec_count)  51 us
    ppermute x3, waiting for transfers between devices, shifted(): return lax.ppermute(x, axis, [(i, (i + by) % count) for i in range(count)])  37.7 us
    transpose x1, local copies, waits for them, and re-layouts, body(): jnp.einsum('paxci,gaxcrj->gpirj', left, right, preferred_element_type=jnp...  22.8 us
    reshape x1, local copies, waits for them, and re-layouts, body(): partial_fields.reshape(groups * mom_count * vec_count, 2, col_count)  19.5 us
    dot_general x1, matrix products, body(): jnp.einsum('paxci,gaxcrj->gpirj', left, right, preferred_element_type=jnp...  9.7 us
  transfers between devices with their start and end apart: 4, of which 3 were waited for; matrix products, arithmetic and copies ran while one was open for 0% of the time, Pallas kernels for 0%

commit v1 on v0

--- a/solution.py
+++ b/solution.py
@@ -1,17 +1,20 @@
+import functools
 import math
 
 import jax
 import jax.numpy as jnp
 import numpy as np
 from jax import lax
+from jax.experimental import pallas as pl
+from jax.experimental.pallas import tpu as pltpu
+from jax.sharding import Mesh
 from jax.sharding import PartitionSpec as P
 
 LATT = 96
-
-
-def shifted(x, axis, by):
-    count = lax.axis_size(axis)
-    return lax.ppermute(x, axis, [(i, (i + by) % count) for i in range(count)])
+VMEM = pl.BlockSpec(memory_space=pltpu.VMEM)
+SMEM = pl.BlockSpec(memory_space=pltpu.SMEM)
+BF16 = jnp.bfloat16
+F32 = jnp.float32
 
 
 def gamma_table():
@@ -28,12 +31,265 @@
             if number >> bit_pos & 1:
                 matrix = matrix @ basis[bit_pos]
         table.append(matrix)
-    table = np.stack(table)
-    return (table.real.astype(np.float32), table.imag.astype(np.float32))
+    return np.stack(table)
+
+
+def shift_lanes(x, by):
+    by = by % x.shape[-1]
+    return x if by == 0 else pltpu.roll(x, by, x.ndim - 1)
+
+
+def prepare_kernel(place, eig, sol, *rest):
+    eig_out, sol_out = rest[:4], rest[4:8]
+    packs, turned = rest[8:]
+    z, spot, half = place[0], place[1], place[2]
+    start = pl.multiple_of(half * 192, 192)
+    parts = [
+        eig[0, pl.ds(start, 96), :].astype(F32),
+        eig[1, pl.ds(start, 96), :].astype(F32),
+        eig[0, pl.ds(start + 96, 96), :].astype(F32),
+        eig[1, pl.ds(start + 96, 96), :].astype(F32),
+    ]
+    lane = lax.broadcasted_iota(jnp.int32, (96, 384), 1)
+    for quarter in range(4):
+        moved = [shift_lanes(part, 96 * (k - quarter)) for k, part in enumerate(parts)]
+        packs[quarter] = jnp.where(
+            lane < 192,
+            jnp.where(lane < 96, moved[0], moved[1]),
+            jnp.where(lane < 288, moved[2], moved[3]),
+        ).astype(BF16)
+    for k in range(4):
+        eig_out[k][...] = packs[z ^ k]
+    for r in range(2):
+        flipped = sol[r].astype(F32).T.astype(BF16)
+        for k in range(4):
+            turned[k, :, r * 384 : (r + 1) * 384] = flipped[k * 48 : (k + 1) * 48]
+    for k in range(4):
+        sol_out[k][...] = turned[spot ^ k]
+
+
+def prepare(place, eig, sol):
+    return pl.pallas_call(
+        prepare_kernel,
+        out_shape=[jax.ShapeDtypeStruct((96, 384), BF16)] * 4
+        + [jax.ShapeDtypeStruct((48, 768), BF16)] * 4,
+        in_specs=[SMEM, VMEM, VMEM],
+        out_specs=[VMEM] * 8,
+        scratch_shapes=[pltpu.VMEM((4, 96, 384), BF16), pltpu.VMEM((4, 48, 768), BF16)],
+        compiler_params=pltpu.CompilerParams(vmem_limit_bytes=32 << 20),
+    )(place, eig, sol)
+
+
+def gather_kernel(*refs):
+    blocks, out = refs[:4], refs[4]
+    for r in range(2):
+        for s in range(4):
+            at = r * 384 + s * 96
+            out[r * 4 + s] = jnp.concatenate([b[:, at : at + 96] for b in blocks], axis=1)
+
+
+def gather_plane(blocks):
+    return pl.pallas_call(
+        gather_kernel,
+        out_shape=jax.ShapeDtypeStruct((8, 48, 384), BF16),
+        in_specs=[VMEM] * 4,
+        out_specs=VMEM,
+    )(*blocks)
+
+
+def fields_kernel(place, col, sign_re, sign_im, *refs):
+    sols = refs[:4]
+    eig, cosine, sine, out, left, right, acc, fields, pairs = refs[4:]
+    spot = place[1]
+    lane = lax.broadcasted_iota(jnp.int32, (96, 384), 1)
+    lane_n = lax.broadcasted_iota(jnp.int32, (32, 384), 1)
+    for k in range(4):
+        sol = sols[k]
+        for g in range(4):
+            for s in range(4):
+                at = g * 4 + s
+                src_re = sol[col[at]].astype(F32)
+                src_im = sol[4 + col[at]].astype(F32)
+                row, lanes = g * 96, slice(s * 384, (s + 1) * 384)
+                left[row : row + 48, lanes] = (
+                    sign_re[at] * src_re - sign_im[at] * src_im
+                ).astype(BF16)
+                left[row + 48 : row + 96, lanes] = (
+                    sign_re[at] * src_im + sign_im[at] * src_re
+                ).astype(BF16)
+
+        def device(m, carry, k=k):
+            both = []
+            for half in range(2):
+                w = eig[spot ^ m, half, k].astype(F32)
+                w192 = shift_lanes(w, 192)
+                w96 = shift_lanes(w, 96)
+                w288 = shift_lanes(w192, 96)
+                for first, middle, last in ((w, w96, w192), (w192, w288, w)):
+                    a = jnp.where(lane < 96, first, jnp.where(lane < 288, middle, last))
+                    both.append((a.reshape(3, 32, 384), shift_lanes(a, 192).reshape(3, 32, 384)))
+            at = pl.multiple_of((k * 4 + m) * 32, 32)
+            cos_all, sin_all = cosine[pl.ds(at, 32), :], sine[pl.ds(at, 32), :]
+            for q in range(4):
+                c0, c1 = cos_all[:, 2 * q : 2 * q + 1], cos_all[:, 2 * q + 1 : 2 * q + 2]
+                s0, s1 = sin_all[:, 2 * q : 2 * q + 1], sin_all[:, 2 * q + 1 : 2 * q + 2]
+                odd = (lane_n % 192) >= 96
+                c = jnp.where(odd, c1, c0)
+                c = jnp.where(lane_n < 192, c, -c)[None]
+                d = -jnp.where(odd, s1, s0)[None]
+                for s in range(4):
+                    a, b = both[s]
+                    y = c * a + d * b
+                    row = pl.multiple_of(s * 384 + m * 96, 96)
+                    right[pl.ds(row, 96), q * 384 : (q + 1) * 384] = y.reshape(96, 384).astype(BF16)
+            return carry
+
+        lax.fori_loop(0, 4, device, 0)
+
+        def columns(n, carry, k=k):
+            at = pl.ds(pl.multiple_of(n * 256, 256), 256)
+            part = jnp.dot(left[...], right[:, at], preferred_element_type=F32)
+            if k == 0:
+                acc[:, at] = part
+            else:
+                acc[:, at] += part
+            return carry
+
+        lax.fori_loop(0, 6, columns, 0)
+
+    flip = jnp.where(lax.broadcasted_iota(jnp.int32, (48, 384), 1) < 192, -1.0, 1.0).astype(F32)
+    for q in range(4):
+        lanes = slice(q * 384, (q + 1) * 384)
+        rows = []
+        for g in range(4):
+            row = g * 96
+            f = acc[row : row + 48, lanes] + flip * shift_lanes(acc[row + 48 : row + 96, lanes], 192)
+            rows.append(f)
+            out[g * 4 + q, 0:48, :] = f.astype(BF16)
+        turned = [flip * shift_lanes(f, 192) for f in rows]
+        for g in range(4):
+            for h in range(g, 4):
+                re = jnp.sum(rows[g] * rows[h], axis=0, keepdims=True)
+                at, mirror = (g * 4 + h) * 2, (h * 4 + g) * 2
+                pairs[at : at + 1, lanes] = re
+                if h > g:
+                    im = jnp.sum(rows[g] * turned[h], axis=0, keepdims=True)
+                    pairs[mirror : mirror + 1, lanes] = re
+                    pairs[at + 1 : at + 2, lanes] = im
+                    pairs[mirror + 1 : mirror + 2, lanes] = -im
+                else:
+                    pairs[at + 1 : at + 2, lanes] = jnp.zeros_like(re)
+    lane_p = lax.broadcasted_iota(jnp.int32, (8, 1536), 1)
+    mom = lax.broadcasted_iota(jnp.int32, (8, 1536), 0)
+    select = (lane_p // 384 * 2 + lane_p % 192 // 96 == mom).astype(F32)
+    total = lax.dot_general(
+        select,
+        pairs[...],
+        (((1,), (1,)), ((), ())),
+        precision=lax.Precision.HIGHEST,
+        preferred_element_type=F32,
+    )
+    high = total.astype(BF16)
+    low = (total - high.astype(F32)).astype(BF16)
+    tail = jnp.concatenate([high, low, jnp.zeros((8, 320), BF16)], axis=1)
+    for block in range(16):
+        out[block, 48:56, :] = tail
+
+
+def local_fields(place, col, sign_re, sign_im, sols, eig, cosine, sine):
+    return pl.pallas_call(
+        fields_kernel,
+        out_shape=jax.ShapeDtypeStruct((16, 56, 384), BF16),
+        in_specs=[SMEM] * 4 + [VMEM] * 7,
+        out_specs=VMEM,
+        scratch_shapes=[
+            pltpu.VMEM((384, 1536), BF16),
+            pltpu.VMEM((1536, 1536), BF16),
+            pltpu.VMEM((384, 1536), F32),
+            pltpu.VMEM((8, 128), F32),
+            pltpu.VMEM((32, 1536), F32),
+        ],
+        compiler_params=pltpu.CompilerParams(vmem_limit_bytes=48 << 20),
+    )(place, col, sign_re, sign_im, *sols, eig, cosine, sine)
+
+
+def join_kernel(blocks, out):
+    for spot in range(4):
+        rows = slice(spot * 48, (spot + 1) * 48)
+        got = [blocks[z * 4 + spot, 0:48, :].astype(F32) for z in range(4)]
+        for r in range(2):
+            for p in range(2):
+                at = r * 192 + p * 96
+                out[r, rows, p * 384 : (p + 1) * 384] = jnp.concatenate(
+                    [g[:, at : at + 96] for g in got], axis=1
+                )
+
+
+def join_fields(blocks):
+    return pl.pallas_call(
+        join_kernel,
+        out_shape=jax.ShapeDtypeStruct((2, 192, 768), F32),
+        in_specs=[VMEM],
+        out_specs=VMEM,
+        compiler_params=pltpu.CompilerParams(vmem_limit_bytes=32 << 20),
+    )(blocks)
+
+
+def swap(x, axis, mask):
+    return lax.ppermute(x, axis, [(i, i ^ mask) for i in range(lax.axis_size(axis))])
+
+
+def fast_body(eigvecs, solutions, momenta, gammas):
+    z, spot, half = lax.axis_index("z"), lax.axis_index("plane"), lax.axis_index("mode")
+    vec_count = eigvecs.shape[3]
+    place = jnp.stack([z, spot, half]).astype(jnp.int32)
+    eig = eigvecs.transpose(0, 2, 1, 3).reshape(2, 384, 384)
+    sol = solutions.transpose(0, 2, 1, 3).reshape(2, 384, 192)
+    prepared = prepare(place, eig, sol)
+    eig_own, sol_own = prepared[:4], prepared[4:]
+    eig_planes = [eig_own[0]] + [swap(eig_own[k], "z", k) for k in range(1, 4)]
+    sol_plane = gather_plane([sol_own[0]] + [swap(sol_own[k], "plane", k) for k in range(1, 4)])
+    sols = [sol_plane] + [swap(sol_plane, "z", k) for k in range(1, 4)]
+    eig_all = lax.all_gather(jnp.stack(eig_planes), ("plane", "mode")).reshape(4, 2, 4, 96, 384)
+
+    table = gamma_table()
+    col_table = jnp.asarray(np.argmax(np.abs(table), axis=2).astype(np.int32))
+    value = table.sum(axis=2)
+    select = (gammas[:, None] == jnp.arange(16, dtype=jnp.int32)[None, :])[:, :, None]
+    col = jnp.sum(jnp.where(select, col_table[None], 0), axis=1).reshape(16)
+    sign_re = jnp.sum(jnp.where(select, jnp.asarray(value.real, F32)[None], 0.0), axis=1).reshape(16)
+    sign_im = jnp.sum(jnp.where(select, jnp.asarray(value.imag, F32)[None], 0.0), axis=1).reshape(16)
+
+    device = (z * 4 + spot) ^ jnp.arange(16, dtype=jnp.int32)
+    site = (device[:, None] * 32 + jnp.arange(32, dtype=jnp.int32)[None, :]).reshape(512)
+    coord_x, coord_y, coord_z = site // (LATT * LATT), site // LATT % LATT, site % LATT
+    phase_int = (
+        coord_x[:, None] * momenta[None, :, 0]
+        + coord_y[:, None] * momenta[None, :, 1]
+        + coord_z[:, None] * momenta[None, :, 2]
+    ) % LATT
+    theta = 2.0 * math.pi / LATT * phase_int.astype(F32)
+
+    sent = local_fields(
+        place, col, sign_re, sign_im, sols, eig_all, jnp.cos(theta), jnp.sin(theta)
+    )
+    got = lax.all_to_all(sent, ("z", "plane"), 0, 0, tiled=True)
+    part = jnp.sum(got[:, 48:, :64].astype(F32), axis=0)
+    part = part[:, :32] + part[:, 32:]
+    part = part + swap(part, "mode", 1)
+    traces = (part / float(vec_count * vec_count)).reshape(8, 4, 4, 2).transpose(1, 2, 0, 3)
+    fields = join_fields(got).transpose(2, 0, 1)
+    return fields, traces
+
+
+def shifted(x, axis, by):
+    count = lax.axis_size(axis)
+    return lax.ppermute(x, axis, [(i, (i + by) % count) for i in range(count)])
 
 
 def select_gammas(gammas):
-    table_re, table_im = gamma_table()
+    table = gamma_table()
+    table_re, table_im = table.real.astype(np.float32), table.imag.astype(np.float32)
     select = (gammas[:, None] == jnp.arange(16, dtype=jnp.int32)[None, :]).astype(jnp.float32)
     count = gammas.shape[0]
     real_part = jnp.dot(
@@ -89,7 +345,7 @@
     return jnp.stack([upper, lower], 1).astype(jnp.bfloat16)
 
 
-def body(eigvecs, solutions, momenta, gammas):
+def general_body(eigvecs, solutions, momenta, gammas):
     local_sites = eigvecs.shape[1]
     vec_count = eigvecs.shape[3]
     col_count = solutions.shape[3]
@@ -144,10 +400,27 @@
 
 
 def solution(mesh):
-    return jax.shard_map(
-        body,
-        mesh=mesh,
-        in_specs=(P(None, "space", None, None), P(None, "space", None, "mode"), P(), P()),
-        out_specs=(P("space", None, "mode"), P()),
-        check_vma=False,
-    )
+    fits = dict(mesh.shape) == {"space": 16, "mode": 2}
+    if fits:
+        cut = Mesh(mesh.devices.reshape(4, 4, 2), ("z", "plane", "mode"))
+        space = ("z", "plane")
+    else:
+        cut, space = mesh, "space"
+
+    def step(eigvecs, solutions, momenta, gammas):
+        sized = eigvecs.shape == (2, 512, 12, 384) and solutions.shape == (2, 512, 12, 384)
+        sized = sized and momenta.shape == (8, 3) and gammas.shape == (4,)
+        return jax.shard_map(
+            fast_body if fits and sized else general_body,
+            mesh=cut if fits and sized else mesh,
+            in_specs=(
+                P(None, space if fits and sized else "space", None, None),
+                P(None, space if fits and sized else "space", None, "mode"),
+                P(),
+                P(),
+            ),
+            out_specs=(P(space if fits and sized else "space", None, "mode"), P()),
+            check_vma=False,
+        )(eigvecs, solutions, momenta, gammas)
+
+    return step

time: 376 us -> 127 us (0.34)
  waiting for transfers between devices: 236 us -> 31 us
  local copies, waits for them, and re-layouts: 44.6 us -> 8.22 us
  Pallas kernels: 0 us -> 32.4 us
  blocking collectives: 51 us -> 23.2 us
  matrix products: 16.5 us -> 0 us
  starting transfers between devices: 4.53 us -> 13.5 us
  other arithmetic: 8.65 us -> 3.93 us
    reduce_scatter x1 -> x0, waiting for transfers between devices: 198 us -> none  [body(): lax.psum_scatter(partial_fields, 'space', scatter_dimension=0, tiled=True)]
    psum x1 -> x0, blocking collectives: 51 us -> none  [body(): traces = lax.psum(total, ('space', 'mode')) / float(vec_count * vec_count)]
    pallas_call x0 -> x4, Pallas kernels: none -> 32.4 us  [the longest x1 28.2 us: local_fields(): pl.pallas_call(fields_kernel, out_shape=jax.ShapeDtypeStruct((16, 56, 384...]
    all_to_all x0 -> x1, blocking collectives: none -> 23.2 us  [fast_body(): got = lax.all_to_all(sent, ('z', 'plane'), 0, 0, tiled=True)]
    transpose x1 -> x0, local copies, waits for them, and re-layouts: 22.8 us -> none  [body(): jnp.einsum('paxci,gaxcrj->gpirj', left, right, preferred_element_type=jnp...]
    reshape x1 -> x3, local copies, waits for them, and re-layouts: 19.5 us -> 0.25 us  [the longest x1 0.09 us: fast_body(): col = jnp.sum(jnp.where(select, col_table[None], 0), axis=1).reshape(16)]
    dot_general x11 -> x0, matrix products: 16.5 us -> none  [the longest x1 9.7 us: body(): jnp.einsum('paxci,gaxcrj->gpirj', left, right, preferred_element_type=jnp...]
    ppermute x3 -> x10, starting transfers between devices: 4.5 us -> 13.4 us  [swap(): lax.ppermute(x, axis, [(i, i ^ mask) for i in range(lax.axis_size(axis))])]
  transfers between devices with their start and end apart: 4 -> 11, of which waited for: 3 -> 6; matrix products, arithmetic and copies ran while one was open for 0% -> 4% of each run, Pallas kernels for 0% -> 3%
where the time goes in v1:
time: 127 us; the launch traced here: 126 us
  Pallas kernels  32.4 us (26%)
  waiting for transfers between devices  31 us (24%)
  blocking collectives  23.2 us (18%)
  between operations  14.1 us (11%)
  starting transfers between devices  13.5 us (11%)
  local copies, waits for them, and re-layouts  8.22 us (6%)
  other arithmetic  3.93 us (3%)
    ppermute x10, waiting for transfers between devices, swap(): lax.ppermute(x, axis, [(i, i ^ mask) for i in range(lax.axis_size(axis))])  31 us
    pallas_call x1, Pallas kernels, local_fields(): pl.pallas_call(fields_kernel, out_shape=jax.ShapeDtypeStruct((16, 56, 384...  28.2 us
    all_to_all x1, blocking collectives, fast_body(): got = lax.all_to_all(sent, ('z', 'plane'), 0, 0, tiled=True)  23.2 us
    ppermute x10, starting transfers between devices, swap(): lax.ppermute(x, axis, [(i, i ^ mask) for i in range(lax.axis_size(axis))])  13.4 us
    unnamed x18, local copies, waits for them, and re-layouts  5.94 us
  transfers between devices with their start and end apart: 11, of which 6 were waited for; matrix products, arithmetic and copies ran while one was open for 4% of the time, Pallas kernels for 3%

profile of v1, /device:TPU:0, one launch (start us, length us, event | category | flops | bytes accessed | tf_op | source)
XLA Modules:
  0.0 126.3 jit_solution(3903025569337532068)
XLA Ops:
  7.3 1.1 copy-done.2
  8.4 1.0 copy-done.3
  9.4 1.0 shard_map.86
  10.3 0.6 copy-done.4
  10.9 3.0 %collective-permute-start.6 = (bf16[96,384]{1,0:T(8,128)(2,1)S(1)}, bf16[96,384]{1,0:T(8,128)(2,1)S(1)}, u32[]{:S(2)}, u32[]{:S(2)}) collective-permute-start(bf16[96,384]{1,0:T(8,128)(2,1)S(1)} %get-tuple-element.15), channel_id=1, source_target_pairs={{0,8},{8,0},{16,24},{24,16},{1,9},{9,1},{17,25},{25,17},{2,10},{10... | collective-permute-start | bytes 221192 | tf_op jit(solution)/shard_map/ppermute | solution.py:239
  14.0 2.6 %collective-permute-start.7 = (bf16[96,384]{1,0:T(8,128)(2,1)S(1)}, bf16[96,384]{1,0:T(8,128)(2,1)S(1)}, u32[]{:S(2)}, u32[]{:S(2)}) collective-permute-start(bf16[96,384]{1,0:T(8,128)(2,1)S(1)} %get-tuple-element.16), channel_id=1, source_target_pairs={{0,16},{8,24},{16,0},{24,8},{1,17},{9,25},{17,1},{25,9},{2,18},{10... | collective-permute-start | bytes 221192 | tf_op jit(solution)/shard_map/ppermute | solution.py:239
  16.6 5.2 %collective-permute-done.7 = bf16[96,384]{1,0:T(8,128)(2,1)S(1)} collective-permute-done((bf16[96,384]{1,0:T(8,128)(2,1)S(1)}, bf16[96,384]{1,0:T(8,128)(2,1)S(1)}, u32[]{:S(2)}, u32[]{:S(2)}) %collective-permute-start.7) | collective-permute-done | bytes 73760 | tf_op jit(solution)/shard_map/ppermute | solution.py:239
  21.8 1.1 collective-permute-done.8
  22.8 0.8 pad_maximum_fusion
  23.7 1.6 %collective-permute-start.1 = (bf16[48,768]{1,0:T(8,128)(2,1)S(1)}, bf16[48,768]{1,0:T(8,128)(2,1)S(1)}, u32[]{:S(2)}, u32[]{:S(2)}) collective-permute-start(bf16[48,768]{1,0:T(8,128)(2,1)S(1)} %get-tuple-element.12), channel_id=1, source_target_pairs={{0,4},{2,6},{4,0},{6,2},{1,5},{3,7},{5,1},{7,3},{8,12},{10,14},{12... | collective-permute-start | bytes 221192 | tf_op jit(solution)/shard_map/ppermute | solution.py:239
  25.2 0.3 collective-permute-start.2
  26.1 0.7 iota_compare_fusion
  26.9 0.8 slice_bitcast_fusion.2
  27.8 0.8 select_reduce_fusion
  28.6 1.1 collective-permute-done.2.refs_3_
  29.7 0.6 copy-done.7
  30.4 1.9 %shard_map.87.refs_0_ = bf16[8,48,384]{2,1,0:T(8,128)(2,1)} custom-call(bf16[48,768]{1,0:T(8,128)(2,1)} %copy-done.4, bf16[48,768]{1,0:T(8,128)(2,1)} %copy-done.5, bf16[48,768]{1,0:T(8,128)(2,1)} %copy-done.6, bf16[48,768]{1,0:T(8,128)(2,1)} %copy-done.7), custom_call_target="tpu_custom_call" | custom-call | tf_op jit(solution)/shard_map/pallas_call | solution.py:92
  32.3 2.2 %collective-permute-start.5 = (bf16[8,48,384]{2,1,0:T(8,128)(2,1)}, bf16[8,48,384]{2,1,0:T(8,128)(2,1)S(1)}, u32[]{:S(2)}, u32[]{:S(2)}) collective-permute-start(bf16[8,48,384]{2,1,0:T(8,128)(2,1)} %shard_map.87.refs_0_), channel_id=1, source_target_pairs={{0,24},{8,16},{16,8},{24,0},{1,25},{9,17},{17,9},{25,1},{2,26},{10... | collective-permute-start | bytes 884744 | tf_op jit(solution)/shard_map/ppermute | solution.py:239
  34.5 0.4 collective-permute-start.4
  34.8 1.8 %collective-permute-start.3 = (bf16[8,48,384]{2,1,0:T(8,128)(2,1)}, bf16[8,48,384]{2,1,0:T(8,128)(2,1)S(1)}, u32[]{:S(2)}, u32[]{:S(2)}) collective-permute-start(bf16[8,48,384]{2,1,0:T(8,128)(2,1)} %shard_map.87.refs_0_), channel_id=1, source_target_pairs={{0,8},{8,0},{16,24},{24,16},{1,9},{9,1},{17,25},{25,17},{2,10},{10... | collective-permute-start | bytes 884744 | tf_op jit(solution)/shard_map/ppermute | solution.py:239
  36.7 0.2 select_reduce_fusion.2
  37.2 1.0 multiply_sine_fusion
  38.2 6.1 %collective-permute-done.5.refs_3_ = bf16[8,48,384]{2,1,0:T(8,128)(2,1)S(1)} collective-permute-done((bf16[8,48,384]{2,1,0:T(8,128)(2,1)}, bf16[8,48,384]{2,1,0:T(8,128)(2,1)S(1)}, u32[]{:S(2)}, u32[]{:S(2)}) %collective-permute-start.5) | collective-permute-done | bytes 294944 | tf_op jit(solution)/shard_map/ppermute | solution.py:239
  44.3 16.7 %collective-permute-done.4.refs_2_ = bf16[8,48,384]{2,1,0:T(8,128)(2,1)S(1)} collective-permute-done((bf16[8,48,384]{2,1,0:T(8,128)(2,1)}, bf16[8,48,384]{2,1,0:T(8,128)(2,1)S(1)}, u32[]{:S(2)}, u32[]{:S(2)}) %collective-permute-start.4) | collective-permute-done | bytes 294944 | tf_op jit(solution)/shard_map/ppermute | solution.py:239
  61.0 1.7 %copy-done = bf16[32,96,384]{2,1,0:T(8,128)(2,1)S(1)} copy-done((bf16[32,96,384]{2,1,0:T(8,128)(2,1)S(1)}, bf16[32,96,384]{2,1,0:T(8,128)(2,1)}, u32[]{:S(2)}) %copy-start) | copy-done | bytes 2359320
  62.7 1.0 copy-done.1
  63.6 28.2 %shard_map.88 = bf16[16,56,384]{2,1,0:T(8,128)(2,1)S(1)} custom-call(s32[3]{0:T(128)S(1)} %pad_add_fusion.place, s32[16]{0:T(128)S(1)} %reshape.120.col, f32[16]{0:T(128)S(1)} %reshape.121.sign_re, f32[16]{0:T(128)S(1)} %reshape.122.sign_im, bf16[8,48,384]{2,1,0:T(8,128)(2,1)S(1)} %copy-done.1, bf16[8,48,384]{2,1,0:T(8,128)(2,1)S(1)} %collective-permute-done.3.refs_1_, ...), custom_call_target="tpu_custom_call" | custom-call | tf_op jit(solution)/shard_map/pallas_call | solution.py:200
  91.8 23.2 %all_to_all.5.blocks = bf16[16,56,384]{2,1,0:T(8,128)(2,1)S(1)} all-to-all(bf16[16,56,384]{2,1,0:T(8,128)(2,1)S(1)} %shard_map.88), channel_id=1, replica_groups=mesh['z'=4,'plane'=4,'mode'=2] {'z','plane'}, dimensions={0} | all-to-all | bytes 1376256 | tf_op jit(solution)/shard_map/all_to_all | solution.py:276
  115.1 1.5 %collective-permute-start.9 = (f32[8,32]{1,0:T(8,128)S(1)}, f32[8,32]{1,0:T(8,128)S(1)}, u32[]{:S(2)}, u32[]{:S(2)}) collective-permute-start(f32[8,32]{1,0:T(8,128)S(1)} %slice_add_fusion), channel_id=1, source_target_pairs={{0,1},{1,0},{2,3},{3,2},{4,5},{5,4},{6,7},{7,6},{8,9},{9,8},{10,11... | collective-permute-start | bytes 3080 | tf_op jit(solution)/shard_map/ppermute | solution.py:239
  116.6 1.3 %shard_map.89 = f32[2,192,768]{2,1,0:T(8,128)} custom-call(bf16[16,56,384]{2,1,0:T(8,128)(2,1)S(1)} %all_to_all.5.blocks), custom_call_target="tpu_custom_call" | custom-call | tf_op jit(solution)/shard_map/pallas_call | solution.py:229
  117.9 0.8 collective-permute-done.9
  118.8 0.7 copy.13
  (39 shorter events, 1.5 us)
Async XLA Ops:
  7.2 29.5 %copy-start.8 = (s32[16,4]{0,1:T(4,128)S(1)}, s32[16,4]{0,1:T(4,128)}, u32[]{:S(2)}) copy-start(s32[16,4]{0,1:T(4,128)} %constant.64.clone) | copy-start | bytes 772
  7.2 53.8 %all-gather.3.cloned.1.call-start = ((), (), s32[]{:S(2)}) async-start(), calls=%async_computation.1 | async-start | bytes 2654208 | tf_op jit(solution)/shard_map/all_gather | solution.py:253
  7.3 1.1 copy-start.2
  8.4 1.0 copy-start.3
  10.3 0.6 copy-start.4
  10.9 5.6 %collective-permute-start.6 = (bf16[96,384]{1,0:T(8,128)(2,1)S(1)}, bf16[96,384]{1,0:T(8,128)(2,1)S(1)}, u32[]{:S(2)}, u32[]{:S(2)}) collective-permute-start(bf16[96,384]{1,0:T(8,128)(2,1)S(1)} %get-tuple-element.15), channel_id=1, source_target_pairs={{0,8},{8,0},{16,24},{24,16},{1,9},{9,1},{17,25},{25,17},{2,10},{10... | collective-permute-start | bytes 221192 | tf_op jit(solution)/shard_map/ppermute | solution.py:239
  14.0 7.8 %collective-permute-start.7 = (bf16[96,384]{1,0:T(8,128)(2,1)S(1)}, bf16[96,384]{1,0:T(8,128)(2,1)S(1)}, u32[]{:S(2)}, u32[]{:S(2)}) collective-permute-start(bf16[96,384]{1,0:T(8,128)(2,1)S(1)} %get-tuple-element.16), channel_id=1, source_target_pairs={{0,16},{8,24},{16,0},{24,8},{1,17},{9,25},{17,1},{25,9},{2,18},{10... | collective-permute-start | bytes 221192 | tf_op jit(solution)/shard_map/ppermute | solution.py:239
  16.6 6.3 %collective-permute-start.8 = (bf16[96,384]{1,0:T(8,128)(2,1)S(1)}, bf16[96,384]{1,0:T(8,128)(2,1)S(1)}, u32[]{:S(2)}, u32[]{:S(2)}) collective-permute-start(bf16[96,384]{1,0:T(8,128)(2,1)S(1)} %get-tuple-element.17), channel_id=1, source_target_pairs={{0,24},{8,16},{16,8},{24,0},{1,25},{9,17},{17,9},{25,1},{2,26},{10... | collective-permute-start | bytes 221192 | tf_op jit(solution)/shard_map/ppermute | solution.py:239
  23.6 5.0 %collective-permute-start = (bf16[48,768]{1,0:T(8,128)(2,1)S(1)}, bf16[48,768]{1,0:T(8,128)(2,1)S(1)}, u32[]{:S(2)}, u32[]{:S(2)}) collective-permute-start(bf16[48,768]{1,0:T(8,128)(2,1)S(1)} %get-tuple-element.11), channel_id=1, source_target_pairs={{0,2},{2,0},{4,6},{6,4},{1,3},{3,1},{5,7},{7,5},{8,10},{10,8},{12,... | collective-permute-start | bytes 221192 | tf_op jit(solution)/shard_map/ppermute | solution.py:239
  23.7 4.9 %collective-permute-start.1 = (bf16[48,768]{1,0:T(8,128)(2,1)S(1)}, bf16[48,768]{1,0:T(8,128)(2,1)S(1)}, u32[]{:S(2)}, u32[]{:S(2)}) collective-permute-start(bf16[48,768]{1,0:T(8,128)(2,1)S(1)} %get-tuple-element.12), channel_id=1, source_target_pairs={{0,4},{2,6},{4,0},{6,2},{1,5},{3,7},{5,1},{7,3},{8,12},{10,14},{12... | collective-permute-start | bytes 221192 | tf_op jit(solution)/shard_map/ppermute | solution.py:239
  25.2 4.5 %collective-permute-start.2 = (bf16[48,768]{1,0:T(8,128)(2,1)S(1)}, bf16[48,768]{1,0:T(8,128)(2,1)S(1)}, u32[]{:S(2)}, u32[]{:S(2)}) collective-permute-start(bf16[48,768]{1,0:T(8,128)(2,1)S(1)} %get-tuple-element.13), channel_id=1, source_target_pairs={{0,6},{2,4},{4,2},{6,0},{1,7},{3,5},{5,3},{7,1},{8,14},{10,12},{12... | collective-permute-start | bytes 221192 | tf_op jit(solution)/shard_map/ppermute | solution.py:239
  28.6 1.2 copy-start.5
  28.6 1.2 copy-start.6
  29.7 0.6 copy-start.7
  32.3 12.0 %collective-permute-start.5 = (bf16[8,48,384]{2,1,0:T(8,128)(2,1)}, bf16[8,48,384]{2,1,0:T(8,128)(2,1)S(1)}, u32[]{:S(2)}, u32[]{:S(2)}) collective-permute-start(bf16[8,48,384]{2,1,0:T(8,128)(2,1)} %shard_map.87.refs_0_), channel_id=1, source_target_pairs={{0,24},{8,16},{16,8},{24,0},{1,25},{9,17},{17,9},{25,1},{2,26},{10... | collective-permute-start | bytes 884744 | tf_op jit(solution)/shard_map/ppermute | solution.py:239
  34.5 26.5 %collective-permute-start.4 = (bf16[8,48,384]{2,1,0:T(8,128)(2,1)}, bf16[8,48,384]{2,1,0:T(8,128)(2,1)S(1)}, u32[]{:S(2)}, u32[]{:S(2)}) collective-permute-start(bf16[8,48,384]{2,1,0:T(8,128)(2,1)} %shard_map.87.refs_0_), channel_id=1, source_target_pairs={{0,16},{8,24},{16,0},{24,8},{1,17},{9,25},{17,1},{25,9},{2,18},{10... | collective-permute-start | bytes 884744 | tf_op jit(solution)/shard_map/ppermute | solution.py:239
  34.8 26.2 %collective-permute-start.3 = (bf16[8,48,384]{2,1,0:T(8,128)(2,1)}, bf16[8,48,384]{2,1,0:T(8,128)(2,1)S(1)}, u32[]{:S(2)}, u32[]{:S(2)}) collective-permute-start(bf16[8,48,384]{2,1,0:T(8,128)(2,1)} %shard_map.87.refs_0_), channel_id=1, source_target_pairs={{0,8},{8,0},{16,24},{24,16},{1,9},{9,1},{17,25},{25,17},{2,10},{10... | collective-permute-start | bytes 884744 | tf_op jit(solution)/shard_map/ppermute | solution.py:239
  61.0 1.7 %copy-start = (bf16[32,96,384]{2,1,0:T(8,128)(2,1)S(1)}, bf16[32,96,384]{2,1,0:T(8,128)(2,1)}, u32[]{:S(2)}) copy-start(bf16[32,96,384]{2,1,0:T(8,128)(2,1)} %all-gather.3.cloned.1.call-done) | copy-start | bytes 7077892
  62.7 1.0 copy-start.1
  115.1 3.6 %collective-permute-start.9 = (f32[8,32]{1,0:T(8,128)S(1)}, f32[8,32]{1,0:T(8,128)S(1)}, u32[]{:S(2)}, u32[]{:S(2)}) collective-permute-start(f32[8,32]{1,0:T(8,128)S(1)} %slice_add_fusion), channel_id=1, source_target_pairs={{0,1},{1,0},{2,3},{3,2},{4,5},{5,4},{6,7},{7,6},{8,9},{9,8},{10,11... | collective-permute-start | bytes 3080 | tf_op jit(solution)/shard_map/ppermute | solution.py:239
Sparse Core Ops, SparseCore 0:
  23.7 28.8 all-gather.2

commit v2 on v1

--- a/solution.py
+++ b/solution.py
@@ -39,6 +39,12 @@
     return x if by == 0 else pltpu.roll(x, by, x.ndim - 1)
 
 
+def by_quarter(lane, first, second, third, fourth):
+    return jnp.where(
+        lane < 192, jnp.where(lane < 96, first, second), jnp.where(lane < 288, third, fourth)
+    )
+
+
 def prepare_kernel(place, eig, sol, *rest):
     eig_out, sol_out = rest[:4], rest[4:8]
     packs, turned = rest[8:]
@@ -53,11 +59,7 @@
     lane = lax.broadcasted_iota(jnp.int32, (96, 384), 1)
     for quarter in range(4):
         moved = [shift_lanes(part, 96 * (k - quarter)) for k, part in enumerate(parts)]
-        packs[quarter] = jnp.where(
-            lane < 192,
-            jnp.where(lane < 96, moved[0], moved[1]),
-            jnp.where(lane < 288, moved[2], moved[3]),
-        ).astype(BF16)
+        packs[quarter] = by_quarter(lane, *moved).astype(BF16)
     for k in range(4):
         eig_out[k][...] = packs[z ^ k]
     for r in range(2):
@@ -82,10 +84,12 @@
 
 def gather_kernel(*refs):
     blocks, out = refs[:4], refs[4]
+    lane = lax.broadcasted_iota(jnp.int32, (48, 384), 1)
     for r in range(2):
+        parts = [b[:, r * 384 : (r + 1) * 384].astype(F32) for b in blocks]
         for s in range(4):
-            at = r * 384 + s * 96
-            out[r * 4 + s] = jnp.concatenate([b[:, at : at + 96] for b in blocks], axis=1)
+            moved = [shift_lanes(part, 96 * (m - s)) for m, part in enumerate(parts)]
+            out[r * 4 + s] = by_quarter(lane, *moved).astype(BF16)
 
 
 def gather_plane(blocks):
@@ -97,66 +101,82 @@
     )(*blocks)
 
 
-def fields_kernel(place, col, sign_re, sign_im, *refs):
-    sols = refs[:4]
-    eig, cosine, sine, out, left, right, acc, fields, pairs = refs[4:]
-    spot = place[1]
+def build_left(sol, col, sign_re, sign_im, left):
+    for g in range(4):
+        for s in range(4):
+            at = g * 4 + s
+            src_re = sol[col[at]].astype(F32)
+            src_im = sol[4 + col[at]].astype(F32)
+            row, lanes = g * 96, slice(s * 384, (s + 1) * 384)
+            left[row : row + 48, lanes] = (sign_re[at] * src_re - sign_im[at] * src_im).astype(BF16)
+            left[row + 48 : row + 96, lanes] = (
+                sign_re[at] * src_im + sign_im[at] * src_re
+            ).astype(BF16)
+
+
+def build_right(half, eigs, k, cosine, sine, right, m):
     lane = lax.broadcasted_iota(jnp.int32, (96, 384), 1)
     lane_n = lax.broadcasted_iota(jnp.int32, (32, 384), 1)
-    for k in range(4):
-        sol = sols[k]
-        for g in range(4):
-            for s in range(4):
-                at = g * 4 + s
-                src_re = sol[col[at]].astype(F32)
-                src_im = sol[4 + col[at]].astype(F32)
-                row, lanes = g * 96, slice(s * 384, (s + 1) * 384)
-                left[row : row + 48, lanes] = (
-                    sign_re[at] * src_re - sign_im[at] * src_im
-                ).astype(BF16)
-                left[row + 48 : row + 96, lanes] = (
-                    sign_re[at] * src_im + sign_im[at] * src_re
-                ).astype(BF16)
-
-        def device(m, carry, k=k):
-            both = []
-            for half in range(2):
-                w = eig[spot ^ m, half, k].astype(F32)
-                w192 = shift_lanes(w, 192)
-                w96 = shift_lanes(w, 96)
-                w288 = shift_lanes(w192, 96)
-                for first, middle, last in ((w, w96, w192), (w192, w288, w)):
-                    a = jnp.where(lane < 96, first, jnp.where(lane < 288, middle, last))
-                    both.append((a.reshape(3, 32, 384), shift_lanes(a, 192).reshape(3, 32, 384)))
-            at = pl.multiple_of((k * 4 + m) * 32, 32)
-            cos_all, sin_all = cosine[pl.ds(at, 32), :], sine[pl.ds(at, 32), :]
-            for q in range(4):
-                c0, c1 = cos_all[:, 2 * q : 2 * q + 1], cos_all[:, 2 * q + 1 : 2 * q + 2]
-                s0, s1 = sin_all[:, 2 * q : 2 * q + 1], sin_all[:, 2 * q + 1 : 2 * q + 2]
-                odd = (lane_n % 192) >= 96
-                c = jnp.where(odd, c1, c0)
-                c = jnp.where(lane_n < 192, c, -c)[None]
-                d = -jnp.where(odd, s1, s0)[None]
-                for s in range(4):
-                    a, b = both[s]
-                    y = c * a + d * b
-                    row = pl.multiple_of(s * 384 + m * 96, 96)
-                    right[pl.ds(row, 96), q * 384 : (q + 1) * 384] = y.reshape(96, 384).astype(BF16)
-            return carry
-
-        lax.fori_loop(0, 4, device, 0)
-
-        def columns(n, carry, k=k):
-            at = pl.ds(pl.multiple_of(n * 256, 256), 256)
-            part = jnp.dot(left[...], right[:, at], preferred_element_type=F32)
-            if k == 0:
-                acc[:, at] = part
-            else:
-                acc[:, at] += part
-            return carry
-
-        lax.fori_loop(0, 6, columns, 0)
-
+    both = []
+    for other in range(2):
+        w = eigs[m * 2 + other][k].astype(F32)
+        w192 = shift_lanes(w, 192)
+        w96 = shift_lanes(w, 96)
+        w288 = shift_lanes(w192, 96)
+        for low, (first, middle, last) in enumerate(((w, w96, w192), (w192, w288, w))):
+            a = jnp.where(lane < 96, first, jnp.where(lane < 288, middle, last))
+            row = pl.multiple_of(((half ^ other) * 2 + low) * 384 + m * 96, 96)
+            both.append((row, a.reshape(3, 32, 384), shift_lanes(a, 192).reshape(3, 32, 384)))
+    at = (k * 4 + m) * 32
+    cos_all, sin_all = cosine[at : at + 32, :], sine[at : at + 32, :]
+    odd = (lane_n % 192) >= 96
+    for q in range(4):
+        c0, c1 = cos_all[:, 2 * q : 2 * q + 1], cos_all[:, 2 * q + 1 : 2 * q + 2]
+        s0, s1 = sin_all[:, 2 * q : 2 * q + 1], sin_all[:, 2 * q + 1 : 2 * q + 2]
+        c = jnp.where(odd, c1, c0)
+        c = jnp.where(lane_n < 192, c, -c)[None]
+        d = -jnp.where(odd, s1, s0)[None]
+        for row, a, b in both:
+            y = c * a + d * b
+            right[pl.ds(row, 96), q * 384 : (q + 1) * 384] = y.reshape(96, 384).astype(BF16)
+
+
+def multiply(left, right, acc, first, n):
+    at = slice(n * 256, (n + 1) * 256)
+    part = jnp.dot(left[...], right[:, at], preferred_element_type=F32)
+    if first:
+        acc[:, at] = part
+    else:
+        acc[:, at] += part
+
+
+def two_planes(place, col, sign_re, sign_im, sols, eigs, planes, tables, lefts, rights, acc, first):
+    half = place[2]
+    cosine, sine = tables
+    for m in range(4):
+        build_right(half, eigs, planes[0], cosine, sine, rights[0], m)
+    build_left(sols[0], col, sign_re, sign_im, lefts[0])
+    for n in range(6):
+        multiply(lefts[0], rights[0], acc, first, n)
+        if n < 4:
+            build_right(half, eigs, planes[1], cosine, sine, rights[1], n)
+        if n == 4:
+            build_left(sols[1], col, sign_re, sign_im, lefts[1])
+    for n in range(6):
+        multiply(lefts[1], rights[1], acc, False, n)
+
+
+def first_kernel(place, col, sign_re, sign_im, *refs):
+    sols, eigs, tables, acc = refs[:2], refs[2:10], refs[10:12], refs[12]
+    lefts, rights = refs[13:15], refs[15:17]
+    two_planes(place, col, sign_re, sign_im, sols, eigs, (0, 1), tables, lefts, rights, acc, True)
+
+
+def last_kernel(place, col, sign_re, sign_im, *refs):
+    sols, eigs, tables, acc_in, out = refs[:2], refs[2:10], refs[10:12], refs[12], refs[13]
+    lefts, rights, acc, pairs = refs[14:16], refs[16:18], refs[18], refs[19]
+    acc[...] = acc_in[...]
+    two_planes(place, col, sign_re, sign_im, sols, eigs, (2, 3), tables, lefts, rights, acc, False)
     flip = jnp.where(lax.broadcasted_iota(jnp.int32, (48, 384), 1) < 192, -1.0, 1.0).astype(F32)
     for q in range(4):
         lanes = slice(q * 384, (q + 1) * 384)
@@ -196,21 +216,29 @@
         out[block, 48:56, :] = tail
 
 
-def local_fields(place, col, sign_re, sign_im, sols, eig, cosine, sine):
+WORK = [pltpu.VMEM((384, 1536), BF16)] * 2 + [pltpu.VMEM((1536, 1536), BF16)] * 2
+
+
+def first_planes(scalars, sols, eigs, tables):
     return pl.pallas_call(
-        fields_kernel,
+        first_kernel,
+        out_shape=jax.ShapeDtypeStruct((384, 1536), F32),
+        in_specs=[SMEM] * 4 + [VMEM] * 12,
+        out_specs=VMEM,
+        scratch_shapes=WORK,
+        compiler_params=pltpu.CompilerParams(vmem_limit_bytes=40 << 20),
+    )(*scalars, *sols, *eigs, *tables)
+
+
+def last_planes(scalars, sols, eigs, tables, acc):
+    return pl.pallas_call(
+        last_kernel,
         out_shape=jax.ShapeDtypeStruct((16, 56, 384), BF16),
-        in_specs=[SMEM] * 4 + [VMEM] * 7,
+        in_specs=[SMEM] * 4 + [VMEM] * 13,
         out_specs=VMEM,
-        scratch_shapes=[
-            pltpu.VMEM((384, 1536), BF16),
-            pltpu.VMEM((1536, 1536), BF16),
-            pltpu.VMEM((384, 1536), F32),
-            pltpu.VMEM((8, 128), F32),
-            pltpu.VMEM((32, 1536), F32),
-        ],
-        compiler_params=pltpu.CompilerParams(vmem_limit_bytes=48 << 20),
-    )(place, col, sign_re, sign_im, *sols, eig, cosine, sine)
+        scratch_shapes=WORK + [pltpu.VMEM((384, 1536), F32), pltpu.VMEM((32, 1536), F32)],
+        compiler_params=pltpu.CompilerParams(vmem_limit_bytes=40 << 20),
+    )(*scalars, *sols, *eigs, *tables, acc)
 
 
 def join_kernel(blocks, out):
@@ -237,6 +265,11 @@
 
 def swap(x, axis, mask):
     return lax.ppermute(x, axis, [(i, i ^ mask) for i in range(lax.axis_size(axis))])
+
+
+def swap_both(x):
+    pairs = [(i * 2 + y, (i ^ 2) * 2 + (y ^ 1)) for i in range(4) for y in range(2)]
+    return lax.ppermute(x, ("plane", "mode"), pairs)
 
 
 def fast_body(eigvecs, solutions, momenta, gammas):
@@ -250,7 +283,11 @@
     eig_planes = [eig_own[0]] + [swap(eig_own[k], "z", k) for k in range(1, 4)]
     sol_plane = gather_plane([sol_own[0]] + [swap(sol_own[k], "plane", k) for k in range(1, 4)])
     sols = [sol_plane] + [swap(sol_plane, "z", k) for k in range(1, 4)]
-    eig_all = lax.all_gather(jnp.stack(eig_planes), ("plane", "mode")).reshape(4, 2, 4, 96, 384)
+    mine = jnp.stack(eig_planes)
+    chip = [mine, swap(mine, "mode", 1), swap(mine, "plane", 2)]
+    chip.append(swap_both(mine))
+    core = [swap(block, "plane", 1) for block in chip]
+    eigs = [chip[0], chip[1], core[0], core[1], chip[2], chip[3], core[2], core[3]]
 
     table = gamma_table()
     col_table = jnp.asarray(np.argmax(np.abs(table), axis=2).astype(np.int32))
@@ -270,9 +307,9 @@
     ) % LATT
     theta = 2.0 * math.pi / LATT * phase_int.astype(F32)
 
-    sent = local_fields(
-        place, col, sign_re, sign_im, sols, eig_all, jnp.cos(theta), jnp.sin(theta)
-    )
+    scalars, tables = (place, col, sign_re, sign_im), (jnp.cos(theta), jnp.sin(theta))
+    acc = first_planes(scalars, sols[:2], eigs, tables)
+    sent = last_planes(scalars, sols[2:], eigs, tables, acc)
     got = lax.all_to_all(sent, ("z", "plane"), 0, 0, tiled=True)
     part = jnp.sum(got[:, 48:, :64].astype(F32), axis=0)
     part = part[:, :32] + part[:, 32:]

time: 127 us -> 92.5 us (0.73)
  waiting for transfers between devices: 31 us -> 15.2 us
  between operations: 14.1 us -> 0.79 us
  Pallas kernels: 32.4 us -> 24.3 us
  starting transfers between devices: 13.5 us -> 20.3 us
  local copies, waits for them, and re-layouts: 8.22 us -> 5.92 us
    ppermute x10 -> x16, waiting for transfers between devices: 31 us -> 12.9 us  [swap(): lax.ppermute(x, axis, [(i, i ^ mask) for i in range(lax.axis_size(axis))])]
    pallas_call x1 -> x2, Pallas kernels: 28.2 us -> 20.1 us  [the longest x1 10.4 us: last_planes(): pl.pallas_call(last_kernel, out_shape=jax.ShapeDtypeStruct((16, 56, 384),...]
    ppermute x10 -> x16, starting transfers between devices: 13.4 us -> 18.8 us  [swap(): lax.ppermute(x, axis, [(i, i ^ mask) for i in range(lax.axis_size(axis))])]
    ppermute x0 -> x1, waiting for transfers between devices: none -> 2.32 us  [swap_both(): return lax.ppermute(x, ('plane', 'mode'), pairs)]
    unnamed x18 -> x16, local copies, waits for them, and re-layouts: 5.94 us -> 3.65 us
    ppermute x0 -> x1, starting transfers between devices: none -> 1.55 us  [swap_both(): return lax.ppermute(x, ('plane', 'mode'), pairs)]
  transfers between devices with their start and end apart: 11 -> 17, of which waited for: 6 -> 6; matrix products, arithmetic and copies ran while one was open for 4% -> 5% of each run, Pallas kernels for 3% -> 14%
where the time goes in v2:
time: 92.5 us; the launch traced here: 92.2 us
  Pallas kernels  24.3 us (26%)
  blocking collectives  22.2 us (24%)
  starting transfers between devices  20.3 us (22%)
  waiting for transfers between devices  15.2 us (16%)
  local copies, waits for them, and re-layouts  5.92 us (6%)
  other arithmetic  3.39 us (4%)
    all_to_all x1, blocking collectives, fast_body(): got = lax.all_to_all(sent, ('z', 'plane'), 0, 0, tiled=True)  22.2 us
    ppermute x16, starting transfers between devices, swap(): lax.ppermute(x, axis, [(i, i ^ mask) for i in range(lax.axis_size(axis))])  18.8 us
    ppermute x16, waiting for transfers between devices, swap(): lax.ppermute(x, axis, [(i, i ^ mask) for i in range(lax.axis_size(axis))])  12.9 us
    pallas_call x1, Pallas kernels, last_planes(): pl.pallas_call(last_kernel, out_shape=jax.ShapeDtypeStruct((16, 56, 384),...  10.4 us
    pallas_call x1, Pallas kernels, first_planes(): pl.pallas_call(first_kernel, out_shape=jax.ShapeDtypeStruct((384, 1536),...  9.62 us
    unnamed x16, local copies, waits for them, and re-layouts  3.65 us
    ppermute x1, waiting for transfers between devices, swap_both(): return lax.ppermute(x, ('plane', 'mode'), pairs)  2.32 us
    pallas_call x1, Pallas kernels, gather_plane(): pl.pallas_call(gather_kernel, out_shape=jax.ShapeDtypeStruct((8, 48, 384)...  1.97 us
  transfers between devices with their start and end apart: 17, of which 6 were waited for; matrix products, arithmetic and copies ran while one was open for 5% of the time, Pallas kernels for 14%

profile of v2, /device:TPU:0, one launch (start us, length us, event | category | flops | bytes accessed | tf_op | source)
XLA Modules:
  0.0 92.2 jit_solution(8326560174162970457)
XLA Ops:
  0.7 1.1 %copy-done.1 = bf16[2,32,12,384]{3,1,2,0:T(8,128)(2,1)S(1)} copy-done((bf16[2,32,12,384]{3,1,2,0:T(8,128)(2,1)S(1)}, bf16[2,32,12,384]{3,1,2,0:T(8,128)(2,1)}, u32[]{:S(2)}) %copy-start.1) | copy-done | bytes 589848
  1.8 1.0 %copy-done.2 = bf16[2,32,12,192]{3,1,2,0:T(8,128)(2,1)S(1)} copy-done((bf16[2,32,12,192]{3,1,2,0:T(8,128)(2,1)S(1)}, bf16[2,32,12,192]{3,1,2,0:T(8,128)(2,1)}, u32[]{:S(2)}) %copy-start.2) | copy-done | bytes 294936
  2.8 1.0 %shard_map.86 = (bf16[96,384]{1,0:T(8,128)(2,1)S(1)}, bf16[96,384]{1,0:T(8,128)(2,1)S(1)}, bf16[96,384]{1,0:T(8,128)(2,1)S(1)}, bf16[96,384]{1,0:T(8,128)(2,1)S(...) custom-call(s32[3]{0:T(128)S(1)} %pad_add_fusion.place, ...), custom_call_target="tpu_custom_call" | custom-call | tf_op jit(solution)/shard_map/pallas_call | solution.py:74
  3.8 0.5 collective-permute-start
  4.3 2.6 %collective-permute-start.1 = (bf16[48,768]{1,0:T(8,128)(2,1)S(1)}, bf16[48,768]{1,0:T(8,128)(2,1)S(1)}, u32[]{:S(2)}, u32[]{:S(2)}) collective-permute-start(bf16[48,768]{1,0:T(8,128)(2,1)S(1)} %get-tuple-element.12), channel_id=1, source_target_pairs={{0,4},{2,6},{4,0},{6,2},{1,5},{3,7},{5,1},{7,3},{8,12},{10,14},{12... | collective-permute-start | bytes 221192 | tf_op jit(solution)/shard_map/ppermute | solution.py:267
  6.8 1.6 %collective-permute-start.5 = (bf16[96,384]{1,0:T(8,128)(2,1)S(1)}, bf16[96,384]{1,0:T(8,128)(2,1)S(1)}, u32[]{:S(2)}, u32[]{:S(2)}) collective-permute-start(bf16[96,384]{1,0:T(8,128)(2,1)S(1)} %get-tuple-element.15), channel_id=1, source_target_pairs={{0,8},{8,0},{16,24},{24,16},{1,9},{9,1},{17,25},{25,17},{2,10},{10... | collective-permute-start | bytes 221192 | tf_op jit(solution)/shard_map/ppermute | solution.py:267
  8.4 2.6 %collective-permute-start.6 = (bf16[96,384]{1,0:T(8,128)(2,1)S(1)}, bf16[96,384]{1,0:T(8,128)(2,1)S(1)}, u32[]{:S(2)}, u32[]{:S(2)}) collective-permute-start(bf16[96,384]{1,0:T(8,128)(2,1)S(1)} %get-tuple-element.16), channel_id=1, source_target_pairs={{0,16},{8,24},{16,0},{24,8},{1,17},{9,25},{17,1},{25,9},{2,18},{10... | collective-permute-start | bytes 221192 | tf_op jit(solution)/shard_map/ppermute | solution.py:267
  11.4 0.8 slice_bitcast_fusion.2
  12.6 0.7 iota_compare_fusion
  13.4 3.9 %collective-permute-done.6 = bf16[96,384]{1,0:T(8,128)(2,1)S(1)} collective-permute-done((bf16[96,384]{1,0:T(8,128)(2,1)S(1)}, bf16[96,384]{1,0:T(8,128)(2,1)S(1)}, u32[]{:S(2)}, u32[]{:S(2)}) %collective-permute-start.6) | collective-permute-done | bytes 73760 | tf_op jit(solution)/shard_map/ppermute | solution.py:267
  17.3 1.6 %collective-permute-start.12 = (bf16[4,96,384]{2,1,0:T(8,128)(2,1)S(1)}, bf16[4,96,384]{2,1,0:T(8,128)(2,1)S(1)}, u32[]{:S(2)}, u32[]{:S(2)}) collective-permute-start(bf16[4,96,384]{2,1,0:T(8,128)(2,1)S(1)} %pad_maximum_fusion.refs_2_), channel_id=1, source_target_pairs={{0,5},{1,4},{2,7},{3,6},{4,1},{5,0},{6,3},{7,2},{8,13},{9,12},{10,... | collective-permute-start | bytes 884744 | tf_op jit(solution)/shard_map/ppermute | solution.py:272
  18.9 1.5 %collective-permute-start.11 = (bf16[4,96,384]{2,1,0:T(8,128)(2,1)S(1)}, bf16[4,96,384]{2,1,0:T(8,128)(2,1)S(1)}, u32[]{:S(2)}, u32[]{:S(2)}) collective-permute-start(bf16[4,96,384]{2,1,0:T(8,128)(2,1)S(1)} %pad_maximum_fusion.refs_2_), channel_id=1, source_target_pairs={{0,4},{2,6},{4,0},{6,2},{1,5},{3,7},{5,1},{7,3},{8,12},{10,14},{12... | collective-permute-start | bytes 884744 | tf_op jit(solution)/shard_map/ppermute | solution.py:267
  20.4 0.6 collective-permute-start.8
  21.1 0.6 copy-done.6
  21.6 2.0 %shard_map.87.refs_0_ = bf16[8,48,384]{2,1,0:T(8,128)(2,1)} custom-call(bf16[48,768]{1,0:T(8,128)(2,1)} %copy-done.3, bf16[48,768]{1,0:T(8,128)(2,1)} %copy-done.4, bf16[48,768]{1,0:T(8,128)(2,1)} %copy-done.5, bf16[48,768]{1,0:T(8,128)(2,1)} %copy-done.6), custom_call_target="tpu_custom_call" | custom-call | tf_op jit(solution)/shard_map/pallas_call | solution.py:96
  23.6 1.5 %collective-permute-start.15 = (bf16[8,48,384]{2,1,0:T(8,128)(2,1)}, bf16[8,48,384]{2,1,0:T(8,128)(2,1)S(1)}, u32[]{:S(2)}, u32[]{:S(2)}) collective-permute-start(bf16[8,48,384]{2,1,0:T(8,128)(2,1)} %shard_map.87.refs_0_), channel_id=1, source_target_pairs={{0,8},{8,0},{16,24},{24,16},{1,9},{9,1},{17,25},{25,17},{2,10},{10... | collective-permute-start | bytes 884744 | tf_op jit(solution)/shard_map/ppermute | solution.py:267
  25.1 0.8 select_reduce_fusion
  25.9 2.3 %collective-permute-done.12.refs_7_ = bf16[4,96,384]{2,1,0:T(8,128)(2,1)S(1)} collective-permute-done((bf16[4,96,384]{2,1,0:T(8,128)(2,1)S(1)}, bf16[4,96,384]{2,1,0:T(8,128)(2,1)S(1)}, u32[]{:S(2)}, u32[]{:S(2)}) %collective-permute-start.12) | collective-permute-done | bytes 294944 | tf_op jit(solution)/shard_map/ppermute | solution.py:272
  28.3 2.5 %collective-permute-start.4 = (bf16[8,48,384]{2,1,0:T(8,128)(2,1)}, bf16[8,48,384]{2,1,0:T(8,128)(2,1)S(1)}, u32[]{:S(2)}, u32[]{:S(2)}) collective-permute-start(bf16[8,48,384]{2,1,0:T(8,128)(2,1)} %shard_map.87.refs_0_), channel_id=1, source_target_pairs={{0,24},{8,16},{16,8},{24,0},{1,25},{9,17},{17,9},{25,1},{2,26},{10... | collective-permute-start | bytes 884744 | tf_op jit(solution)/shard_map/ppermute | solution.py:267
  30.8 1.2 %collective-permute-done.11.refs_6_ = bf16[4,96,384]{2,1,0:T(8,128)(2,1)S(1)} collective-permute-done((bf16[4,96,384]{2,1,0:T(8,128)(2,1)S(1)}, bf16[4,96,384]{2,1,0:T(8,128)(2,1)S(1)}, u32[]{:S(2)}, u32[]{:S(2)}) %collective-permute-start.11) | collective-permute-done | bytes 294944 | tf_op jit(solution)/shard_map/ppermute | solution.py:267
  31.9 3.1 %collective-permute-start.3 = (bf16[8,48,384]{2,1,0:T(8,128)(2,1)}, bf16[8,48,384]{2,1,0:T(8,128)(2,1)S(1)}, u32[]{:S(2)}, u32[]{:S(2)}) collective-permute-start(bf16[8,48,384]{2,1,0:T(8,128)(2,1)} %shard_map.87.refs_0_), channel_id=1, source_target_pairs={{0,16},{8,24},{16,0},{24,8},{1,17},{9,25},{17,1},{25,9},{2,18},{10... | collective-permute-start | bytes 884744 | tf_op jit(solution)/shard_map/ppermute | solution.py:267
  35.1 0.5 collective-permute-start.13
  36.2 1.2 %multiply_sine_fusion = (f32[512,8]{1,0:T(8,128)S(1)}, f32[512,8]{1,0:T(8,128)S(1)}) fusion(f32[512,8]{1,0:T(8,128)S(1)} %copy.12), kind=kLoop, calls=%fused_computation.1 | loop fusion | flops 4096 | bytes 49152 | tf_op jit(solution)/shard_map/sin | solution.py:310
  37.5 1.0 %copy-done = bf16[8,48,384]{2,1,0:T(8,128)(2,1)S(1)} copy-done((bf16[8,48,384]{2,1,0:T(8,128)(2,1)S(1)}, bf16[8,48,384]{2,1,0:T(8,128)(2,1)}, u32[]{:S(2)}) %copy-start) | copy-done | bytes 294936
  38.4 9.6 %shard_map.88.refs_12_ = f32[384,1536]{1,0:T(8,128)S(1)} custom-call(s32[3]{0:T(128)S(1)} %pad_add_fusion.place, s32[16]{0:T(128)S(1)} %reshape.117.col, f32[16]{0:T(128)S(1)} %reshape.118.sign_re, f32[16]{0:T(128)S(1)} %reshape.119.sign_im, bf16[8,48,384]{2,1,0:T(8,128)(2,1)S(1)} %copy-done, bf16[8,48,384]{2,1,0:T(8,128)(2,1)S(1)} %collective-permute-done.15.refs_1_, ...), custom_call_target="tpu_custom_call" | custom-call | tf_op jit(solution)/shard_map/pallas_call | solution.py:223
  48.1 7.0 %collective-permute-done.3.refs_0_ = bf16[8,48,384]{2,1,0:T(8,128)(2,1)S(1)} collective-permute-done((bf16[8,48,384]{2,1,0:T(8,128)(2,1)}, bf16[8,48,384]{2,1,0:T(8,128)(2,1)S(1)}, u32[]{:S(2)}, u32[]{:S(2)}) %collective-permute-start.3) | collective-permute-done | bytes 294944 | tf_op jit(solution)/shard_map/ppermute | solution.py:267
  55.0 10.4 %shard_map.89 = bf16[16,56,384]{2,1,0:T(8,128)(2,1)S(1)} custom-call(s32[3]{0:T(128)S(1)} %pad_add_fusion.place, s32[16]{0:T(128)S(1)} %reshape.117.col, f32[16]{0:T(128)S(1)} %reshape.118.sign_re, f32[16]{0:T(128)S(1)} %reshape.119.sign_im, bf16[8,48,384]{2,1,0:T(8,128)(2,1)S(1)} %collective-permute-done.3.refs_0_, ...), custom_call_target="tpu_custom_call" | custom-call | tf_op jit(solution)/shard_map/pallas_call | solution.py:234
  65.5 22.2 %all_to_all.5.blocks = bf16[16,56,384]{2,1,0:T(8,128)(2,1)S(1)} all-to-all(bf16[16,56,384]{2,1,0:T(8,128)(2,1)S(1)} %shard_map.89), channel_id=1, replica_groups=mesh['z'=4,'plane'=4,'mode'=2] {'z','plane'}, dimensions={0} | all-to-all | bytes 1376256 | tf_op jit(solution)/shard_map/all_to_all | solution.py:313
  87.8 1.5 %collective-permute-start.16 = (f32[8,32]{1,0:T(8,128)S(1)}, f32[8,32]{1,0:T(8,128)S(1)}, u32[]{:S(2)}, u32[]{:S(2)}) collective-permute-start(f32[8,32]{1,0:T(8,128)S(1)} %slice_add_fusion), channel_id=1, source_target_pairs={{0,1},{1,0},{2,3},{3,2},{4,5},{5,4},{6,7},{7,6},{8,9},{9,8},{10,11... | collective-permute-start | bytes 3080 | tf_op jit(solution)/shard_map/ppermute | solution.py:267
  89.4 1.3 %shard_map.90 = f32[2,192,768]{2,1,0:T(8,128)} custom-call(bf16[16,56,384]{2,1,0:T(8,128)(2,1)S(1)} %all_to_all.5.blocks), custom_call_target="tpu_custom_call" | custom-call | tf_op jit(solution)/shard_map/pallas_call | solution.py:257
  90.7 0.8 collective-permute-done.16
  91.5 0.7 copy.13
  (49 shorter events, 2.0 us)
Async XLA Ops:
  0.6 35.0 %copy-start.7 = (s32[16,4]{0,1:T(4,128)S(1)}, s32[16,4]{0,1:T(4,128)}, u32[]{:S(2)}) copy-start(s32[16,4]{0,1:T(4,128)} %constant.64.clone) | copy-start | bytes 772
  0.7 1.1 %copy-start.1 = (bf16[2,32,12,384]{3,1,2,0:T(8,128)(2,1)S(1)}, bf16[2,32,12,384]{3,1,2,0:T(8,128)(2,1)}, u32[]{:S(2)}) copy-start(bf16[2,32,12,384]{3,1,2,0:T(8,128)(2,1)} %param.7) | copy-start | bytes 1769476
  1.8 1.0 %copy-start.2 = (bf16[2,32,12,192]{3,1,2,0:T(8,128)(2,1)S(1)}, bf16[2,32,12,192]{3,1,2,0:T(8,128)(2,1)}, u32[]{:S(2)}) copy-start(bf16[2,32,12,192]{3,1,2,0:T(8,128)(2,1)} %param.8) | copy-start | bytes 884740
  3.7 16.7 %copy-start.3 = (bf16[48,768]{1,0:T(8,128)(2,1)}, bf16[48,768]{1,0:T(8,128)(2,1)S(1)}, u32[]{:S(2)}) copy-start(bf16[48,768]{1,0:T(8,128)(2,1)S(1)} %get-tuple-element.10.refs_0_) | copy-start | bytes 221188
  3.8 16.6 %collective-permute-start = (bf16[48,768]{1,0:T(8,128)(2,1)S(1)}, bf16[48,768]{1,0:T(8,128)(2,1)S(1)}, u32[]{:S(2)}, u32[]{:S(2)}) collective-permute-start(bf16[48,768]{1,0:T(8,128)(2,1)S(1)} %get-tuple-element.11), channel_id=1, source_target_pairs={{0,2},{2,0},{4,6},{6,4},{1,3},{3,1},{5,7},{7,5},{8,10},{10,8},{12,... | collective-permute-start | bytes 221192 | tf_op jit(solution)/shard_map/ppermute | solution.py:267
  4.3 16.1 %collective-permute-start.1 = (bf16[48,768]{1,0:T(8,128)(2,1)S(1)}, bf16[48,768]{1,0:T(8,128)(2,1)S(1)}, u32[]{:S(2)}, u32[]{:S(2)}) collective-permute-start(bf16[48,768]{1,0:T(8,128)(2,1)S(1)} %get-tuple-element.12), channel_id=1, source_target_pairs={{0,4},{2,6},{4,0},{6,2},{1,5},{3,7},{5,1},{7,3},{8,12},{10,14},{12... | collective-permute-start | bytes 221192 | tf_op jit(solution)/shard_map/ppermute | solution.py:267
  6.8 6.5 %collective-permute-start.5 = (bf16[96,384]{1,0:T(8,128)(2,1)S(1)}, bf16[96,384]{1,0:T(8,128)(2,1)S(1)}, u32[]{:S(2)}, u32[]{:S(2)}) collective-permute-start(bf16[96,384]{1,0:T(8,128)(2,1)S(1)} %get-tuple-element.15), channel_id=1, source_target_pairs={{0,8},{8,0},{16,24},{24,16},{1,9},{9,1},{17,25},{25,17},{2,10},{10... | collective-permute-start | bytes 221192 | tf_op jit(solution)/shard_map/ppermute | solution.py:267
  8.4 8.9 %collective-permute-start.6 = (bf16[96,384]{1,0:T(8,128)(2,1)S(1)}, bf16[96,384]{1,0:T(8,128)(2,1)S(1)}, u32[]{:S(2)}, u32[]{:S(2)}) collective-permute-start(bf16[96,384]{1,0:T(8,128)(2,1)S(1)} %get-tuple-element.16), channel_id=1, source_target_pairs={{0,16},{8,24},{16,0},{24,8},{1,17},{9,25},{17,1},{25,9},{2,18},{10... | collective-permute-start | bytes 221192 | tf_op jit(solution)/shard_map/ppermute | solution.py:267
  11.0 6.3 %collective-permute-start.7 = (bf16[96,384]{1,0:T(8,128)(2,1)S(1)}, bf16[96,384]{1,0:T(8,128)(2,1)S(1)}, u32[]{:S(2)}, u32[]{:S(2)}) collective-permute-start(bf16[96,384]{1,0:T(8,128)(2,1)S(1)} %get-tuple-element.17), channel_id=1, source_target_pairs={{0,24},{8,16},{16,8},{24,0},{1,25},{9,17},{17,9},{25,1},{2,26},{10... | collective-permute-start | bytes 221192 | tf_op jit(solution)/shard_map/ppermute | solution.py:267
  13.4 7.6 %collective-permute-start.2 = (bf16[48,768]{1,0:T(8,128)(2,1)S(1)}, bf16[48,768]{1,0:T(8,128)(2,1)S(1)}, u32[]{:S(2)}, u32[]{:S(2)}) collective-permute-start(bf16[48,768]{1,0:T(8,128)(2,1)S(1)} %get-tuple-element.13), channel_id=1, source_target_pairs={{0,6},{2,4},{4,2},{6,0},{1,7},{3,5},{5,3},{7,1},{8,14},{10,12},{12... | collective-permute-start | bytes 221192 | tf_op jit(solution)/shard_map/ppermute | solution.py:267
  17.3 10.9 %collective-permute-start.12 = (bf16[4,96,384]{2,1,0:T(8,128)(2,1)S(1)}, bf16[4,96,384]{2,1,0:T(8,128)(2,1)S(1)}, u32[]{:S(2)}, u32[]{:S(2)}) collective-permute-start(bf16[4,96,384]{2,1,0:T(8,128)(2,1)S(1)} %pad_maximum_fusion.refs_2_), channel_id=1, source_target_pairs={{0,5},{1,4},{2,7},{3,6},{4,1},{5,0},{6,3},{7,2},{8,13},{9,12},{10,... | collective-permute-start | bytes 884744 | tf_op jit(solution)/shard_map/ppermute | solution.py:272
  18.9 13.0 %collective-permute-start.11 = (bf16[4,96,384]{2,1,0:T(8,128)(2,1)S(1)}, bf16[4,96,384]{2,1,0:T(8,128)(2,1)S(1)}, u32[]{:S(2)}, u32[]{:S(2)}) collective-permute-start(bf16[4,96,384]{2,1,0:T(8,128)(2,1)S(1)} %pad_maximum_fusion.refs_2_), channel_id=1, source_target_pairs={{0,4},{2,6},{4,0},{6,2},{1,5},{3,7},{5,1},{7,3},{8,12},{10,14},{12... | collective-permute-start | bytes 884744 | tf_op jit(solution)/shard_map/ppermute | solution.py:267
  20.4 0.6 copy-start.4
  20.4 14.7 %collective-permute-start.9 = (bf16[4,96,384]{2,1,0:T(8,128)(2,1)S(1)}, bf16[4,96,384]{2,1,0:T(8,128)(2,1)S(1)}, u32[]{:S(2)}, u32[]{:S(2)}) collective-permute-start(bf16[4,96,384]{2,1,0:T(8,128)(2,1)S(1)} %pad_maximum_fusion.refs_2_), channel_id=1, source_target_pairs={{0,2},{2,0},{4,6},{6,4},{1,3},{3,1},{5,7},{7,5},{8,10},{10,8},{12,... | collective-permute-start | bytes 884744 | tf_op jit(solution)/shard_map/ppermute | solution.py:267
  20.4 0.6 copy-start.5
  20.4 14.6 %collective-permute-start.8 = (bf16[4,96,384]{2,1,0:T(8,128)(2,1)S(1)}, bf16[4,96,384]{2,1,0:T(8,128)(2,1)S(1)}, u32[]{:S(2)}, u32[]{:S(2)}) collective-permute-start(bf16[4,96,384]{2,1,0:T(8,128)(2,1)S(1)} %pad_maximum_fusion.refs_2_), channel_id=1, source_target_pairs={{0,1},{1,0},{2,3},{3,2},{4,5},{5,4},{6,7},{7,6},{8,9},{9,8},{10,11... | collective-permute-start | bytes 884744 | tf_op jit(solution)/shard_map/ppermute | solution.py:267
  21.0 0.6 copy-start.6
  23.6 12.0 %collective-permute-start.15 = (bf16[8,48,384]{2,1,0:T(8,128)(2,1)}, bf16[8,48,384]{2,1,0:T(8,128)(2,1)S(1)}, u32[]{:S(2)}, u32[]{:S(2)}) collective-permute-start(bf16[8,48,384]{2,1,0:T(8,128)(2,1)} %shard_map.87.refs_0_), channel_id=1, source_target_pairs={{0,8},{8,0},{16,24},{24,16},{1,9},{9,1},{17,25},{25,17},{2,10},{10... | collective-permute-start | bytes 884744 | tf_op jit(solution)/shard_map/ppermute | solution.py:267
  28.3 19.8 %collective-permute-start.4 = (bf16[8,48,384]{2,1,0:T(8,128)(2,1)}, bf16[8,48,384]{2,1,0:T(8,128)(2,1)S(1)}, u32[]{:S(2)}, u32[]{:S(2)}) collective-permute-start(bf16[8,48,384]{2,1,0:T(8,128)(2,1)} %shard_map.87.refs_0_), channel_id=1, source_target_pairs={{0,24},{8,16},{16,8},{24,0},{1,25},{9,17},{17,9},{25,1},{2,26},{10... | collective-permute-start | bytes 884744 | tf_op jit(solution)/shard_map/ppermute | solution.py:267
  31.9 23.1 %collective-permute-start.3 = (bf16[8,48,384]{2,1,0:T(8,128)(2,1)}, bf16[8,48,384]{2,1,0:T(8,128)(2,1)S(1)}, u32[]{:S(2)}, u32[]{:S(2)}) collective-permute-start(bf16[8,48,384]{2,1,0:T(8,128)(2,1)} %shard_map.87.refs_0_), channel_id=1, source_target_pairs={{0,16},{8,24},{16,0},{24,8},{1,17},{9,25},{17,1},{25,9},{2,18},{10... | collective-permute-start | bytes 884744 | tf_op jit(solution)/shard_map/ppermute | solution.py:267
  35.1 2.3 %collective-permute-start.14 = (bf16[4,96,384]{2,1,0:T(8,128)(2,1)S(1)}, bf16[4,96,384]{2,1,0:T(8,128)(2,1)S(1)}, u32[]{:S(2)}, u32[]{:S(2)}) collective-permute-start(bf16[4,96,384]{2,1,0:T(8,128)(2,1)S(1)} %collective-permute-done.12.refs_7_), channel_id=1, source_target_pairs={{0,2},{2,0},{4,6},{6,4},{1,3},{3,1},{5,7},{7,5},{8,10},{10,8},{12,... | collective-permute-start | bytes 884744 | tf_op jit(solution)/shard_map/ppermute | solution.py:267
  35.1 2.3 %collective-permute-start.13 = (bf16[4,96,384]{2,1,0:T(8,128)(2,1)S(1)}, bf16[4,96,384]{2,1,0:T(8,128)(2,1)S(1)}, u32[]{:S(2)}, u32[]{:S(2)}) collective-permute-start(bf16[4,96,384]{2,1,0:T(8,128)(2,1)S(1)} %collective-permute-done.11.refs_6_), channel_id=1, source_target_pairs={{0,2},{2,0},{4,6},{6,4},{1,3},{3,1},{5,7},{7,5},{8,10},{10,8},{12,... | collective-permute-start | bytes 884744 | tf_op jit(solution)/shard_map/ppermute | solution.py:267
  35.6 1.9 %collective-permute-start.10 = (bf16[4,96,384]{2,1,0:T(8,128)(2,1)S(1)}, bf16[4,96,384]{2,1,0:T(8,128)(2,1)S(1)}, u32[]{:S(2)}, u32[]{:S(2)}) collective-permute-start(bf16[4,96,384]{2,1,0:T(8,128)(2,1)S(1)} %collective-permute-done.8.refs_3_), channel_id=1, source_target_pairs={{0,2},{2,0},{4,6},{6,4},{1,3},{3,1},{5,7},{7,5},{8,10},{10,8},{12,... | collective-permute-start | bytes 884744 | tf_op jit(solution)/shard_map/ppermute | solution.py:267
  37.5 1.0 %copy-start = (bf16[8,48,384]{2,1,0:T(8,128)(2,1)S(1)}, bf16[8,48,384]{2,1,0:T(8,128)(2,1)}, u32[]{:S(2)}) copy-start(bf16[8,48,384]{2,1,0:T(8,128)(2,1)} %shard_map.87.refs_0_) | copy-start | bytes 884740
  87.8 3.6 %collective-permute-start.16 = (f32[8,32]{1,0:T(8,128)S(1)}, f32[8,32]{1,0:T(8,128)S(1)}, u32[]{:S(2)}, u32[]{:S(2)}) collective-permute-start(f32[8,32]{1,0:T(8,128)S(1)} %slice_add_fusion), channel_id=1, source_target_pairs={{0,1},{1,0},{2,3},{3,2},{4,5},{5,4},{6,7},{7,6},{8,9},{9,8},{10,11... | collective-permute-start | bytes 3080 | tf_op jit(solution)/shard_map/ppermute | solution.py:267

commit v3 on v0

--- a/solution.py
+++ b/solution.py
@@ -1,17 +1,21 @@
+import functools
 import math
 
 import jax
 import jax.numpy as jnp
 import numpy as np
 from jax import lax
+from jax.experimental import pallas as pl
+from jax.experimental.pallas import tpu as pltpu
+from jax.sharding import Mesh
 from jax.sharding import PartitionSpec as P
 
 LATT = 96
-
-
-def shifted(x, axis, by):
-    count = lax.axis_size(axis)
-    return lax.ppermute(x, axis, [(i, (i + by) % count) for i in range(count)])
+VMEM = pl.BlockSpec(memory_space=pltpu.VMEM)
+SMEM = pl.BlockSpec(memory_space=pltpu.SMEM)
+HBM = pl.BlockSpec(memory_space=pltpu.HBM)
+BF16 = jnp.bfloat16
+F32 = jnp.float32
 
 
 def gamma_table():
@@ -28,12 +32,358 @@
             if number >> bit_pos & 1:
                 matrix = matrix @ basis[bit_pos]
         table.append(matrix)
-    table = np.stack(table)
-    return (table.real.astype(np.float32), table.imag.astype(np.float32))
+    return np.stack(table)
+
+
+def shift_lanes(x, by):
+    by = by % x.shape[-1]
+    return x if by == 0 else pltpu.roll(x, by, x.ndim - 1)
+
+
+def by_quarter(lane, first, second, third, fourth):
+    tiles = []
+    for k, (low, high) in enumerate(((first, second), (second, third), (third, fourth))):
+        at = slice(k * 128, (k + 1) * 128)
+        tiles.append(jnp.where(lane[:, at] < (k + 1) * 96, wide(low, at), wide(high, at)))
+    return jnp.concatenate(tiles, axis=1)
+
+
+def wide(x, at):
+    return x[:, at] if x.shape[1] > 1 else x
+
+
+def here():
+    return lax.axis_index("z"), lax.axis_index("x"), lax.axis_index("core")
+
+
+def prepare_sol_kernel(sol, sol_own, sol_other, turned):
+    x = lax.axis_index("x")
+    for r in range(2):
+        flipped = sol[r].astype(F32).T.astype(BF16)
+        for k in range(2):
+            turned[k, :, r * 384 : (r + 1) * 384] = flipped[k * 96 : (k + 1) * 96]
+    sol_own[...] = turned[x]
+    sol_other[...] = turned[x ^ 1]
+
+
+def prepare_sol(sol):
+    return pl.pallas_call(
+        prepare_sol_kernel,
+        out_shape=[jax.ShapeDtypeStruct((96, 768), BF16)] * 2,
+        in_specs=[VMEM],
+        out_specs=[VMEM] * 2,
+        scratch_shapes=[pltpu.VMEM((2, 96, 768), BF16)],
+        compiler_params=pltpu.CompilerParams(vmem_limit_bytes=16 << 20),
+    )(sol)
+
+
+def prepare_eig_kernel(momenta, eig, after, full, *rest):
+    eig_out, (cosine, sine, packs) = rest[:3], rest[3:]
+    (z, x, core), half = here(), lax.axis_index("mode")
+    lane = lax.broadcasted_iota(jnp.int32, (96, 384), 1)
+    for side in range(2):
+        at = side * 192
+        parts = [
+            eig[r, at + low * 96 : at + low * 96 + 96, :].astype(F32)
+            for low in range(2)
+            for r in range(2)
+        ]
+        for quarter in range(4):
+            moved = [shift_lanes(part, 96 * (k - quarter)) for k, part in enumerate(parts)]
+            packs[quarter, side] = by_quarter(lane, *moved).astype(BF16)
+    full[0:96] = packs[z, 0]
+    full[96:192] = packs[z, 1]
+    for k in range(1, 4):
+        eig_out[k - 1][...] = packs[z ^ k, half]
+    shape = cosine.shape[::-1]
+    mom = lax.broadcasted_iota(jnp.int32, shape, 0)
+    lane = lax.broadcasted_iota(jnp.int32, shape, 1)
+    device = (z * 4 + x * 2 + core) ^ ((lane >> 5) << 1)
+    site = (device * 32 + (lane & 31)).astype(F32)
+    line = jnp.floor((site + 0.5) * (1.0 / LATT))
+    coord_x = jnp.floor((line + 0.5) * (1.0 / LATT))
+    coords = (coord_x, line - LATT * coord_x, site - LATT * line)
+    steps = jnp.zeros(shape, F32)
+    for axis, coord in enumerate(coords):
+        factor = jnp.zeros(shape, F32)
+        for p in range(8):
+            factor = jnp.where(mom == p, momenta[axis, p].astype(F32), factor)
+        steps += factor * coord
+    steps -= LATT * jnp.floor((steps + 0.5) * (1.0 / LATT))
+    theta = 2.0 * math.pi / LATT * steps
+    cosine[...] = jnp.cos(theta).T
+    sine[...] = jnp.sin(theta).T
+
+
+def prepare_eig(momenta, eig, after):
+    return pl.pallas_call(
+        prepare_eig_kernel,
+        out_shape=[jax.ShapeDtypeStruct((192, 384), BF16)]
+        + [jax.ShapeDtypeStruct((96, 384), BF16)] * 3
+        + [jax.ShapeDtypeStruct((256, 8), F32)] * 2,
+        in_specs=[SMEM, VMEM, HBM],
+        out_specs=[VMEM] * 6,
+        scratch_shapes=[pltpu.VMEM((4, 2, 96, 384), BF16)],
+        compiler_params=pltpu.CompilerParams(vmem_limit_bytes=16 << 20),
+    )(momenta, eig, after)
+
+
+def build_base(first, second, base):
+    lane = lax.broadcasted_iota(jnp.int32, (96, 384), 1)
+    parts = [
+        [plane[m, :, r * 384 : (r + 1) * 384].astype(F32) for plane in (first, second) for m in range(2)]
+        for r in range(2)
+    ]
+    for t in range(4):
+        re, im = [
+            by_quarter(lane, *[shift_lanes(x, 96 * (k - t)) for k, x in enumerate(part)])
+            for part in parts
+        ]
+        for turn, x in enumerate((re, -im, -re, im)):
+            base[turn * 4 + t] = x.astype(BF16)
+
+
+def build_left(base, gammas, table, left):
+    for g in range(4):
+        for part in range(2):
+            at = g * 192 + part * 96
+            for s in range(4):
+                source = table[gammas[g] * 8 + part * 4 + s]
+                left[at : at + 96, s * 384 : (s + 1) * 384] = base[source]
+
+
+def build_phases(cosine, sine, at, phases):
+    lane = lax.broadcasted_iota(jnp.int32, (32, 384), 1)
+    for part, table in enumerate((cosine, sine)):
+        rows = table[at : at + 32, :]
+        for h in range(2):
+            four = [rows[:, p : p + 1] for p in (2 * h, 2 * h + 1, 2 * h + 4, 2 * h + 5)]
+            phases[h, part] = by_quarter(lane, *four)
+
+
+def build_right(blocks, k, m, cosine, sine, right, phases, spread):
+    lane = lax.broadcasted_iota(jnp.int32, (96, 384), 1)
+    build_phases(cosine, sine, (k * 2 + m) * 32, phases)
+    for side, (spin, block) in enumerate(blocks):
+        w = block.astype(F32)
+        turns = [shift_lanes(w, 96 * by) for by in range(4)]
+        for part in range(4):
+            x = by_quarter(lane, *[turns[(k4 - part) % 4] for k4 in range(4)])
+            spread[side, part] = -x if part % 2 else x
+    for h in range(2):
+        cos, sin = phases[h, 0][None], phases[h, 1][None]
+        for side, (spin, _) in enumerate(blocks):
+            for low in range(2):
+                re = spread[side, low * 2].reshape(3, 32, 384)
+                im = spread[side, low * 2 + 1].reshape(3, 32, 384)
+                at = (spin + low) * 384 + (k % 2) * 192 + m * 96
+                rows = slice(at, at + 96)
+                right[h, rows, 0:384] = (cos * re + sin * im).reshape(96, 384).astype(BF16)
+                right[h, rows, 384:768] = (cos * im - sin * re).reshape(96, 384).astype(BF16)
+
+
+def far_blocks(eigs, k, m):
+    x = lax.axis_index("x")
+    return [(half * 2, eigs[x ^ m, half, k - 1]) for half in range(2)]
+
+
+def product(left, right, side, n):
+    at = slice(n * 256, (n + 1) * 256)
+    return at, jnp.dot(left[...], right[side, :, at], preferred_element_type=F32)
+
+
+def near_kernel(gammas, table, *refs):
+    sols, fulls, eigs, (cosine, sine) = refs[:2], refs[2:4], refs[4], refs[5:7]
+    accs, far_right, (base, left, right, phases, spread) = refs[7:9], refs[9], refs[10:]
+    work = (phases, spread)
+    for m in range(2):
+        blocks = [(0, fulls[m][0:96]), (2, fulls[m][96:192])]
+        build_right(blocks, 0, m, cosine, sine, right, *work)
+    build_base(*sols, base)
+    build_left(base, gammas, table, left)
+    for k in range(1, 4):
+        for m in range(2):
+            build_right(far_blocks(eigs, k, m), k, m, cosine, sine, far_right if k > 1 else right, *work)
+    core = lax.axis_index("core")
+    for acc, side in ((accs[0], core), (accs[1], core ^ 1)):
+        for n in range(3):
+            at, part = product(left, right, side, n)
+            acc[:, at] = part
+
+
+def given_kernel(gammas, table, first, second, right, acc, out, left, base):
+    build_base(first, second, base)
+    build_left(base, gammas, table, left)
+    for n in range(3):
+        at, part = product(left, right, lax.axis_index("core") ^ 1, n)
+        out[:, at] = (acc[:, at] + part).astype(BF16)
+
+
+def own_kernel(left, right, acc, out):
+    for n in range(3):
+        at, part = product(left, right, lax.axis_index("core"), n)
+        out[:, at] = acc[:, at] + part
+
+
+def finish_kernel(own, got, *rest):
+    outs, pairs = rest[:8], rest[8]
+    z, x, _ = here()
+    low = lax.broadcasted_iota(jnp.int32, (96, 384), 1) < 192
+    gs, res, ims = [z ^ k for k in range(4)], [], []
+    for k in range(4):
+        (a, b), (c, d) = [
+            [
+                own[pl.ds(at, 96), lanes] + got[pl.ds(at, 96), lanes].astype(F32)
+                for lanes in (slice(0, 384), slice(384, 768))
+            ]
+            for at in (pl.multiple_of(gs[k] * 192, 96), pl.multiple_of(gs[k] * 192 + 96, 96))
+        ]
+        re, im = a - d, b + c
+        res.append(re)
+        ims.append(im)
+        first = jnp.where(low, re, shift_lanes(im, 192))
+        second = jnp.where(low, shift_lanes(re, 192), im)
+        outs[k * 2][0:96] = jnp.where(x == 0, first, second).astype(BF16)
+        outs[k * 2 + 1][0:96] = jnp.where(x == 0, second, first).astype(BF16)
+    for i in range(4):
+        for k in range(i, 4):
+            at, mirror = (gs[i] * 4 + gs[k]) * 2, (gs[k] * 4 + gs[i]) * 2
+            both = jnp.sum(res[i] * res[k] + ims[i] * ims[k], axis=0, keepdims=True)
+            pairs[pl.ds(at, 1), :] = both
+            if k > i:
+                turn = jnp.sum(ims[i] * res[k] - res[i] * ims[k], axis=0, keepdims=True)
+                pairs[pl.ds(mirror, 1), :] = both
+                pairs[pl.ds(at + 1, 1), :] = turn
+                pairs[pl.ds(mirror + 1, 1), :] = -turn
+            else:
+                pairs[pl.ds(at + 1, 1), :] = jnp.zeros_like(both)
+    lane_p = lax.broadcasted_iota(jnp.int32, (8, 384), 1)
+    mom = lax.broadcasted_iota(jnp.int32, (8, 384), 0)
+    total = lax.dot_general(
+        (lane_p // 96 == mom).astype(F32),
+        pairs[...],
+        (((1,), (1,)), ((), ())),
+        precision=lax.Precision.HIGHEST,
+        preferred_element_type=F32,
+    )
+    high = total.astype(BF16)
+    low_part = (total - high.astype(F32)).astype(BF16)
+    tail = jnp.concatenate([high, low_part, jnp.zeros((8, 320), BF16)], axis=1)
+    for k in range(8):
+        outs[k][96:104] = tail
+
+
+BASE = pltpu.VMEM((16, 96, 384), BF16)
+SPREAD = [pltpu.VMEM((2, 2, 32, 384), F32), pltpu.VMEM((2, 4, 96, 384), F32)]
+
+
+def call(kernel, inputs, scalars, out_shape, scratch=(), limit=24):
+    return pl.pallas_call(
+        kernel,
+        out_shape=out_shape,
+        in_specs=[SMEM] * len(scalars) + [VMEM] * len(inputs),
+        out_specs=jax.tree.map(lambda _: VMEM, out_shape),
+        scratch_shapes=scratch,
+        compiler_params=pltpu.CompilerParams(vmem_limit_bytes=limit << 20),
+    )(*scalars, *inputs)
+
+
+def join_kernel(*refs):
+    got, out, blocks = refs[:8], refs[8], refs[9]
+    z, x, _ = here()
+    for k in range(8):
+        blocks[(z ^ (k // 2)) * 2 + (x ^ (k % 2))] = got[k][0:96]
+    for side in range(2):
+        rows = slice(side * 96, (side + 1) * 96)
+        parts = [blocks[k * 2 + side].astype(F32) for k in range(4)]
+        for r in range(2):
+            for p in range(2):
+                at = r * 192 + p * 96
+                out[r, rows, p * 384 : (p + 1) * 384] = jnp.concatenate(
+                    [part[:, at : at + 96] for part in parts], axis=1
+                )
+
+
+def swap(x, axis, mask):
+    return lax.ppermute(x, axis, [(i, i ^ mask) for i in range(lax.axis_size(axis))])
+
+
+def fast_body(eigvecs, solutions, momenta, gammas):
+    vec_count = eigvecs.shape[3]
+    eig = eigvecs.transpose(0, 2, 1, 3).reshape(2, 384, 384)
+    sol = solutions.transpose(0, 2, 1, 3).reshape(2, 384, 192)
+    sol_own, sol_other = prepare_sol(sol)
+    full, *eig_own, cosine, sine = prepare_eig(momenta.T, eig, sol_other)
+    tables = (cosine, sine)
+    sol_pair = jnp.stack([sol_own, swap(sol_other, "x", 1)])
+    mine = jnp.stack([swap(eig_own[k - 1], "z", k) for k in range(1, 4)])
+    sols = [sol_pair] + [swap(sol_pair, "z", k) for k in range(1, 4)]
+
+    table = gamma_table()
+    spin = np.argmax(np.abs(table), axis=2)
+    turn = np.round(np.angle(table.sum(axis=2)) / (np.pi / 2)).astype(int) % 4
+    rows = np.stack([turn * 4 + spin, (turn + 3) % 4 * 4 + spin], axis=1)
+    scalars = (gammas, jnp.asarray(rows.astype(np.int32).reshape(128)))
+
+    total = jax.ShapeDtypeStruct((768, 768), F32)
+    left, right = pltpu.VMEM((768, 1536), BF16), (2, 1536, 768)
+    eig_all = lax.all_gather(mine, ("x", "mode")).reshape(2, 2, 3, 96, 384)
+    acc_own, acc_other, right = call(
+        near_kernel,
+        [*sols[:2], full, swap(full, "x", 1), eig_all, *tables],
+        scalars,
+        [total] * 2 + [jax.ShapeDtypeStruct(right, BF16)],
+        [
+            BASE,
+            left,
+            pltpu.VMEM(right, BF16),
+            *SPREAD,
+        ],
+        36,
+    )
+    given, left = call(
+        given_kernel,
+        [*sols[2:], right, acc_other],
+        scalars,
+        [jax.ShapeDtypeStruct((768, 768), BF16), jax.ShapeDtypeStruct((768, 1536), BF16)],
+        [BASE],
+    )
+    taken = swap(given, "core", 1)
+    own = call(own_kernel, [left, right, acc_own], [], total)
+    sent = call(
+        finish_kernel,
+        [own, taken],
+        [],
+        [jax.ShapeDtypeStruct((104, 384), BF16)] * 8,
+        [pltpu.VMEM((32, 384), F32)],
+    )
+    got = [sent[0]] + [swap(sent[k], ("z", "x"), k) for k in range(1, 8)]
+    part = sum(block[96:100, :64].astype(F32) for block in got)
+    part = part[:, :32] + part[:, 32:]
+    other = swap(part, "core", 1) + swap(part, ("core", "mode"), 3)
+    part = part + swap(part, "mode", 1)
+    first = lax.axis_index("core") == 0
+    pair = jnp.stack([jnp.where(first, part, other), jnp.where(first, other, part)])
+    traces = (pair / float(vec_count * vec_count)).reshape(2, 2, 2, 4, 4, 2)
+    traces = traces.transpose(3, 4, 1, 0, 2, 5).reshape(4, 4, 8, 2)
+    fields = call(
+        join_kernel,
+        got,
+        [],
+        jax.ShapeDtypeStruct((2, 192, 768), F32),
+        [pltpu.VMEM((8, 96, 384), BF16)],
+    ).transpose(2, 0, 1)
+    return fields, traces
+
+
+def shifted(x, axis, by):
+    count = lax.axis_size(axis)
+    return lax.ppermute(x, axis, [(i, (i + by) % count) for i in range(count)])
 
 
 def select_gammas(gammas):
-    table_re, table_im = gamma_table()
+    table = gamma_table()
+    table_re, table_im = table.real.astype(np.float32), table.imag.astype(np.float32)
     select = (gammas[:, None] == jnp.arange(16, dtype=jnp.int32)[None, :]).astype(jnp.float32)
     count = gammas.shape[0]
     real_part = jnp.dot(
@@ -89,7 +439,7 @@
     return jnp.stack([upper, lower], 1).astype(jnp.bfloat16)
 
 
-def body(eigvecs, solutions, momenta, gammas):
+def general_body(eigvecs, solutions, momenta, gammas):
     local_sites = eigvecs.shape[1]
     vec_count = eigvecs.shape[3]
     col_count = solutions.shape[3]
@@ -144,10 +494,27 @@
 
 
 def solution(mesh):
-    return jax.shard_map(
-        body,
-        mesh=mesh,
-        in_specs=(P(None, "space", None, None), P(None, "space", None, "mode"), P(), P()),
-        out_specs=(P("space", None, "mode"), P()),
-        check_vma=False,
-    )
+    fits = dict(mesh.shape) == {"space": 16, "mode": 2}
+    if fits:
+        cut = Mesh(mesh.devices.reshape(4, 2, 2, 2), ("z", "x", "core", "mode"))
+        space = ("z", "x", "core")
+    else:
+        cut, space = mesh, "space"
+
+    def step(eigvecs, solutions, momenta, gammas):
+        sized = eigvecs.shape == (2, 512, 12, 384) and solutions.shape == (2, 512, 12, 384)
+        sized = sized and momenta.shape == (8, 3) and gammas.shape == (4,)
+        return jax.shard_map(
+            fast_body if fits and sized else general_body,
+            mesh=cut if fits and sized else mesh,
+            in_specs=(
+                P(None, space if fits and sized else "space", None, None),
+                P(None, space if fits and sized else "space", None, "mode"),
+                P(),
+                P(),
+            ),
+            out_specs=(P(space if fits and sized else "space", None, "mode"), P()),
+            check_vma=False,
+        )(eigvecs, solutions, momenta, gammas)
+
+    return step

time: 376 us -> 74 us (0.20)
  the two profiles are of different devices: /device:TPU:0 before, /device:TPU:9 now
where the time goes in v3:
time: 74 us; the launch traced here: 73.8 us
  waiting for transfers between devices  21.2 us (29%)
  starting transfers between devices  19 us (26%)
  Pallas kernels  17.1 us (23%)
  blocking collectives  11.5 us (16%)
  local copies, waits for them, and re-layouts  3.99 us (5%)
  between operations  0.78 us (1%)
    ppermute x19, waiting for transfers between devices, swap(): lax.ppermute(x, axis, [(i, i ^ mask) for i in range(lax.axis_size(axis))])  21.2 us
    ppermute x19, starting transfers between devices, swap(): lax.ppermute(x, axis, [(i, i ^ mask) for i in range(lax.axis_size(axis))])  19 us
    pallas_call x5, Pallas kernels, call(): pl.pallas_call(kernel, out_shape=out_shape, in_specs=[SMEM] * len(scalars...  15.8 us
    all_gather x1, blocking collectives, fast_body(): eig_all = lax.all_gather(mine, ('x', 'mode')).reshape(2, 2, 3, 96, 384)  11.5 us
    unnamed x11, local copies, waits for them, and re-layouts  3.48 us
  transfers between devices with their start and end apart: 19, of which 8 were waited for; matrix products, arithmetic and copies ran while one was open for 0% of the time, Pallas kernels for 17%

profile of v3, /device:TPU:9, one launch (start us, length us, event | category | flops | bytes accessed | tf_op | source)
XLA Modules:
  0.0 73.8 jit_solution(2715083372613601180)
XLA Ops:
  0.7 1.0 %copy-done.1 = bf16[2,32,12,192]{3,1,2,0:T(8,128)(2,1)S(1)} copy-done((bf16[2,32,12,192]{3,1,2,0:T(8,128)(2,1)S(1)}, bf16[2,32,12,192]{3,1,2,0:T(8,128)(2,1)}, u32[]{:S(2)}) %copy-start.1) | copy-done | bytes 294936
  1.9 1.3 %collective-permute-start = (bf16[96,768]{1,0:T(8,128)(2,1)S(1)}, bf16[96,768]{1,0:T(8,128)(2,1)S(1)}, u32[]{:S(2)}, u32[]{:S(2)}) collective-permute-start(bf16[96,768]{1,0:T(8,128)(2,1)S(1)} %get-tuple-element.24.after), channel_id=1, source_target_pairs={{0,4},{4,0},{1,5},{5,1},{2,6},{6,2},{3,7},{7,3},{8,12},{12,8},{9,1... | collective-permute-start | bytes 442376 | tf_op jit(solution)/shard_map/ppermute | solution.py:308
  3.1 1.1 %copy-done = bf16[2,32,12,384]{3,1,2,0:T(8,128)(2,1)S(1)} copy-done((bf16[2,32,12,384]{3,1,2,0:T(8,128)(2,1)S(1)}, bf16[2,32,12,384]{3,1,2,0:T(8,128)(2,1)}, u32[]{:S(2)}) %copy-start) | copy-done | bytes 589848
  4.2 0.7 copy-done.2
  4.9 1.1 %shard_map.69 = (bf16[192,384]{1,0:T(8,128)(2,1)S(1)}, bf16[96,384]{1,0:T(8,128)(2,1)S(1)}, bf16[96,384]{1,0:T(8,128)(2,1)S(1)}, bf16[96,384]{1,0:T(8,128)(2,1)S...) custom-call(s32[3,8]{1,0:T(4,128)S(1)} %bitcast.21, bf16[2,384,384]{2,1,0:T(8,128)(2,1)S(1)} %bitcast.18, ...), custom_call_target="tpu_custom_call" | custom-call | tf_op jit(solution)/shard_map/pallas_call | solution.py:119
  6.3 2.3 %collective-permute-start.6 = (bf16[96,384]{1,0:T(8,128)(2,1)S(1)}, bf16[96,384]{1,0:T(8,128)(2,1)S(1)}, u32[]{:S(2)}, u32[]{:S(2)}) collective-permute-start(bf16[96,384]{1,0:T(8,128)(2,1)S(1)} %get-tuple-element.27), channel_id=1, source_target_pairs={{0,16},{8,24},{16,0},{24,8},{1,17},{9,25},{17,1},{25,9},{2,18},{10... | collective-permute-start | bytes 221192 | tf_op jit(solution)/shard_map/ppermute | solution.py:308
  8.8 1.2 %collective-permute-start.3 = (bf16[2,96,768]{2,1,0:T(8,128)(2,1)S(1)}, bf16[2,96,768]{2,1,0:T(8,128)(2,1)S(1)}, u32[]{:S(2)}, u32[]{:S(2)}) collective-permute-start(bf16[2,96,768]{2,1,0:T(8,128)(2,1)S(1)} %pad_maximum_fusion.refs_0_), channel_id=1, source_target_pairs={{0,8},{8,0},{16,24},{24,16},{1,9},{9,1},{17,25},{25,17},{2,10},{10... | collective-permute-start | bytes 884744 | tf_op jit(solution)/shard_map/ppermute | solution.py:308
  10.0 2.2 %collective-permute-start.1 = (bf16[2,96,768]{2,1,0:T(8,128)(2,1)S(1)}, bf16[2,96,768]{2,1,0:T(8,128)(2,1)S(1)}, u32[]{:S(2)}, u32[]{:S(2)}) collective-permute-start(bf16[2,96,768]{2,1,0:T(8,128)(2,1)S(1)} %pad_maximum_fusion.refs_0_), channel_id=1, source_target_pairs={{0,16},{8,24},{16,0},{24,8},{1,17},{9,25},{17,1},{25,9},{2,18},{10... | collective-permute-start | bytes 884744 | tf_op jit(solution)/shard_map/ppermute | solution.py:308
  12.6 1.6 %collective-permute-done.7 = bf16[96,384]{1,0:T(8,128)(2,1)S(1)} collective-permute-done((bf16[96,384]{1,0:T(8,128)(2,1)S(1)}, bf16[96,384]{1,0:T(8,128)(2,1)S(1)}, u32[]{:S(2)}, u32[]{:S(2)}) %collective-permute-start.7) | collective-permute-done | bytes 73760 | tf_op jit(solution)/shard_map/ppermute | solution.py:308
  14.3 11.5 %all-gather = bf16[12,96,384]{2,1,0:T(8,128)(2,1)S(1)} all-gather(bf16[3,96,384]{2,1,0:T(8,128)(2,1)S(1)} %pad_maximum_fusion.1), channel_id=2, replica_groups=mesh['z'=4,'x'=2,'core'=2,'mode'=2] {'x','mode'}, dimensions={0}, use_global_device_ids=true | all-gather | bytes 1105920 | tf_op jit(solution)/shard_map/all_gather | solution.py:330
  25.8 8.4 %shard_map.70 = (f32[768,768]{1,0:T(8,128)S(1)}, f32[768,768]{1,0:T(8,128)S(1)}, bf16[2,1536,768]{2,1,0:T(8,128)(2,1)S(1)}) custom-call(s32[4]{0:T(128)S(1)} %copy-done.3, s32[128]{0:T(128)S(1)} %copy-done.4, bf16[2,96,768]{2,1,0:T(8,128)(2,1)S(1)} %pad_maximum_fusion.refs_0_, bf16[2,96,768]{2,1,0:T(8,128)(2,1)S(1)} %collective-permute-done.3.refs_1_, ...), custom_call_target="tpu_custom_call" | custom-call | tf_op jit(solution)/shard_map/pallas_call | solution.py:281
  34.2 6.4 %collective-permute-done.2.second = bf16[2,96,768]{2,1,0:T(8,128)(2,1)S(1)} collective-permute-done((bf16[2,96,768]{2,1,0:T(8,128)(2,1)S(1)}, bf16[2,96,768]{2,1,0:T(8,128)(2,1)S(1)}, u32[]{:S(2)}, u32[]{:S(2)}) %collective-permute-start.2) | collective-permute-done | bytes 294944 | tf_op jit(solution)/shard_map/ppermute | solution.py:308
  40.6 3.1 %shard_map.71 = (bf16[768,768]{1,0:T(8,128)(2,1)S(1)}, bf16[768,1536]{1,0:T(8,128)(2,1)S(1)}) custom-call(s32[4]{0:T(128)S(1)} %copy-done.3, s32[128]{0:T(128)S(1)} %copy-done.4, bf16[2,96,768]{2,1,0:T(8,128)(2,1)S(1)} %collective-permute-done.1.first, bf16[2,96,768]{2,1,0:T(8,128)(2,1)S(1)} %collective-permute-done.2.second, ...), custom_call_target="tpu_custom_call" | custom-call | tf_op jit(solution)/shard_map/pallas_call | solution.py:281
  43.7 1.4 %collective-permute-start.8 = (bf16[768,768]{1,0:T(8,128)(2,1)S(1)}, bf16[768,768]{1,0:T(8,128)(2,1)S(1)}, u32[]{:S(2)}, u32[]{:S(2)}) collective-permute-start(bf16[768,768]{1,0:T(8,128)(2,1)S(1)} %get-tuple-element.35), channel_id=1, source_target_pairs={{0,2},{2,0},{1,3},{3,1},{4,6},{6,4},{5,7},{7,5},{8,10},{10,8},{9,1... | collective-permute-start | bytes 3538952 | tf_op jit(solution)/shard_map/ppermute | solution.py:308
  45.1 2.0 %shard_map.72.own = f32[768,768]{1,0:T(8,128)S(1)} custom-call(bf16[768,1536]{1,0:T(8,128)(2,1)S(1)} %get-tuple-element.33.left, bf16[2,1536,768]{2,1,0:T(8,128)(2,1)S(1)} %get-tuple-element.31.right, f32[768,768]{1,0:T(8,128)S(1)} %get-tuple-element.34.acc), custom_call_target="tpu_custom_call" | custom-call | tf_op jit(solution)/shard_map/pallas_call | solution.py:281
  47.1 0.5 collective-permute-done.8.got
  47.6 0.9 %shard_map.73 = (bf16[104,384]{1,0:T(8,128)(2,1)S(1)}, bf16[104,384]{1,0:T(8,128)(2,1)S(1)}, bf16[104,384]{1,0:T(8,128)(2,1)S(1)}, bf16[104,384]{1,0:T(8,128)(2,...) custom-call(f32[768,768]{1,0:T(8,128)S(1)} %shard_map.72.own, ...), custom_call_target="tpu_custom_call" | custom-call | tf_op jit(solution)/shard_map/pallas_call | solution.py:281
  48.6 1.4 %collective-permute-start.11 = (bf16[104,384]{1,0:T(8,128)(2,1)S(1)}, bf16[104,384]{1,0:T(8,128)(2,1)S(1)}, u32[]{:S(2)}, u32[]{:S(2)}) collective-permute-start(bf16[104,384]{1,0:T(8,128)(2,1)S(1)} %get-tuple-element.39), channel_id=1, source_target_pairs={{0,12},{4,8},{8,4},{12,0},{16,28},{20,24},{24,20},{28,16},{1,13},{... | collective-permute-start | bytes 239624 | tf_op jit(solution)/shard_map/ppermute | solution.py:308
  50.0 1.1 %collective-permute-start.12 = (bf16[104,384]{1,0:T(8,128)(2,1)S(1)}, bf16[104,384]{1,0:T(8,128)(2,1)S(1)}, u32[]{:S(2)}, u32[]{:S(2)}) collective-permute-start(bf16[104,384]{1,0:T(8,128)(2,1)S(1)} %get-tuple-element.40), channel_id=1, source_target_pairs={{0,16},{4,20},{8,24},{12,28},{16,0},{20,4},{24,8},{28,12},{1,17},{... | collective-permute-start | bytes 239624 | tf_op jit(solution)/shard_map/ppermute | solution.py:308
  51.1 2.2 %collective-permute-start.13 = (bf16[104,384]{1,0:T(8,128)(2,1)S(1)}, bf16[104,384]{1,0:T(8,128)(2,1)S(1)}, u32[]{:S(2)}, u32[]{:S(2)}) collective-permute-start(bf16[104,384]{1,0:T(8,128)(2,1)S(1)} %get-tuple-element.41), channel_id=1, source_target_pairs={{0,20},{4,16},{8,28},{12,24},{16,4},{20,0},{24,12},{28,8},{1,21},{... | collective-permute-start | bytes 239624 | tf_op jit(solution)/shard_map/ppermute | solution.py:308
  53.3 1.3 %collective-permute-start.14 = (bf16[104,384]{1,0:T(8,128)(2,1)S(1)}, bf16[104,384]{1,0:T(8,128)(2,1)S(1)}, u32[]{:S(2)}, u32[]{:S(2)}) collective-permute-start(bf16[104,384]{1,0:T(8,128)(2,1)S(1)} %get-tuple-element.42), channel_id=1, source_target_pairs={{0,24},{4,28},{8,16},{12,20},{16,8},{20,12},{24,0},{28,4},{1,25},{... | collective-permute-start | bytes 239624 | tf_op jit(solution)/shard_map/ppermute | solution.py:308
  54.7 1.2 %collective-permute-start.9 = (bf16[104,384]{1,0:T(8,128)(2,1)S(1)}, bf16[104,384]{1,0:T(8,128)(2,1)S(1)}, u32[]{:S(2)}, u32[]{:S(2)}) collective-permute-start(bf16[104,384]{1,0:T(8,128)(2,1)S(1)} %get-tuple-element.37), channel_id=1, source_target_pairs={{0,4},{4,0},{8,12},{12,8},{16,20},{20,16},{24,28},{28,24},{1,5},{5... | collective-permute-start | bytes 239624 | tf_op jit(solution)/shard_map/ppermute | solution.py:308
  55.9 0.7 collective-permute-done.12.refs_4_
  56.6 5.3 %collective-permute-done.13.refs_5_ = bf16[104,384]{1,0:T(8,128)(2,1)S(1)} collective-permute-done((bf16[104,384]{1,0:T(8,128)(2,1)S(1)}, bf16[104,384]{1,0:T(8,128)(2,1)S(1)}, u32[]{:S(2)}, u32[]{:S(2)}) %collective-permute-start.13) | collective-permute-done | bytes 79904 | tf_op jit(solution)/shard_map/ppermute | solution.py:308
  61.9 3.2 %collective-permute-done.14.refs_6_ = bf16[104,384]{1,0:T(8,128)(2,1)S(1)} collective-permute-done((bf16[104,384]{1,0:T(8,128)(2,1)S(1)}, bf16[104,384]{1,0:T(8,128)(2,1)S(1)}, u32[]{:S(2)}, u32[]{:S(2)}) %collective-permute-start.14) | collective-permute-done | bytes 79904 | tf_op jit(solution)/shard_map/ppermute | solution.py:308
  65.1 1.9 %collective-permute-done.15.refs_7_ = bf16[104,384]{1,0:T(8,128)(2,1)S(1)} collective-permute-done((bf16[104,384]{1,0:T(8,128)(2,1)S(1)}, bf16[104,384]{1,0:T(8,128)(2,1)S(1)}, u32[]{:S(2)}, u32[]{:S(2)}) %collective-permute-start.15) | collective-permute-done | bytes 79904 | tf_op jit(solution)/shard_map/ppermute | solution.py:308
  67.2 1.2 %collective-permute-start.16 = (f32[4,32]{1,0:T(4,128)S(1)}, f32[4,32]{1,0:T(4,128)S(1)}, u32[]{:S(2)}, u32[]{:S(2)}) collective-permute-start(f32[4,32]{1,0:T(4,128)S(1)} %slice_add_fusion), channel_id=1, source_target_pairs={{0,1},{1,0},{2,3},{3,2},{4,5},{5,4},{6,7},{7,6},{8,9},{9,8},{10,11... | collective-permute-start | bytes 1544 | tf_op jit(solution)/shard_map/ppermute | solution.py:308
  68.4 1.0 %collective-permute-start.17 = (f32[4,32]{1,0:T(4,128)S(1)}, f32[4,32]{1,0:T(4,128)S(1)}, u32[]{:S(2)}, u32[]{:S(2)}) collective-permute-start(f32[4,32]{1,0:T(4,128)S(1)} %slice_add_fusion), channel_id=1, source_target_pairs={{0,2},{2,0},{1,3},{3,1},{4,6},{6,4},{5,7},{7,5},{8,10},{10,8},{9,1... | collective-permute-start | bytes 1544 | tf_op jit(solution)/shard_map/ppermute | solution.py:308
  69.5 1.4 %shard_map.74 = f32[2,192,768]{2,1,0:T(8,128)} custom-call(bf16[104,384]{1,0:T(8,128)(2,1)S(1)} %get-tuple-element.36.refs_0_, bf16[104,384]{1,0:T(8,128)(2,1)S(1)} %collective-permute-done.9.refs_1_, bf16[104,384]{1,0:T(8,128)(2,1)S(1)} %collective-permute-done.10.refs_2_, bf16[104,384]{1,0:T(8,128)(2,1)S(1)} %collective-permute-done.11.refs_3_, ...), custom_call_target="tpu_custom_call" | custom-call | tf_op jit(solution)/shard_map/pallas_call | solution.py:281
  70.9 1.5 %collective-permute-done.18 = f32[4,32]{1,0:T(4,128)S(1)} collective-permute-done((f32[4,32]{1,0:T(4,128)S(1)}, f32[4,32]{1,0:T(4,128)S(1)}, u32[]{:S(2)}, u32[]{:S(2)}) %collective-permute-start.18) | collective-permute-done | bytes 544 | tf_op jit(solution)/shard_map/ppermute | solution.py:308
  72.8 0.3 copy.9
  73.1 0.7 copy.10
  (34 shorter events, 1.9 us)
Async XLA Ops:
  0.6 25.2 %copy-start.4 = (s32[128]{0:T(128)S(1)}, s32[128]{0:T(128)}, u32[]{:S(2)}) copy-start(s32[128]{0:T(128)} %constant.11.clone.table) | copy-start | bytes 1540
  0.6 25.2 %copy-start.3 = (s32[4]{0:T(128)S(1)}, s32[4]{0:T(128)}, u32[]{:S(2)}) copy-start(s32[4]{0:T(128)} %gammas.3) | copy-start | bytes 52
  0.7 1.0 %copy-start.1 = (bf16[2,32,12,192]{3,1,2,0:T(8,128)(2,1)S(1)}, bf16[2,32,12,192]{3,1,2,0:T(8,128)(2,1)}, u32[]{:S(2)}) copy-start(bf16[2,32,12,192]{3,1,2,0:T(8,128)(2,1)} %param.6) | copy-start | bytes 884740
  1.9 6.9 %collective-permute-start = (bf16[96,768]{1,0:T(8,128)(2,1)S(1)}, bf16[96,768]{1,0:T(8,128)(2,1)S(1)}, u32[]{:S(2)}, u32[]{:S(2)}) collective-permute-start(bf16[96,768]{1,0:T(8,128)(2,1)S(1)} %get-tuple-element.24.after), channel_id=1, source_target_pairs={{0,4},{4,0},{1,5},{5,1},{2,6},{6,2},{3,7},{7,3},{8,12},{12,8},{9,1... | collective-permute-start | bytes 442376 | tf_op jit(solution)/shard_map/ppermute | solution.py:308
  3.1 1.1 %copy-start = (bf16[2,32,12,384]{3,1,2,0:T(8,128)(2,1)S(1)}, bf16[2,32,12,384]{3,1,2,0:T(8,128)(2,1)}, u32[]{:S(2)}) copy-start(bf16[2,32,12,384]{3,1,2,0:T(8,128)(2,1)} %param.5) | copy-start | bytes 1769476
  4.2 0.7 copy-start.2
  6.0 6.1 %collective-permute-start.5 = (bf16[96,384]{1,0:T(8,128)(2,1)S(1)}, bf16[96,384]{1,0:T(8,128)(2,1)S(1)}, u32[]{:S(2)}, u32[]{:S(2)}) collective-permute-start(bf16[96,384]{1,0:T(8,128)(2,1)S(1)} %get-tuple-element.26), channel_id=1, source_target_pairs={{0,8},{8,0},{16,24},{24,16},{1,9},{9,1},{17,25},{25,17},{2,10},{10... | collective-permute-start | bytes 221192 | tf_op jit(solution)/shard_map/ppermute | solution.py:308
  6.3 6.1 %collective-permute-start.6 = (bf16[96,384]{1,0:T(8,128)(2,1)S(1)}, bf16[96,384]{1,0:T(8,128)(2,1)S(1)}, u32[]{:S(2)}, u32[]{:S(2)}) collective-permute-start(bf16[96,384]{1,0:T(8,128)(2,1)S(1)} %get-tuple-element.27), channel_id=1, source_target_pairs={{0,16},{8,24},{16,0},{24,8},{1,17},{9,25},{17,1},{25,9},{2,18},{10... | collective-permute-start | bytes 221192 | tf_op jit(solution)/shard_map/ppermute | solution.py:308
  8.6 5.7 %collective-permute-start.7 = (bf16[96,384]{1,0:T(8,128)(2,1)S(1)}, bf16[96,384]{1,0:T(8,128)(2,1)S(1)}, u32[]{:S(2)}, u32[]{:S(2)}) collective-permute-start(bf16[96,384]{1,0:T(8,128)(2,1)S(1)} %get-tuple-element.28), channel_id=1, source_target_pairs={{0,24},{8,16},{16,8},{24,0},{1,25},{9,17},{17,9},{25,1},{2,26},{10... | collective-permute-start | bytes 221192 | tf_op jit(solution)/shard_map/ppermute | solution.py:308
  8.8 17.0 %collective-permute-start.3 = (bf16[2,96,768]{2,1,0:T(8,128)(2,1)S(1)}, bf16[2,96,768]{2,1,0:T(8,128)(2,1)S(1)}, u32[]{:S(2)}, u32[]{:S(2)}) collective-permute-start(bf16[2,96,768]{2,1,0:T(8,128)(2,1)S(1)} %pad_maximum_fusion.refs_0_), channel_id=1, source_target_pairs={{0,8},{8,0},{16,24},{24,16},{1,9},{9,1},{17,25},{25,17},{2,10},{10... | collective-permute-start | bytes 884744 | tf_op jit(solution)/shard_map/ppermute | solution.py:308
  10.0 24.3 %collective-permute-start.1 = (bf16[2,96,768]{2,1,0:T(8,128)(2,1)S(1)}, bf16[2,96,768]{2,1,0:T(8,128)(2,1)S(1)}, u32[]{:S(2)}, u32[]{:S(2)}) collective-permute-start(bf16[2,96,768]{2,1,0:T(8,128)(2,1)S(1)} %pad_maximum_fusion.refs_0_), channel_id=1, source_target_pairs={{0,16},{8,24},{16,0},{24,8},{1,17},{9,25},{17,1},{25,9},{2,18},{10... | collective-permute-start | bytes 884744 | tf_op jit(solution)/shard_map/ppermute | solution.py:308
  12.1 28.5 %collective-permute-start.2 = (bf16[2,96,768]{2,1,0:T(8,128)(2,1)S(1)}, bf16[2,96,768]{2,1,0:T(8,128)(2,1)S(1)}, u32[]{:S(2)}, u32[]{:S(2)}) collective-permute-start(bf16[2,96,768]{2,1,0:T(8,128)(2,1)S(1)} %pad_maximum_fusion.refs_0_), channel_id=1, source_target_pairs={{0,24},{8,16},{16,8},{24,0},{1,25},{9,17},{17,9},{25,1},{2,26},{10... | collective-permute-start | bytes 884744 | tf_op jit(solution)/shard_map/ppermute | solution.py:308
  12.4 13.4 %collective-permute-start.4 = (bf16[192,384]{1,0:T(8,128)(2,1)S(1)}, bf16[192,384]{1,0:T(8,128)(2,1)S(1)}, u32[]{:S(2)}, u32[]{:S(2)}) collective-permute-start(bf16[192,384]{1,0:T(8,128)(2,1)S(1)} %get-tuple-element.25.refs_2_), channel_id=1, source_target_pairs={{0,4},{4,0},{1,5},{5,1},{2,6},{6,2},{3,7},{7,3},{8,12},{12,8},{9,1... | collective-permute-start | bytes 442376 | tf_op jit(solution)/shard_map/ppermute | solution.py:308
  43.7 3.9 %collective-permute-start.8 = (bf16[768,768]{1,0:T(8,128)(2,1)S(1)}, bf16[768,768]{1,0:T(8,128)(2,1)S(1)}, u32[]{:S(2)}, u32[]{:S(2)}) collective-permute-start(bf16[768,768]{1,0:T(8,128)(2,1)S(1)} %get-tuple-element.35), channel_id=1, source_target_pairs={{0,2},{2,0},{1,3},{3,1},{4,6},{6,4},{5,7},{7,5},{8,10},{10,8},{9,1... | collective-permute-start | bytes 3538952 | tf_op jit(solution)/shard_map/ppermute | solution.py:308
  48.5 6.1 %collective-permute-start.10 = (bf16[104,384]{1,0:T(8,128)(2,1)S(1)}, bf16[104,384]{1,0:T(8,128)(2,1)S(1)}, u32[]{:S(2)}, u32[]{:S(2)}) collective-permute-start(bf16[104,384]{1,0:T(8,128)(2,1)S(1)} %get-tuple-element.38), channel_id=1, source_target_pairs={{0,8},{4,12},{8,0},{12,4},{16,24},{20,28},{24,16},{28,20},{1,9},{5... | collective-permute-start | bytes 239624 | tf_op jit(solution)/shard_map/ppermute | solution.py:308
  48.6 6.2 %collective-permute-start.11 = (bf16[104,384]{1,0:T(8,128)(2,1)S(1)}, bf16[104,384]{1,0:T(8,128)(2,1)S(1)}, u32[]{:S(2)}, u32[]{:S(2)}) collective-permute-start(bf16[104,384]{1,0:T(8,128)(2,1)S(1)} %get-tuple-element.39), channel_id=1, source_target_pairs={{0,12},{4,8},{8,4},{12,0},{16,28},{20,24},{24,20},{28,16},{1,13},{... | collective-permute-start | bytes 239624 | tf_op jit(solution)/shard_map/ppermute | solution.py:308
  50.0 6.6 %collective-permute-start.12 = (bf16[104,384]{1,0:T(8,128)(2,1)S(1)}, bf16[104,384]{1,0:T(8,128)(2,1)S(1)}, u32[]{:S(2)}, u32[]{:S(2)}) collective-permute-start(bf16[104,384]{1,0:T(8,128)(2,1)S(1)} %get-tuple-element.40), channel_id=1, source_target_pairs={{0,16},{4,20},{8,24},{12,28},{16,0},{20,4},{24,8},{28,12},{1,17},{... | collective-permute-start | bytes 239624 | tf_op jit(solution)/shard_map/ppermute | solution.py:308
  51.1 10.8 %collective-permute-start.13 = (bf16[104,384]{1,0:T(8,128)(2,1)S(1)}, bf16[104,384]{1,0:T(8,128)(2,1)S(1)}, u32[]{:S(2)}, u32[]{:S(2)}) collective-permute-start(bf16[104,384]{1,0:T(8,128)(2,1)S(1)} %get-tuple-element.41), channel_id=1, source_target_pairs={{0,20},{4,16},{8,28},{12,24},{16,4},{20,0},{24,12},{28,8},{1,21},{... | collective-permute-start | bytes 239624 | tf_op jit(solution)/shard_map/ppermute | solution.py:308
  53.3 11.8 %collective-permute-start.14 = (bf16[104,384]{1,0:T(8,128)(2,1)S(1)}, bf16[104,384]{1,0:T(8,128)(2,1)S(1)}, u32[]{:S(2)}, u32[]{:S(2)}) collective-permute-start(bf16[104,384]{1,0:T(8,128)(2,1)S(1)} %get-tuple-element.42), channel_id=1, source_target_pairs={{0,24},{4,28},{8,16},{12,20},{16,8},{20,12},{24,0},{28,4},{1,25},{... | collective-permute-start | bytes 239624 | tf_op jit(solution)/shard_map/ppermute | solution.py:308
  54.6 12.5 %collective-permute-start.15 = (bf16[104,384]{1,0:T(8,128)(2,1)S(1)}, bf16[104,384]{1,0:T(8,128)(2,1)S(1)}, u32[]{:S(2)}, u32[]{:S(2)}) collective-permute-start(bf16[104,384]{1,0:T(8,128)(2,1)S(1)} %get-tuple-element.43), channel_id=1, source_target_pairs={{0,28},{4,24},{8,20},{12,16},{16,12},{20,8},{24,4},{28,0},{1,29},{... | collective-permute-start | bytes 239624 | tf_op jit(solution)/shard_map/ppermute | solution.py:308
  54.7 12.3 %collective-permute-start.9 = (bf16[104,384]{1,0:T(8,128)(2,1)S(1)}, bf16[104,384]{1,0:T(8,128)(2,1)S(1)}, u32[]{:S(2)}, u32[]{:S(2)}) collective-permute-start(bf16[104,384]{1,0:T(8,128)(2,1)S(1)} %get-tuple-element.37), channel_id=1, source_target_pairs={{0,4},{4,0},{8,12},{12,8},{16,20},{20,16},{24,28},{28,24},{1,5},{5... | collective-permute-start | bytes 239624 | tf_op jit(solution)/shard_map/ppermute | solution.py:308
  67.2 3.8 %collective-permute-start.16 = (f32[4,32]{1,0:T(4,128)S(1)}, f32[4,32]{1,0:T(4,128)S(1)}, u32[]{:S(2)}, u32[]{:S(2)}) collective-permute-start(f32[4,32]{1,0:T(4,128)S(1)} %slice_add_fusion), channel_id=1, source_target_pairs={{0,1},{1,0},{2,3},{3,2},{4,5},{5,4},{6,7},{7,6},{8,9},{9,8},{10,11... | collective-permute-start | bytes 1544 | tf_op jit(solution)/shard_map/ppermute | solution.py:308
  68.4 2.5 %collective-permute-start.17 = (f32[4,32]{1,0:T(4,128)S(1)}, f32[4,32]{1,0:T(4,128)S(1)}, u32[]{:S(2)}, u32[]{:S(2)}) collective-permute-start(f32[4,32]{1,0:T(4,128)S(1)} %slice_add_fusion), channel_id=1, source_target_pairs={{0,2},{2,0},{1,3},{3,1},{4,6},{6,4},{5,7},{7,5},{8,10},{10,8},{9,1... | collective-permute-start | bytes 1544 | tf_op jit(solution)/shard_map/ppermute | solution.py:308
  69.4 3.0 %collective-permute-start.18 = (f32[4,32]{1,0:T(4,128)S(1)}, f32[4,32]{1,0:T(4,128)S(1)}, u32[]{:S(2)}, u32[]{:S(2)}) collective-permute-start(f32[4,32]{1,0:T(4,128)S(1)} %slice_add_fusion), channel_id=1, source_target_pairs={{0,3},{1,2},{2,1},{3,0},{4,7},{5,6},{6,5},{7,4},{8,11},{9,10},{10,... | collective-permute-start | bytes 1544 | tf_op jit(solution)/shard_map/ppermute | solution.py:308

commit v4 on v3

--- a/solution.py
+++ b/solution.py
@@ -16,6 +16,10 @@
 HBM = pl.BlockSpec(memory_space=pltpu.HBM)
 BF16 = jnp.bfloat16
 F32 = jnp.float32
+
+
+ORDER = (6, 4, 7, 5, 3, 2, 1)
+COST = pl.CostEstimate(flops=2_000_000_000, bytes_accessed=8_000_000, transcendentals=0)
 
 
 def gamma_table():
@@ -74,12 +78,13 @@
         out_specs=[VMEM] * 2,
         scratch_shapes=[pltpu.VMEM((2, 96, 768), BF16)],
         compiler_params=pltpu.CompilerParams(vmem_limit_bytes=16 << 20),
+        cost_estimate=COST,
     )(sol)
 
 
-def prepare_eig_kernel(momenta, eig, after, full, *rest):
-    eig_out, (cosine, sine, packs) = rest[:3], rest[3:]
-    (z, x, core), half = here(), lax.axis_index("mode")
+def prepare_eig_kernel(eig, after, full, *rest):
+    eig_out, packs = rest[:3], rest[3]
+    z, half = lax.axis_index("z"), lax.axis_index("mode")
     lane = lax.broadcasted_iota(jnp.int32, (96, 384), 1)
     for side in range(2):
         at = side * 192
@@ -95,6 +100,10 @@
     full[96:192] = packs[z, 1]
     for k in range(1, 4):
         eig_out[k - 1][...] = packs[z ^ k, half]
+
+
+def site_phases(momenta, cosine, sine):
+    z, x, core = here()
     shape = cosine.shape[::-1]
     mom = lax.broadcasted_iota(jnp.int32, shape, 0)
     lane = lax.broadcasted_iota(jnp.int32, shape, 1)
@@ -115,23 +124,22 @@
     sine[...] = jnp.sin(theta).T
 
 
-def prepare_eig(momenta, eig, after):
+def prepare_eig(eig, after):
     return pl.pallas_call(
         prepare_eig_kernel,
         out_shape=[jax.ShapeDtypeStruct((192, 384), BF16)]
-        + [jax.ShapeDtypeStruct((96, 384), BF16)] * 3
-        + [jax.ShapeDtypeStruct((256, 8), F32)] * 2,
-        in_specs=[SMEM, VMEM, HBM],
-        out_specs=[VMEM] * 6,
+        + [jax.ShapeDtypeStruct((96, 384), BF16)] * 3,
+        in_specs=[VMEM, HBM],
+        out_specs=[VMEM] * 4,
         scratch_shapes=[pltpu.VMEM((4, 2, 96, 384), BF16)],
         compiler_params=pltpu.CompilerParams(vmem_limit_bytes=16 << 20),
-    )(momenta, eig, after)
+    )(eig, after)
 
 
 def build_base(first, second, base):
     lane = lax.broadcasted_iota(jnp.int32, (96, 384), 1)
     parts = [
-        [plane[m, :, r * 384 : (r + 1) * 384].astype(F32) for plane in (first, second) for m in range(2)]
+        [plane[m, :, r * 384 : (r + 1) * 384] for plane in (first, second) for m in range(2)]
         for r in range(2)
     ]
     for t in range(4):
@@ -140,7 +148,7 @@
             for part in parts
         ]
         for turn, x in enumerate((re, -im, -re, im)):
-            base[turn * 4 + t] = x.astype(BF16)
+            base[turn * 4 + t] = x
 
 
 def build_left(base, gammas, table, left):
@@ -192,9 +200,10 @@
     return at, jnp.dot(left[...], right[side, :, at], preferred_element_type=F32)
 
 
-def near_kernel(gammas, table, *refs):
-    sols, fulls, eigs, (cosine, sine) = refs[:2], refs[2:4], refs[4], refs[5:7]
-    accs, far_right, (base, left, right, phases, spread) = refs[7:9], refs[9], refs[10:]
+def near_kernel(gammas, table, momenta, *refs):
+    sols, fulls, eigs, accs, far_right = refs[:2], refs[2:4], refs[4], refs[5:7], refs[7]
+    base, left, right, phases, spread, cosine, sine = refs[8:]
+    site_phases(momenta, cosine, sine)
     work = (phases, spread)
     for m in range(2):
         blocks = [(0, fulls[m][0:96]), (2, fulls[m][96:192])]
@@ -211,7 +220,7 @@
             acc[:, at] = part
 
 
-def given_kernel(gammas, table, first, second, right, acc, out, left, base):
+def given_kernel(gammas, table, second, first, right, acc, out, left, base):
     build_base(first, second, base)
     build_left(base, gammas, table, left)
     for n in range(3):
@@ -243,8 +252,11 @@
         ims.append(im)
         first = jnp.where(low, re, shift_lanes(im, 192))
         second = jnp.where(low, shift_lanes(re, 192), im)
-        outs[k * 2][0:96] = jnp.where(x == 0, first, second).astype(BF16)
-        outs[k * 2 + 1][0:96] = jnp.where(x == 0, second, first).astype(BF16)
+        for tile in range(3):
+            lanes, rows = slice(tile * 128, (tile + 1) * 128), slice(tile * 96, (tile + 1) * 96)
+            one, two = first[:, lanes], second[:, lanes]
+            outs[k * 2][rows] = jnp.where(x == 0, one, two).astype(BF16)
+            outs[k * 2 + 1][rows] = jnp.where(x == 0, two, one).astype(BF16)
     for i in range(4):
         for k in range(i, 4):
             at, mirror = (gs[i] * 4 + gs[k]) * 2, (gs[k] * 4 + gs[i]) * 2
@@ -268,9 +280,9 @@
     )
     high = total.astype(BF16)
     low_part = (total - high.astype(F32)).astype(BF16)
-    tail = jnp.concatenate([high, low_part, jnp.zeros((8, 320), BF16)], axis=1)
+    tail = jnp.concatenate([high, low_part, jnp.zeros((8, 64), BF16)], axis=1)
     for k in range(8):
-        outs[k][96:104] = tail
+        outs[k][288:296] = tail
 
 
 BASE = pltpu.VMEM((16, 96, 384), BF16)
@@ -291,8 +303,10 @@
 def join_kernel(*refs):
     got, out, blocks = refs[:8], refs[8], refs[9]
     z, x, _ = here()
-    for k in range(8):
-        blocks[(z ^ (k // 2)) * 2 + (x ^ (k % 2))] = got[k][0:96]
+    for k, block in zip((0,) + ORDER, got):
+        for tile in range(3):
+            lanes = slice(tile * 128, (tile + 1) * 128)
+            blocks[(z ^ (k // 2)) * 2 + (x ^ (k % 2)), :, lanes] = block[tile * 96 : tile * 96 + 96]
     for side in range(2):
         rows = slice(side * 96, (side + 1) * 96)
         parts = [blocks[k * 2 + side].astype(F32) for k in range(4)]
@@ -304,6 +318,19 @@
                 )
 
 
+def traces_kernel(vec_count, own, core, own_mode, core_mode, out):
+    mine, other = own[...] + own_mode[...], core[...] + core_mode[...]
+    first = lax.axis_index("core") == 0
+    low, high = jnp.where(first, mine, other), jnp.where(first, other, mine)
+    rows = jnp.concatenate([low[0:2], high[0:2], low[2:4], high[2:4]], axis=0)
+    rows = rows * (1.0 / float(vec_count * vec_count))
+    turned = jnp.concatenate([rows, jnp.zeros((8, 96), F32)], axis=1).T
+    for g in range(4):
+        for k in range(4):
+            at = (g * 4 + k) * 2
+            out[g, k] = turned[at : at + 2]
+
+
 def swap(x, axis, mask):
     return lax.ppermute(x, axis, [(i, i ^ mask) for i in range(lax.axis_size(axis))])
 
@@ -313,8 +340,7 @@
     eig = eigvecs.transpose(0, 2, 1, 3).reshape(2, 384, 384)
     sol = solutions.transpose(0, 2, 1, 3).reshape(2, 384, 192)
     sol_own, sol_other = prepare_sol(sol)
-    full, *eig_own, cosine, sine = prepare_eig(momenta.T, eig, sol_other)
-    tables = (cosine, sine)
+    full, *eig_own = prepare_eig(eig, sol_other)
     sol_pair = jnp.stack([sol_own, swap(sol_other, "x", 1)])
     mine = jnp.stack([swap(eig_own[k - 1], "z", k) for k in range(1, 4)])
     sols = [sol_pair] + [swap(sol_pair, "z", k) for k in range(1, 4)]
@@ -330,20 +356,22 @@
     eig_all = lax.all_gather(mine, ("x", "mode")).reshape(2, 2, 3, 96, 384)
     acc_own, acc_other, right = call(
         near_kernel,
-        [*sols[:2], full, swap(full, "x", 1), eig_all, *tables],
-        scalars,
+        [*sols[:2], full, swap(full, "x", 1), eig_all],
+        [*scalars, momenta.T],
         [total] * 2 + [jax.ShapeDtypeStruct(right, BF16)],
         [
             BASE,
             left,
             pltpu.VMEM(right, BF16),
             *SPREAD,
+            pltpu.VMEM((256, 8), F32),
+            pltpu.VMEM((256, 8), F32),
         ],
         36,
     )
     given, left = call(
         given_kernel,
-        [*sols[2:], right, acc_other],
+        [sols[3], sols[2], right, acc_other],
         scalars,
         [jax.ShapeDtypeStruct((768, 768), BF16), jax.ShapeDtypeStruct((768, 1536), BF16)],
         [BASE],
@@ -354,18 +382,19 @@
         finish_kernel,
         [own, taken],
         [],
-        [jax.ShapeDtypeStruct((104, 384), BF16)] * 8,
+        [jax.ShapeDtypeStruct((296, 128), BF16)] * 8,
         [pltpu.VMEM((32, 384), F32)],
     )
-    got = [sent[0]] + [swap(sent[k], ("z", "x"), k) for k in range(1, 8)]
-    part = sum(block[96:100, :64].astype(F32) for block in got)
+    got = [sent[0]] + [swap(sent[k], ("z", "x"), k) for k in ORDER]
+    part = sum(block[288:292, :64].astype(F32) for block in got)
     part = part[:, :32] + part[:, 32:]
-    other = swap(part, "core", 1) + swap(part, ("core", "mode"), 3)
-    part = part + swap(part, "mode", 1)
-    first = lax.axis_index("core") == 0
-    pair = jnp.stack([jnp.where(first, part, other), jnp.where(first, other, part)])
-    traces = (pair / float(vec_count * vec_count)).reshape(2, 2, 2, 4, 4, 2)
-    traces = traces.transpose(3, 4, 1, 0, 2, 5).reshape(4, 4, 8, 2)
+    others = [swap(part, "core", 1), swap(part, "mode", 1), swap(part, ("core", "mode"), 3)]
+    traces = call(
+        functools.partial(traces_kernel, vec_count),
+        [part, *others],
+        [],
+        jax.ShapeDtypeStruct((4, 4, 2, 8), F32),
+    ).transpose(0, 1, 3, 2)
     fields = call(
         join_kernel,
         got,

time: 74 us -> 69 us (0.932)
  the two profiles are of different devices: /device:TPU:9 before, /device:TPU:0 now
where the time goes in v4:
time: 69 us; the launch traced here: 68.8 us
  starting transfers between devices  28.7 us (42%)
  Pallas kernels  16.7 us (24%)
  blocking collectives  12.7 us (18%)
  waiting for transfers between devices  8.76 us (13%)
  local copies, waits for them, and re-layouts  1.01 us (1%)
  between operations  0.79 us (1%)
    ppermute x19, starting transfers between devices, swap(): lax.ppermute(x, axis, [(i, i ^ mask) for i in range(lax.axis_size(axis))])  28.7 us
    pallas_call x6, Pallas kernels, call(): pl.pallas_call(kernel, out_shape=out_shape, in_specs=[SMEM] * len(scalars...  16 us
    all_gather x1, blocking collectives, fast_body(): eig_all = lax.all_gather(mine, ('x', 'mode')).reshape(2, 2, 3, 96, 384)  12.7 us
    ppermute x19, waiting for transfers between devices, swap(): lax.ppermute(x, axis, [(i, i ^ mask) for i in range(lax.axis_size(axis))])  8.76 us
  transfers between devices with their start and end apart: 19, of which 7 were waited for; matrix products, arithmetic and copies ran while one was open for 0% of the time, Pallas kernels for 17%

profile of v4, /device:TPU:0, one launch (start us, length us, event | category | flops | bytes accessed | tf_op | source)
XLA Modules:
  0.0 68.8 jit_solution(6696691898396979662)
XLA Ops:
  0.6 1.0 %copy-done.4 = bf16[2,32,12,192]{3,1,2,0:T(8,128)(2,1)S(1)} copy-done((bf16[2,32,12,192]{3,1,2,0:T(8,128)(2,1)S(1)}, bf16[2,32,12,192]{3,1,2,0:T(8,128)(2,1)}, u32[]{:S(2)}) %copy-start.4) | copy-done | bytes 294936
  1.9 3.0 %collective-permute-start = (bf16[96,768]{1,0:T(8,128)(2,1)S(1)}, bf16[96,768]{1,0:T(8,128)(2,1)S(1)}, u32[]{:S(2)}, u32[]{:S(2)}) collective-permute-start(bf16[96,768]{1,0:T(8,128)(2,1)S(1)} %get-tuple-element.22.after), channel_id=1, source_target_pairs={{0,4},{4,0},{1,5},{5,1},{2,6},{6,2},{3,7},{7,3},{8,12},{12,8},{9,1... | collective-permute-start | bytes 442376 | tf_op jit(solution)/shard_map/ppermute | solution.py:335
  4.9 0.5 shard_map.69
  5.4 1.6 %collective-permute-start.5 = (bf16[96,384]{1,0:T(8,128)(2,1)S(1)}, bf16[96,384]{1,0:T(8,128)(2,1)S(1)}, u32[]{:S(2)}, u32[]{:S(2)}) collective-permute-start(bf16[96,384]{1,0:T(8,128)(2,1)S(1)} %get-tuple-element.24), channel_id=1, source_target_pairs={{0,8},{8,0},{16,24},{24,16},{1,9},{9,1},{17,25},{25,17},{2,10},{10... | collective-permute-start | bytes 221192 | tf_op jit(solution)/shard_map/ppermute | solution.py:335
  7.0 2.6 %collective-permute-start.6 = (bf16[96,384]{1,0:T(8,128)(2,1)S(1)}, bf16[96,384]{1,0:T(8,128)(2,1)S(1)}, u32[]{:S(2)}, u32[]{:S(2)}) collective-permute-start(bf16[96,384]{1,0:T(8,128)(2,1)S(1)} %get-tuple-element.25), channel_id=1, source_target_pairs={{0,16},{8,24},{16,0},{24,8},{1,17},{9,25},{17,1},{25,9},{2,18},{10... | collective-permute-start | bytes 221192 | tf_op jit(solution)/shard_map/ppermute | solution.py:335
  9.6 0.2 collective-permute-start.7
  9.9 0.8 %collective-permute-start.3 = (bf16[2,96,768]{2,1,0:T(8,128)(2,1)S(1)}, bf16[2,96,768]{2,1,0:T(8,128)(2,1)S(1)}, u32[]{:S(2)}, u32[]{:S(2)}) collective-permute-start(bf16[2,96,768]{2,1,0:T(8,128)(2,1)S(1)} %pad_maximum_fusion.refs_0_), channel_id=1, source_target_pairs={{0,8},{8,0},{16,24},{24,16},{1,9},{9,1},{17,25},{25,17},{2,10},{10... | collective-permute-start | bytes 884744 | tf_op jit(solution)/shard_map/ppermute | solution.py:335
  10.6 3.5 %collective-permute-start.2 = (bf16[2,96,768]{2,1,0:T(8,128)(2,1)S(1)}, bf16[2,96,768]{2,1,0:T(8,128)(2,1)S(1)}, u32[]{:S(2)}, u32[]{:S(2)}) collective-permute-start(bf16[2,96,768]{2,1,0:T(8,128)(2,1)S(1)} %pad_maximum_fusion.refs_0_), channel_id=1, source_target_pairs={{0,16},{8,24},{16,0},{24,8},{1,17},{9,25},{17,1},{25,9},{2,18},{10... | collective-permute-start | bytes 884744 | tf_op jit(solution)/shard_map/ppermute | solution.py:335
  14.1 0.2 collective-permute-start.1
  14.3 0.4 collective-permute-done.6
  14.8 1.0 %collective-permute-start.4 = (bf16[192,384]{1,0:T(8,128)(2,1)S(1)}, bf16[192,384]{1,0:T(8,128)(2,1)S(1)}, u32[]{:S(2)}, u32[]{:S(2)}) collective-permute-start(bf16[192,384]{1,0:T(8,128)(2,1)S(1)} %get-tuple-element.23.refs_2_), channel_id=1, source_target_pairs={{0,4},{4,0},{1,5},{5,1},{2,6},{6,2},{3,7},{7,3},{8,12},{12,8},{9,1... | collective-permute-start | bytes 442376 | tf_op jit(solution)/shard_map/ppermute | solution.py:335
  15.7 0.9 %collective-permute-done.7 = bf16[96,384]{1,0:T(8,128)(2,1)S(1)} collective-permute-done((bf16[96,384]{1,0:T(8,128)(2,1)S(1)}, bf16[96,384]{1,0:T(8,128)(2,1)S(1)}, u32[]{:S(2)}, u32[]{:S(2)}) %collective-permute-start.7) | collective-permute-done | bytes 73760 | tf_op jit(solution)/shard_map/ppermute | solution.py:335
  16.7 12.7 %all-gather = bf16[12,96,384]{2,1,0:T(8,128)(2,1)S(1)} all-gather(bf16[3,96,384]{2,1,0:T(8,128)(2,1)S(1)} %pad_maximum_fusion.1), channel_id=2, replica_groups=mesh['z'=4,'x'=2,'core'=2,'mode'=2] {'x','mode'}, dimensions={0}, use_global_device_ids=true | all-gather | bytes 1105920 | tf_op jit(solution)/shard_map/all_gather | solution.py:356
  29.4 7.9 %shard_map.70 = (f32[768,768]{1,0:T(8,128)S(1)}, f32[768,768]{1,0:T(8,128)S(1)}, bf16[2,1536,768]{2,1,0:T(8,128)(2,1)S(1)}) custom-call(s32[4]{0:T(128)S(1)} %copy-done.2, s32[128]{0:T(128)S(1)} %copy-done.3, s32[3,8]{1,0:T(4,128)S(1)} %bitcast.18, bf16[2,96,768]{2,1,0:T(8,128)(2,1)S(1)} %pad_maximum_fusion.refs_0_, ...), custom_call_target="tpu_custom_call" | custom-call | tf_op jit(solution)/shard_map/pallas_call | solution.py:293
  37.4 3.1 %shard_map.71 = (bf16[768,768]{1,0:T(8,128)(2,1)S(1)}, bf16[768,1536]{1,0:T(8,128)(2,1)S(1)}) custom-call(s32[4]{0:T(128)S(1)} %copy-done.2, s32[128]{0:T(128)S(1)} %copy-done.3, bf16[2,96,768]{2,1,0:T(8,128)(2,1)S(1)} %collective-permute-done.1.second, bf16[2,96,768]{2,1,0:T(8,128)(2,1)S(1)} %collective-permute-done.2.first, ...), custom_call_target="tpu_custom_call" | custom-call | tf_op jit(solution)/shard_map/pallas_call | solution.py:293
  40.5 2.0 %shard_map.72.own = f32[768,768]{1,0:T(8,128)S(1)} custom-call(bf16[768,1536]{1,0:T(8,128)(2,1)S(1)} %get-tuple-element.29.left, bf16[2,1536,768]{2,1,0:T(8,128)(2,1)S(1)} %get-tuple-element.27.right, f32[768,768]{1,0:T(8,128)S(1)} %get-tuple-element.30.acc), custom_call_target="tpu_custom_call" | custom-call | tf_op jit(solution)/shard_map/pallas_call | solution.py:293
  42.5 0.8 %collective-permute-done.8.got = bf16[768,768]{1,0:T(8,128)(2,1)S(1)} collective-permute-done((bf16[768,768]{1,0:T(8,128)(2,1)S(1)}, bf16[768,768]{1,0:T(8,128)(2,1)S(1)}, u32[]{:S(2)}, u32[]{:S(2)}) %collective-permute-start.8) | collective-permute-done | bytes 1179680 | tf_op jit(solution)/shard_map/ppermute | solution.py:335
  43.3 0.9 %shard_map.73 = (bf16[296,128]{1,0:T(8,128)(2,1)S(1)}, bf16[296,128]{1,0:T(8,128)(2,1)S(1)}, bf16[296,128]{1,0:T(8,128)(2,1)S(1)}, bf16[296,128]{1,0:T(8,128)(2,...) custom-call(f32[768,768]{1,0:T(8,128)S(1)} %shard_map.72.own, ...), custom_call_target="tpu_custom_call" | custom-call | tf_op jit(solution)/shard_map/pallas_call | solution.py:293
  44.2 2.7 %collective-permute-start.9 = (bf16[296,128]{1,0:T(8,128)(2,1)S(1)}, bf16[296,128]{1,0:T(8,128)(2,1)S(1)}, u32[]{:S(2)}, u32[]{:S(2)}) collective-permute-start(bf16[296,128]{1,0:T(8,128)(2,1)S(1)} %get-tuple-element.33), channel_id=1, source_target_pairs={{0,24},{4,28},{8,16},{12,20},{16,8},{20,12},{24,0},{28,4},{1,25},{... | collective-permute-start | bytes 227336 | tf_op jit(solution)/shard_map/ppermute | solution.py:335
  46.9 3.4 %collective-permute-start.10 = (bf16[296,128]{1,0:T(8,128)(2,1)S(1)}, bf16[296,128]{1,0:T(8,128)(2,1)S(1)}, u32[]{:S(2)}, u32[]{:S(2)}) collective-permute-start(bf16[296,128]{1,0:T(8,128)(2,1)S(1)} %get-tuple-element.34), channel_id=1, source_target_pairs={{0,16},{4,20},{8,24},{12,28},{16,0},{20,4},{24,8},{28,12},{1,17},{... | collective-permute-start | bytes 227336 | tf_op jit(solution)/shard_map/ppermute | solution.py:335
  50.3 2.9 %collective-permute-start.11 = (bf16[296,128]{1,0:T(8,128)(2,1)S(1)}, bf16[296,128]{1,0:T(8,128)(2,1)S(1)}, u32[]{:S(2)}, u32[]{:S(2)}) collective-permute-start(bf16[296,128]{1,0:T(8,128)(2,1)S(1)} %get-tuple-element.35), channel_id=1, source_target_pairs={{0,28},{4,24},{8,20},{12,16},{16,12},{20,8},{24,4},{28,0},{1,29},{... | collective-permute-start | bytes 227336 | tf_op jit(solution)/shard_map/ppermute | solution.py:335
  53.3 2.8 %collective-permute-start.13 = (bf16[296,128]{1,0:T(8,128)(2,1)S(1)}, bf16[296,128]{1,0:T(8,128)(2,1)S(1)}, u32[]{:S(2)}, u32[]{:S(2)}) collective-permute-start(bf16[296,128]{1,0:T(8,128)(2,1)S(1)} %get-tuple-element.37), channel_id=1, source_target_pairs={{0,12},{4,8},{8,4},{12,0},{16,28},{20,24},{24,20},{28,16},{1,13},{... | collective-permute-start | bytes 227336 | tf_op jit(solution)/shard_map/ppermute | solution.py:335
  56.1 1.0 %collective-permute-start.14 = (bf16[296,128]{1,0:T(8,128)(2,1)S(1)}, bf16[296,128]{1,0:T(8,128)(2,1)S(1)}, u32[]{:S(2)}, u32[]{:S(2)}) collective-permute-start(bf16[296,128]{1,0:T(8,128)(2,1)S(1)} %get-tuple-element.38), channel_id=1, source_target_pairs={{0,8},{4,12},{8,0},{12,4},{16,24},{20,28},{24,16},{28,20},{1,9},{5... | collective-permute-start | bytes 227336 | tf_op jit(solution)/shard_map/ppermute | solution.py:335
  57.1 2.9 %collective-permute-done.10.refs_2_ = bf16[296,128]{1,0:T(8,128)(2,1)S(1)} collective-permute-done((bf16[296,128]{1,0:T(8,128)(2,1)S(1)}, bf16[296,128]{1,0:T(8,128)(2,1)S(1)}, u32[]{:S(2)}, u32[]{:S(2)}) %collective-permute-start.10) | collective-permute-done | bytes 75808 | tf_op jit(solution)/shard_map/ppermute | solution.py:335
  60.0 1.0 %collective-permute-start.15 = (bf16[296,128]{1,0:T(8,128)(2,1)S(1)}, bf16[296,128]{1,0:T(8,128)(2,1)S(1)}, u32[]{:S(2)}, u32[]{:S(2)}) collective-permute-start(bf16[296,128]{1,0:T(8,128)(2,1)S(1)} %get-tuple-element.39), channel_id=1, source_target_pairs={{0,4},{4,0},{8,12},{12,8},{16,20},{20,16},{24,28},{28,24},{1,5},{5... | collective-permute-start | bytes 227336 | tf_op jit(solution)/shard_map/ppermute | solution.py:335
  61.0 1.9 %collective-permute-done.12.refs_4_ = bf16[296,128]{1,0:T(8,128)(2,1)S(1)} collective-permute-done((bf16[296,128]{1,0:T(8,128)(2,1)S(1)}, bf16[296,128]{1,0:T(8,128)(2,1)S(1)}, u32[]{:S(2)}, u32[]{:S(2)}) %collective-permute-start.12) | collective-permute-done | bytes 75808 | tf_op jit(solution)/shard_map/ppermute | solution.py:335
  62.9 1.5 %collective-permute-done.15.refs_7_ = bf16[296,128]{1,0:T(8,128)(2,1)S(1)} collective-permute-done((bf16[296,128]{1,0:T(8,128)(2,1)S(1)}, bf16[296,128]{1,0:T(8,128)(2,1)S(1)}, u32[]{:S(2)}, u32[]{:S(2)}) %collective-permute-start.15) | collective-permute-done | bytes 75808 | tf_op jit(solution)/shard_map/ppermute | solution.py:335
  64.4 1.6 %collective-permute-start.17 = (f32[4,32]{1,0:T(4,128)S(1)}, f32[4,32]{1,0:T(4,128)S(1)}, u32[]{:S(2)}, u32[]{:S(2)}) collective-permute-start(f32[4,32]{1,0:T(4,128)S(1)} %slice_add_fusion.own), channel_id=1, source_target_pairs={{0,1},{1,0},{2,3},{3,2},{4,5},{5,4},{6,7},{7,6},{8,9},{9,8},{10,11... | collective-permute-start | bytes 1544 | tf_op jit(solution)/shard_map/ppermute | solution.py:335
  66.0 0.3 collective-permute-start.16
  66.3 1.4 %shard_map.74 = f32[2,192,768]{2,1,0:T(8,128)} custom-call(bf16[296,128]{1,0:T(8,128)(2,1)S(1)} %get-tuple-element.32.refs_0_, bf16[296,128]{1,0:T(8,128)(2,1)S(1)} %collective-permute-done.9.refs_1_, bf16[296,128]{1,0:T(8,128)(2,1)S(1)} %collective-permute-done.10.refs_2_, bf16[296,128]{1,0:T(8,128)(2,1)S(1)} %collective-permute-done.11.refs_3_, ...), custom_call_target="tpu_custom_call" | custom-call | tf_op jit(solution)/shard_map/pallas_call | solution.py:293
  67.7 0.4 collective-permute-done.17.own_mode
  68.1 0.7 %shard_map.75 = f32[4,4,2,8]{3,2,1,0:T(2,128)} custom-call(f32[4,32]{1,0:T(4,128)S(1)} %slice_add_fusion.own, f32[4,32]{1,0:T(4,128)S(1)} %collective-permute-done.16.core, f32[4,32]{1,0:T(4,128)S(1)} %collective-permute-done.17.own_mode, f32[4,32]{1,0:T(4,128)S(1)} %collective-permute-done.18.core_mode), custom_call_target="tpu_custom_call" | custom-call | tf_op jit(solution)/shard_map/pallas_call | solution.py:293
  (29 shorter events, 0.5 us)
Async XLA Ops:
  0.6 1.0 %copy-start.4 = (bf16[2,32,12,192]{3,1,2,0:T(8,128)(2,1)S(1)}, bf16[2,32,12,192]{3,1,2,0:T(8,128)(2,1)}, u32[]{:S(2)}) copy-start(bf16[2,32,12,192]{3,1,2,0:T(8,128)(2,1)} %param.6) | copy-start | bytes 884740
  1.6 3.2 %copy-start = (bf16[2,32,12,384]{3,1,2,0:T(8,128)(2,1)S(1)}, bf16[2,32,12,384]{3,1,2,0:T(8,128)(2,1)}, u32[]{:S(2)}) copy-start(bf16[2,32,12,384]{3,1,2,0:T(8,128)(2,1)} %param.5) | copy-start | bytes 1769476
  1.8 27.5 %copy-start.1 = (s32[8,3]{0,1:T(4,128)S(1)}, s32[8,3]{0,1:T(4,128)}, u32[]{:S(2)}) copy-start(s32[8,3]{0,1:T(4,128)} %param.7) | copy-start | bytes 292
  1.8 27.5 %copy-start.2 = (s32[4]{0:T(128)S(1)}, s32[4]{0:T(128)}, u32[]{:S(2)}) copy-start(s32[4]{0:T(128)} %gammas.3) | copy-start | bytes 52
  1.9 27.5 %copy-start.3 = (s32[128]{0:T(128)S(1)}, s32[128]{0:T(128)}, u32[]{:S(2)}) copy-start(s32[128]{0:T(128)} %constant.2.clone.table) | copy-start | bytes 1540
  1.9 8.0 %collective-permute-start = (bf16[96,768]{1,0:T(8,128)(2,1)S(1)}, bf16[96,768]{1,0:T(8,128)(2,1)S(1)}, u32[]{:S(2)}, u32[]{:S(2)}) collective-permute-start(bf16[96,768]{1,0:T(8,128)(2,1)S(1)} %get-tuple-element.22.after), channel_id=1, source_target_pairs={{0,4},{4,0},{1,5},{5,1},{2,6},{6,2},{3,7},{7,3},{8,12},{12,8},{9,1... | collective-permute-start | bytes 442376 | tf_op jit(solution)/shard_map/ppermute | solution.py:335
  5.4 8.7 %collective-permute-start.5 = (bf16[96,384]{1,0:T(8,128)(2,1)S(1)}, bf16[96,384]{1,0:T(8,128)(2,1)S(1)}, u32[]{:S(2)}, u32[]{:S(2)}) collective-permute-start(bf16[96,384]{1,0:T(8,128)(2,1)S(1)} %get-tuple-element.24), channel_id=1, source_target_pairs={{0,8},{8,0},{16,24},{24,16},{1,9},{9,1},{17,25},{25,17},{2,10},{10... | collective-permute-start | bytes 221192 | tf_op jit(solution)/shard_map/ppermute | solution.py:335
  7.0 7.7 %collective-permute-start.6 = (bf16[96,384]{1,0:T(8,128)(2,1)S(1)}, bf16[96,384]{1,0:T(8,128)(2,1)S(1)}, u32[]{:S(2)}, u32[]{:S(2)}) collective-permute-start(bf16[96,384]{1,0:T(8,128)(2,1)S(1)} %get-tuple-element.25), channel_id=1, source_target_pairs={{0,16},{8,24},{16,0},{24,8},{1,17},{9,25},{17,1},{25,9},{2,18},{10... | collective-permute-start | bytes 221192 | tf_op jit(solution)/shard_map/ppermute | solution.py:335
  9.6 7.0 %collective-permute-start.7 = (bf16[96,384]{1,0:T(8,128)(2,1)S(1)}, bf16[96,384]{1,0:T(8,128)(2,1)S(1)}, u32[]{:S(2)}, u32[]{:S(2)}) collective-permute-start(bf16[96,384]{1,0:T(8,128)(2,1)S(1)} %get-tuple-element.26), channel_id=1, source_target_pairs={{0,24},{8,16},{16,8},{24,0},{1,25},{9,17},{17,9},{25,1},{2,26},{10... | collective-permute-start | bytes 221192 | tf_op jit(solution)/shard_map/ppermute | solution.py:335
  9.9 19.5 %collective-permute-start.3 = (bf16[2,96,768]{2,1,0:T(8,128)(2,1)S(1)}, bf16[2,96,768]{2,1,0:T(8,128)(2,1)S(1)}, u32[]{:S(2)}, u32[]{:S(2)}) collective-permute-start(bf16[2,96,768]{2,1,0:T(8,128)(2,1)S(1)} %pad_maximum_fusion.refs_0_), channel_id=1, source_target_pairs={{0,8},{8,0},{16,24},{24,16},{1,9},{9,1},{17,25},{25,17},{2,10},{10... | collective-permute-start | bytes 884744 | tf_op jit(solution)/shard_map/ppermute | solution.py:335
  10.6 26.7 %collective-permute-start.2 = (bf16[2,96,768]{2,1,0:T(8,128)(2,1)S(1)}, bf16[2,96,768]{2,1,0:T(8,128)(2,1)S(1)}, u32[]{:S(2)}, u32[]{:S(2)}) collective-permute-start(bf16[2,96,768]{2,1,0:T(8,128)(2,1)S(1)} %pad_maximum_fusion.refs_0_), channel_id=1, source_target_pairs={{0,16},{8,24},{16,0},{24,8},{1,17},{9,25},{17,1},{25,9},{2,18},{10... | collective-permute-start | bytes 884744 | tf_op jit(solution)/shard_map/ppermute | solution.py:335
  14.1 23.2 %collective-permute-start.1 = (bf16[2,96,768]{2,1,0:T(8,128)(2,1)S(1)}, bf16[2,96,768]{2,1,0:T(8,128)(2,1)S(1)}, u32[]{:S(2)}, u32[]{:S(2)}) collective-permute-start(bf16[2,96,768]{2,1,0:T(8,128)(2,1)S(1)} %pad_maximum_fusion.refs_0_), channel_id=1, source_target_pairs={{0,24},{8,16},{16,8},{24,0},{1,25},{9,17},{17,9},{25,1},{2,26},{10... | collective-permute-start | bytes 884744 | tf_op jit(solution)/shard_map/ppermute | solution.py:335
  14.8 14.6 %collective-permute-start.4 = (bf16[192,384]{1,0:T(8,128)(2,1)S(1)}, bf16[192,384]{1,0:T(8,128)(2,1)S(1)}, u32[]{:S(2)}, u32[]{:S(2)}) collective-permute-start(bf16[192,384]{1,0:T(8,128)(2,1)S(1)} %get-tuple-element.23.refs_2_), channel_id=1, source_target_pairs={{0,4},{4,0},{1,5},{5,1},{2,6},{6,2},{3,7},{7,3},{8,12},{12,8},{9,1... | collective-permute-start | bytes 442376 | tf_op jit(solution)/shard_map/ppermute | solution.py:335
  40.4 2.9 %collective-permute-start.8 = (bf16[768,768]{1,0:T(8,128)(2,1)S(1)}, bf16[768,768]{1,0:T(8,128)(2,1)S(1)}, u32[]{:S(2)}, u32[]{:S(2)}) collective-permute-start(bf16[768,768]{1,0:T(8,128)(2,1)S(1)} %get-tuple-element.31), channel_id=1, source_target_pairs={{0,2},{2,0},{1,3},{3,1},{4,6},{6,4},{5,7},{7,5},{8,10},{10,8},{9,1... | collective-permute-start | bytes 3538952 | tf_op jit(solution)/shard_map/ppermute | solution.py:335
  44.2 11.9 %collective-permute-start.9 = (bf16[296,128]{1,0:T(8,128)(2,1)S(1)}, bf16[296,128]{1,0:T(8,128)(2,1)S(1)}, u32[]{:S(2)}, u32[]{:S(2)}) collective-permute-start(bf16[296,128]{1,0:T(8,128)(2,1)S(1)} %get-tuple-element.33), channel_id=1, source_target_pairs={{0,24},{4,28},{8,16},{12,20},{16,8},{20,12},{24,0},{28,4},{1,25},{... | collective-permute-start | bytes 227336 | tf_op jit(solution)/shard_map/ppermute | solution.py:335
  46.9 13.1 %collective-permute-start.10 = (bf16[296,128]{1,0:T(8,128)(2,1)S(1)}, bf16[296,128]{1,0:T(8,128)(2,1)S(1)}, u32[]{:S(2)}, u32[]{:S(2)}) collective-permute-start(bf16[296,128]{1,0:T(8,128)(2,1)S(1)} %get-tuple-element.34), channel_id=1, source_target_pairs={{0,16},{4,20},{8,24},{12,28},{16,0},{20,4},{24,8},{28,12},{1,17},{... | collective-permute-start | bytes 227336 | tf_op jit(solution)/shard_map/ppermute | solution.py:335
  50.3 10.7 %collective-permute-start.11 = (bf16[296,128]{1,0:T(8,128)(2,1)S(1)}, bf16[296,128]{1,0:T(8,128)(2,1)S(1)}, u32[]{:S(2)}, u32[]{:S(2)}) collective-permute-start(bf16[296,128]{1,0:T(8,128)(2,1)S(1)} %get-tuple-element.35), channel_id=1, source_target_pairs={{0,28},{4,24},{8,20},{12,16},{16,12},{20,8},{24,4},{28,0},{1,29},{... | collective-permute-start | bytes 227336 | tf_op jit(solution)/shard_map/ppermute | solution.py:335
  53.3 9.6 %collective-permute-start.12 = (bf16[296,128]{1,0:T(8,128)(2,1)S(1)}, bf16[296,128]{1,0:T(8,128)(2,1)S(1)}, u32[]{:S(2)}, u32[]{:S(2)}) collective-permute-start(bf16[296,128]{1,0:T(8,128)(2,1)S(1)} %get-tuple-element.36), channel_id=1, source_target_pairs={{0,20},{4,16},{8,28},{12,24},{16,4},{20,0},{24,12},{28,8},{1,21},{... | collective-permute-start | bytes 227336 | tf_op jit(solution)/shard_map/ppermute | solution.py:335
  53.3 9.6 %collective-permute-start.13 = (bf16[296,128]{1,0:T(8,128)(2,1)S(1)}, bf16[296,128]{1,0:T(8,128)(2,1)S(1)}, u32[]{:S(2)}, u32[]{:S(2)}) collective-permute-start(bf16[296,128]{1,0:T(8,128)(2,1)S(1)} %get-tuple-element.37), channel_id=1, source_target_pairs={{0,12},{4,8},{8,4},{12,0},{16,28},{20,24},{24,20},{28,16},{1,13},{... | collective-permute-start | bytes 227336 | tf_op jit(solution)/shard_map/ppermute | solution.py:335
  56.1 6.8 %collective-permute-start.14 = (bf16[296,128]{1,0:T(8,128)(2,1)S(1)}, bf16[296,128]{1,0:T(8,128)(2,1)S(1)}, u32[]{:S(2)}, u32[]{:S(2)}) collective-permute-start(bf16[296,128]{1,0:T(8,128)(2,1)S(1)} %get-tuple-element.38), channel_id=1, source_target_pairs={{0,8},{4,12},{8,0},{12,4},{16,24},{20,28},{24,16},{28,20},{1,9},{5... | collective-permute-start | bytes 227336 | tf_op jit(solution)/shard_map/ppermute | solution.py:335
  60.0 4.4 %collective-permute-start.15 = (bf16[296,128]{1,0:T(8,128)(2,1)S(1)}, bf16[296,128]{1,0:T(8,128)(2,1)S(1)}, u32[]{:S(2)}, u32[]{:S(2)}) collective-permute-start(bf16[296,128]{1,0:T(8,128)(2,1)S(1)} %get-tuple-element.39), channel_id=1, source_target_pairs={{0,4},{4,0},{8,12},{12,8},{16,20},{20,16},{24,28},{28,24},{1,5},{5... | collective-permute-start | bytes 227336 | tf_op jit(solution)/shard_map/ppermute | solution.py:335
  64.4 3.3 %collective-permute-start.18 = (f32[4,32]{1,0:T(4,128)S(1)}, f32[4,32]{1,0:T(4,128)S(1)}, u32[]{:S(2)}, u32[]{:S(2)}) collective-permute-start(f32[4,32]{1,0:T(4,128)S(1)} %slice_add_fusion.own), channel_id=1, source_target_pairs={{0,3},{1,2},{2,1},{3,0},{4,7},{5,6},{6,5},{7,4},{8,11},{9,10},{10,... | collective-permute-start | bytes 1544 | tf_op jit(solution)/shard_map/ppermute | solution.py:335
  64.4 3.7 %collective-permute-start.17 = (f32[4,32]{1,0:T(4,128)S(1)}, f32[4,32]{1,0:T(4,128)S(1)}, u32[]{:S(2)}, u32[]{:S(2)}) collective-permute-start(f32[4,32]{1,0:T(4,128)S(1)} %slice_add_fusion.own), channel_id=1, source_target_pairs={{0,1},{1,0},{2,3},{3,2},{4,5},{5,4},{6,7},{7,6},{8,9},{9,8},{10,11... | collective-permute-start | bytes 1544 | tf_op jit(solution)/shard_map/ppermute | solution.py:335
  66.0 2.1 %collective-permute-start.16 = (f32[4,32]{1,0:T(4,128)S(1)}, f32[4,32]{1,0:T(4,128)S(1)}, u32[]{:S(2)}, u32[]{:S(2)}) collective-permute-start(f32[4,32]{1,0:T(4,128)S(1)} %slice_add_fusion.own), channel_id=1, source_target_pairs={{0,2},{2,0},{1,3},{3,1},{4,6},{6,4},{5,7},{7,5},{8,10},{10,8},{9,1... | collective-permute-start | bytes 1544 | tf_op jit(solution)/shard_map/ppermute | solution.py:335

commit v5 on v4

--- a/solution.py
+++ b/solution.py
@@ -18,7 +18,7 @@
 F32 = jnp.float32
 
 
-ORDER = (6, 4, 7, 5, 3, 2, 1)
+ORDER = (6, 4, 2, 7, 5, 3, 1)
 COST = pl.CostEstimate(flops=2_000_000_000, bytes_accessed=8_000_000, transcendentals=0)
 
 

time: 69 us -> 68.3 us (0.990)
  starting transfers between devices: 28.7 us -> 27.8 us
    ppermute x19, starting transfers between devices: 28.7 us -> 27.8 us  [swap(): lax.ppermute(x, axis, [(i, i ^ mask) for i in range(lax.axis_size(axis))])]
where the time goes in v5:
time: 68.3 us; the launch traced here: 68.1 us
  starting transfers between devices  27.8 us (41%)
  Pallas kernels  16.7 us (24%)
  blocking collectives  12.7 us (19%)
  waiting for transfers between devices  8.98 us (13%)
  local copies, waits for them, and re-layouts  1.01 us (1%)
  between operations  0.79 us (1%)
    ppermute x19, starting transfers between devices, swap(): lax.ppermute(x, axis, [(i, i ^ mask) for i in range(lax.axis_size(axis))])  27.8 us
    pallas_call x6, Pallas kernels, call(): pl.pallas_call(kernel, out_shape=out_shape, in_specs=[SMEM] * len(scalars...  16 us
    all_gather x1, blocking collectives, fast_body(): eig_all = lax.all_gather(mine, ('x', 'mode')).reshape(2, 2, 3, 96, 384)  12.7 us
    ppermute x19, waiting for transfers between devices, swap(): lax.ppermute(x, axis, [(i, i ^ mask) for i in range(lax.axis_size(axis))])  8.98 us
  transfers between devices with their start and end apart: 19, of which 7 were waited for; matrix products, arithmetic and copies ran while one was open for 0% of the time, Pallas kernels for 17%

profile of v5, /device:TPU:0, one launch (start us, length us, event | category | flops | bytes accessed | tf_op | source)
XLA Modules:
  0.0 68.1 jit_solution(4829503321496734737)
XLA Ops:
  0.6 1.0 %copy-done.4 = bf16[2,32,12,192]{3,1,2,0:T(8,128)(2,1)S(1)} copy-done((bf16[2,32,12,192]{3,1,2,0:T(8,128)(2,1)S(1)}, bf16[2,32,12,192]{3,1,2,0:T(8,128)(2,1)}, u32[]{:S(2)}) %copy-start.4) | copy-done | bytes 294936
  1.9 3.0 %collective-permute-start = (bf16[96,768]{1,0:T(8,128)(2,1)S(1)}, bf16[96,768]{1,0:T(8,128)(2,1)S(1)}, u32[]{:S(2)}, u32[]{:S(2)}) collective-permute-start(bf16[96,768]{1,0:T(8,128)(2,1)S(1)} %get-tuple-element.22.after), channel_id=1, source_target_pairs={{0,4},{4,0},{1,5},{5,1},{2,6},{6,2},{3,7},{7,3},{8,12},{12,8},{9,1... | collective-permute-start | bytes 442376 | tf_op jit(solution)/shard_map/ppermute | solution.py:335
  4.9 0.5 shard_map.69
  5.4 1.6 %collective-permute-start.5 = (bf16[96,384]{1,0:T(8,128)(2,1)S(1)}, bf16[96,384]{1,0:T(8,128)(2,1)S(1)}, u32[]{:S(2)}, u32[]{:S(2)}) collective-permute-start(bf16[96,384]{1,0:T(8,128)(2,1)S(1)} %get-tuple-element.24), channel_id=1, source_target_pairs={{0,8},{8,0},{16,24},{24,16},{1,9},{9,1},{17,25},{25,17},{2,10},{10... | collective-permute-start | bytes 221192 | tf_op jit(solution)/shard_map/ppermute | solution.py:335
  7.0 2.6 %collective-permute-start.6 = (bf16[96,384]{1,0:T(8,128)(2,1)S(1)}, bf16[96,384]{1,0:T(8,128)(2,1)S(1)}, u32[]{:S(2)}, u32[]{:S(2)}) collective-permute-start(bf16[96,384]{1,0:T(8,128)(2,1)S(1)} %get-tuple-element.25), channel_id=1, source_target_pairs={{0,16},{8,24},{16,0},{24,8},{1,17},{9,25},{17,1},{25,9},{2,18},{10... | collective-permute-start | bytes 221192 | tf_op jit(solution)/shard_map/ppermute | solution.py:335
  9.6 0.2 collective-permute-start.7
  9.9 0.8 %collective-permute-start.3 = (bf16[2,96,768]{2,1,0:T(8,128)(2,1)S(1)}, bf16[2,96,768]{2,1,0:T(8,128)(2,1)S(1)}, u32[]{:S(2)}, u32[]{:S(2)}) collective-permute-start(bf16[2,96,768]{2,1,0:T(8,128)(2,1)S(1)} %pad_maximum_fusion.refs_0_), channel_id=1, source_target_pairs={{0,8},{8,0},{16,24},{24,16},{1,9},{9,1},{17,25},{25,17},{2,10},{10... | collective-permute-start | bytes 884744 | tf_op jit(solution)/shard_map/ppermute | solution.py:335
  10.6 3.5 %collective-permute-start.2 = (bf16[2,96,768]{2,1,0:T(8,128)(2,1)S(1)}, bf16[2,96,768]{2,1,0:T(8,128)(2,1)S(1)}, u32[]{:S(2)}, u32[]{:S(2)}) collective-permute-start(bf16[2,96,768]{2,1,0:T(8,128)(2,1)S(1)} %pad_maximum_fusion.refs_0_), channel_id=1, source_target_pairs={{0,16},{8,24},{16,0},{24,8},{1,17},{9,25},{17,1},{25,9},{2,18},{10... | collective-permute-start | bytes 884744 | tf_op jit(solution)/shard_map/ppermute | solution.py:335
  14.1 0.2 collective-permute-start.1
  14.3 0.4 collective-permute-done.6
  14.8 1.0 %collective-permute-start.4 = (bf16[192,384]{1,0:T(8,128)(2,1)S(1)}, bf16[192,384]{1,0:T(8,128)(2,1)S(1)}, u32[]{:S(2)}, u32[]{:S(2)}) collective-permute-start(bf16[192,384]{1,0:T(8,128)(2,1)S(1)} %get-tuple-element.23.refs_2_), channel_id=1, source_target_pairs={{0,4},{4,0},{1,5},{5,1},{2,6},{6,2},{3,7},{7,3},{8,12},{12,8},{9,1... | collective-permute-start | bytes 442376 | tf_op jit(solution)/shard_map/ppermute | solution.py:335
  15.7 0.9 %collective-permute-done.7 = bf16[96,384]{1,0:T(8,128)(2,1)S(1)} collective-permute-done((bf16[96,384]{1,0:T(8,128)(2,1)S(1)}, bf16[96,384]{1,0:T(8,128)(2,1)S(1)}, u32[]{:S(2)}, u32[]{:S(2)}) %collective-permute-start.7) | collective-permute-done | bytes 73760 | tf_op jit(solution)/shard_map/ppermute | solution.py:335
  16.7 12.7 %all-gather = bf16[12,96,384]{2,1,0:T(8,128)(2,1)S(1)} all-gather(bf16[3,96,384]{2,1,0:T(8,128)(2,1)S(1)} %pad_maximum_fusion.1), channel_id=2, replica_groups=mesh['z'=4,'x'=2,'core'=2,'mode'=2] {'x','mode'}, dimensions={0}, use_global_device_ids=true | all-gather | bytes 1105920 | tf_op jit(solution)/shard_map/all_gather | solution.py:356
  29.4 7.9 %shard_map.70 = (f32[768,768]{1,0:T(8,128)S(1)}, f32[768,768]{1,0:T(8,128)S(1)}, bf16[2,1536,768]{2,1,0:T(8,128)(2,1)S(1)}) custom-call(s32[4]{0:T(128)S(1)} %copy-done.2, s32[128]{0:T(128)S(1)} %copy-done.3, s32[3,8]{1,0:T(4,128)S(1)} %bitcast.18, bf16[2,96,768]{2,1,0:T(8,128)(2,1)S(1)} %pad_maximum_fusion.refs_0_, ...), custom_call_target="tpu_custom_call" | custom-call | tf_op jit(solution)/shard_map/pallas_call | solution.py:293
  37.4 3.1 %shard_map.71 = (bf16[768,768]{1,0:T(8,128)(2,1)S(1)}, bf16[768,1536]{1,0:T(8,128)(2,1)S(1)}) custom-call(s32[4]{0:T(128)S(1)} %copy-done.2, s32[128]{0:T(128)S(1)} %copy-done.3, bf16[2,96,768]{2,1,0:T(8,128)(2,1)S(1)} %collective-permute-done.1.second, bf16[2,96,768]{2,1,0:T(8,128)(2,1)S(1)} %collective-permute-done.2.first, ...), custom_call_target="tpu_custom_call" | custom-call | tf_op jit(solution)/shard_map/pallas_call | solution.py:293
  40.5 2.0 %shard_map.72.own = f32[768,768]{1,0:T(8,128)S(1)} custom-call(bf16[768,1536]{1,0:T(8,128)(2,1)S(1)} %get-tuple-element.29.left, bf16[2,1536,768]{2,1,0:T(8,128)(2,1)S(1)} %get-tuple-element.27.right, f32[768,768]{1,0:T(8,128)S(1)} %get-tuple-element.30.acc), custom_call_target="tpu_custom_call" | custom-call | tf_op jit(solution)/shard_map/pallas_call | solution.py:293
  42.5 0.8 %collective-permute-done.8.got = bf16[768,768]{1,0:T(8,128)(2,1)S(1)} collective-permute-done((bf16[768,768]{1,0:T(8,128)(2,1)S(1)}, bf16[768,768]{1,0:T(8,128)(2,1)S(1)}, u32[]{:S(2)}, u32[]{:S(2)}) %collective-permute-start.8) | collective-permute-done | bytes 1179680 | tf_op jit(solution)/shard_map/ppermute | solution.py:335
  43.3 0.9 %shard_map.73 = (bf16[296,128]{1,0:T(8,128)(2,1)S(1)}, bf16[296,128]{1,0:T(8,128)(2,1)S(1)}, bf16[296,128]{1,0:T(8,128)(2,1)S(1)}, bf16[296,128]{1,0:T(8,128)(2,...) custom-call(f32[768,768]{1,0:T(8,128)S(1)} %shard_map.72.own, ...), custom_call_target="tpu_custom_call" | custom-call | tf_op jit(solution)/shard_map/pallas_call | solution.py:293
  44.2 2.7 %collective-permute-start.9 = (bf16[296,128]{1,0:T(8,128)(2,1)S(1)}, bf16[296,128]{1,0:T(8,128)(2,1)S(1)}, u32[]{:S(2)}, u32[]{:S(2)}) collective-permute-start(bf16[296,128]{1,0:T(8,128)(2,1)S(1)} %get-tuple-element.33), channel_id=1, source_target_pairs={{0,24},{4,28},{8,16},{12,20},{16,8},{20,12},{24,0},{28,4},{1,25},{... | collective-permute-start | bytes 227336 | tf_op jit(solution)/shard_map/ppermute | solution.py:335
  46.9 3.4 %collective-permute-start.10 = (bf16[296,128]{1,0:T(8,128)(2,1)S(1)}, bf16[296,128]{1,0:T(8,128)(2,1)S(1)}, u32[]{:S(2)}, u32[]{:S(2)}) collective-permute-start(bf16[296,128]{1,0:T(8,128)(2,1)S(1)} %get-tuple-element.34), channel_id=1, source_target_pairs={{0,16},{4,20},{8,24},{12,28},{16,0},{20,4},{24,8},{28,12},{1,17},{... | collective-permute-start | bytes 227336 | tf_op jit(solution)/shard_map/ppermute | solution.py:335
  50.5 2.8 %collective-permute-start.12 = (bf16[296,128]{1,0:T(8,128)(2,1)S(1)}, bf16[296,128]{1,0:T(8,128)(2,1)S(1)}, u32[]{:S(2)}, u32[]{:S(2)}) collective-permute-start(bf16[296,128]{1,0:T(8,128)(2,1)S(1)} %get-tuple-element.36), channel_id=1, source_target_pairs={{0,28},{4,24},{8,20},{12,16},{16,12},{20,8},{24,4},{28,0},{1,29},{... | collective-permute-start | bytes 227336 | tf_op jit(solution)/shard_map/ppermute | solution.py:335
  53.3 1.4 %collective-permute-start.13 = (bf16[296,128]{1,0:T(8,128)(2,1)S(1)}, bf16[296,128]{1,0:T(8,128)(2,1)S(1)}, u32[]{:S(2)}, u32[]{:S(2)}) collective-permute-start(bf16[296,128]{1,0:T(8,128)(2,1)S(1)} %get-tuple-element.37), channel_id=1, source_target_pairs={{0,20},{4,16},{8,28},{12,24},{16,4},{20,0},{24,12},{28,8},{1,21},{... | collective-permute-start | bytes 227336 | tf_op jit(solution)/shard_map/ppermute | solution.py:335
  54.7 1.5 %collective-permute-start.14 = (bf16[296,128]{1,0:T(8,128)(2,1)S(1)}, bf16[296,128]{1,0:T(8,128)(2,1)S(1)}, u32[]{:S(2)}, u32[]{:S(2)}) collective-permute-start(bf16[296,128]{1,0:T(8,128)(2,1)S(1)} %get-tuple-element.38), channel_id=1, source_target_pairs={{0,12},{4,8},{8,4},{12,0},{16,28},{20,24},{24,20},{28,16},{1,13},{... | collective-permute-start | bytes 227336 | tf_op jit(solution)/shard_map/ppermute | solution.py:335
  56.2 2.8 %collective-permute-done.10.refs_2_ = bf16[296,128]{1,0:T(8,128)(2,1)S(1)} collective-permute-done((bf16[296,128]{1,0:T(8,128)(2,1)S(1)}, bf16[296,128]{1,0:T(8,128)(2,1)S(1)}, u32[]{:S(2)}, u32[]{:S(2)}) %collective-permute-start.10) | collective-permute-done | bytes 75808 | tf_op jit(solution)/shard_map/ppermute | solution.py:335
  59.1 1.0 %collective-permute-start.15 = (bf16[296,128]{1,0:T(8,128)(2,1)S(1)}, bf16[296,128]{1,0:T(8,128)(2,1)S(1)}, u32[]{:S(2)}, u32[]{:S(2)}) collective-permute-start(bf16[296,128]{1,0:T(8,128)(2,1)S(1)} %get-tuple-element.39), channel_id=1, source_target_pairs={{0,4},{4,0},{8,12},{12,8},{16,20},{20,16},{24,28},{28,24},{1,5},{5... | collective-permute-start | bytes 227336 | tf_op jit(solution)/shard_map/ppermute | solution.py:335
  60.1 2.8 %collective-permute-done.13.refs_5_ = bf16[296,128]{1,0:T(8,128)(2,1)S(1)} collective-permute-done((bf16[296,128]{1,0:T(8,128)(2,1)S(1)}, bf16[296,128]{1,0:T(8,128)(2,1)S(1)}, u32[]{:S(2)}, u32[]{:S(2)}) %collective-permute-start.13) | collective-permute-done | bytes 75808 | tf_op jit(solution)/shard_map/ppermute | solution.py:335
  62.9 0.8 %collective-permute-done.15.refs_7_ = bf16[296,128]{1,0:T(8,128)(2,1)S(1)} collective-permute-done((bf16[296,128]{1,0:T(8,128)(2,1)S(1)}, bf16[296,128]{1,0:T(8,128)(2,1)S(1)}, u32[]{:S(2)}, u32[]{:S(2)}) %collective-permute-start.15) | collective-permute-done | bytes 75808 | tf_op jit(solution)/shard_map/ppermute | solution.py:335
  63.8 1.6 %collective-permute-start.17 = (f32[4,32]{1,0:T(4,128)S(1)}, f32[4,32]{1,0:T(4,128)S(1)}, u32[]{:S(2)}, u32[]{:S(2)}) collective-permute-start(f32[4,32]{1,0:T(4,128)S(1)} %slice_add_fusion.own), channel_id=1, source_target_pairs={{0,1},{1,0},{2,3},{3,2},{4,5},{5,4},{6,7},{7,6},{8,9},{9,8},{10,11... | collective-permute-start | bytes 1544 | tf_op jit(solution)/shard_map/ppermute | solution.py:335
  65.4 0.3 collective-permute-start.16
  65.6 1.4 %shard_map.74 = f32[2,192,768]{2,1,0:T(8,128)} custom-call(bf16[296,128]{1,0:T(8,128)(2,1)S(1)} %get-tuple-element.32.refs_0_, bf16[296,128]{1,0:T(8,128)(2,1)S(1)} %collective-permute-done.9.refs_1_, bf16[296,128]{1,0:T(8,128)(2,1)S(1)} %collective-permute-done.10.refs_2_, bf16[296,128]{1,0:T(8,128)(2,1)S(1)} %collective-permute-done.11.refs_3_, ...), custom_call_target="tpu_custom_call" | custom-call | tf_op jit(solution)/shard_map/pallas_call | solution.py:293
  67.1 0.4 collective-permute-done.17.own_mode
  67.5 0.7 %shard_map.75 = f32[4,4,2,8]{3,2,1,0:T(2,128)} custom-call(f32[4,32]{1,0:T(4,128)S(1)} %slice_add_fusion.own, f32[4,32]{1,0:T(4,128)S(1)} %collective-permute-done.16.core, f32[4,32]{1,0:T(4,128)S(1)} %collective-permute-done.17.own_mode, f32[4,32]{1,0:T(4,128)S(1)} %collective-permute-done.18.core_mode), custom_call_target="tpu_custom_call" | custom-call | tf_op jit(solution)/shard_map/pallas_call | solution.py:293
  (29 shorter events, 0.6 us)
Async XLA Ops:
  0.6 1.0 %copy-start.4 = (bf16[2,32,12,192]{3,1,2,0:T(8,128)(2,1)S(1)}, bf16[2,32,12,192]{3,1,2,0:T(8,128)(2,1)}, u32[]{:S(2)}) copy-start(bf16[2,32,12,192]{3,1,2,0:T(8,128)(2,1)} %param.6) | copy-start | bytes 884740
  1.6 3.2 %copy-start = (bf16[2,32,12,384]{3,1,2,0:T(8,128)(2,1)S(1)}, bf16[2,32,12,384]{3,1,2,0:T(8,128)(2,1)}, u32[]{:S(2)}) copy-start(bf16[2,32,12,384]{3,1,2,0:T(8,128)(2,1)} %param.5) | copy-start | bytes 1769476
  1.8 27.5 %copy-start.1 = (s32[8,3]{0,1:T(4,128)S(1)}, s32[8,3]{0,1:T(4,128)}, u32[]{:S(2)}) copy-start(s32[8,3]{0,1:T(4,128)} %param.7) | copy-start | bytes 292
  1.8 27.5 %copy-start.2 = (s32[4]{0:T(128)S(1)}, s32[4]{0:T(128)}, u32[]{:S(2)}) copy-start(s32[4]{0:T(128)} %gammas.3) | copy-start | bytes 52
  1.9 27.5 %copy-start.3 = (s32[128]{0:T(128)S(1)}, s32[128]{0:T(128)}, u32[]{:S(2)}) copy-start(s32[128]{0:T(128)} %constant.2.clone.table) | copy-start | bytes 1540
  1.9 8.0 %collective-permute-start = (bf16[96,768]{1,0:T(8,128)(2,1)S(1)}, bf16[96,768]{1,0:T(8,128)(2,1)S(1)}, u32[]{:S(2)}, u32[]{:S(2)}) collective-permute-start(bf16[96,768]{1,0:T(8,128)(2,1)S(1)} %get-tuple-element.22.after), channel_id=1, source_target_pairs={{0,4},{4,0},{1,5},{5,1},{2,6},{6,2},{3,7},{7,3},{8,12},{12,8},{9,1... | collective-permute-start | bytes 442376 | tf_op jit(solution)/shard_map/ppermute | solution.py:335
  5.4 8.7 %collective-permute-start.5 = (bf16[96,384]{1,0:T(8,128)(2,1)S(1)}, bf16[96,384]{1,0:T(8,128)(2,1)S(1)}, u32[]{:S(2)}, u32[]{:S(2)}) collective-permute-start(bf16[96,384]{1,0:T(8,128)(2,1)S(1)} %get-tuple-element.24), channel_id=1, source_target_pairs={{0,8},{8,0},{16,24},{24,16},{1,9},{9,1},{17,25},{25,17},{2,10},{10... | collective-permute-start | bytes 221192 | tf_op jit(solution)/shard_map/ppermute | solution.py:335
  7.0 7.7 %collective-permute-start.6 = (bf16[96,384]{1,0:T(8,128)(2,1)S(1)}, bf16[96,384]{1,0:T(8,128)(2,1)S(1)}, u32[]{:S(2)}, u32[]{:S(2)}) collective-permute-start(bf16[96,384]{1,0:T(8,128)(2,1)S(1)} %get-tuple-element.25), channel_id=1, source_target_pairs={{0,16},{8,24},{16,0},{24,8},{1,17},{9,25},{17,1},{25,9},{2,18},{10... | collective-permute-start | bytes 221192 | tf_op jit(solution)/shard_map/ppermute | solution.py:335
  9.6 7.0 %collective-permute-start.7 = (bf16[96,384]{1,0:T(8,128)(2,1)S(1)}, bf16[96,384]{1,0:T(8,128)(2,1)S(1)}, u32[]{:S(2)}, u32[]{:S(2)}) collective-permute-start(bf16[96,384]{1,0:T(8,128)(2,1)S(1)} %get-tuple-element.26), channel_id=1, source_target_pairs={{0,24},{8,16},{16,8},{24,0},{1,25},{9,17},{17,9},{25,1},{2,26},{10... | collective-permute-start | bytes 221192 | tf_op jit(solution)/shard_map/ppermute | solution.py:335
  9.9 19.5 %collective-permute-start.3 = (bf16[2,96,768]{2,1,0:T(8,128)(2,1)S(1)}, bf16[2,96,768]{2,1,0:T(8,128)(2,1)S(1)}, u32[]{:S(2)}, u32[]{:S(2)}) collective-permute-start(bf16[2,96,768]{2,1,0:T(8,128)(2,1)S(1)} %pad_maximum_fusion.refs_0_), channel_id=1, source_target_pairs={{0,8},{8,0},{16,24},{24,16},{1,9},{9,1},{17,25},{25,17},{2,10},{10... | collective-permute-start | bytes 884744 | tf_op jit(solution)/shard_map/ppermute | solution.py:335
  10.6 26.7 %collective-permute-start.2 = (bf16[2,96,768]{2,1,0:T(8,128)(2,1)S(1)}, bf16[2,96,768]{2,1,0:T(8,128)(2,1)S(1)}, u32[]{:S(2)}, u32[]{:S(2)}) collective-permute-start(bf16[2,96,768]{2,1,0:T(8,128)(2,1)S(1)} %pad_maximum_fusion.refs_0_), channel_id=1, source_target_pairs={{0,16},{8,24},{16,0},{24,8},{1,17},{9,25},{17,1},{25,9},{2,18},{10... | collective-permute-start | bytes 884744 | tf_op jit(solution)/shard_map/ppermute | solution.py:335
  14.1 23.2 %collective-permute-start.1 = (bf16[2,96,768]{2,1,0:T(8,128)(2,1)S(1)}, bf16[2,96,768]{2,1,0:T(8,128)(2,1)S(1)}, u32[]{:S(2)}, u32[]{:S(2)}) collective-permute-start(bf16[2,96,768]{2,1,0:T(8,128)(2,1)S(1)} %pad_maximum_fusion.refs_0_), channel_id=1, source_target_pairs={{0,24},{8,16},{16,8},{24,0},{1,25},{9,17},{17,9},{25,1},{2,26},{10... | collective-permute-start | bytes 884744 | tf_op jit(solution)/shard_map/ppermute | solution.py:335
  14.8 14.6 %collective-permute-start.4 = (bf16[192,384]{1,0:T(8,128)(2,1)S(1)}, bf16[192,384]{1,0:T(8,128)(2,1)S(1)}, u32[]{:S(2)}, u32[]{:S(2)}) collective-permute-start(bf16[192,384]{1,0:T(8,128)(2,1)S(1)} %get-tuple-element.23.refs_2_), channel_id=1, source_target_pairs={{0,4},{4,0},{1,5},{5,1},{2,6},{6,2},{3,7},{7,3},{8,12},{12,8},{9,1... | collective-permute-start | bytes 442376 | tf_op jit(solution)/shard_map/ppermute | solution.py:335
  40.4 2.9 %collective-permute-start.8 = (bf16[768,768]{1,0:T(8,128)(2,1)S(1)}, bf16[768,768]{1,0:T(8,128)(2,1)S(1)}, u32[]{:S(2)}, u32[]{:S(2)}) collective-permute-start(bf16[768,768]{1,0:T(8,128)(2,1)S(1)} %get-tuple-element.31), channel_id=1, source_target_pairs={{0,2},{2,0},{1,3},{3,1},{4,6},{6,4},{5,7},{7,5},{8,10},{10,8},{9,1... | collective-permute-start | bytes 3538952 | tf_op jit(solution)/shard_map/ppermute | solution.py:335
  44.2 10.5 %collective-permute-start.9 = (bf16[296,128]{1,0:T(8,128)(2,1)S(1)}, bf16[296,128]{1,0:T(8,128)(2,1)S(1)}, u32[]{:S(2)}, u32[]{:S(2)}) collective-permute-start(bf16[296,128]{1,0:T(8,128)(2,1)S(1)} %get-tuple-element.33), channel_id=1, source_target_pairs={{0,24},{4,28},{8,16},{12,20},{16,8},{20,12},{24,0},{28,4},{1,25},{... | collective-permute-start | bytes 227336 | tf_op jit(solution)/shard_map/ppermute | solution.py:335
  46.9 12.1 %collective-permute-start.10 = (bf16[296,128]{1,0:T(8,128)(2,1)S(1)}, bf16[296,128]{1,0:T(8,128)(2,1)S(1)}, u32[]{:S(2)}, u32[]{:S(2)}) collective-permute-start(bf16[296,128]{1,0:T(8,128)(2,1)S(1)} %get-tuple-element.34), channel_id=1, source_target_pairs={{0,16},{4,20},{8,24},{12,28},{16,0},{20,4},{24,8},{28,12},{1,17},{... | collective-permute-start | bytes 227336 | tf_op jit(solution)/shard_map/ppermute | solution.py:335
  50.3 9.8 %collective-permute-start.11 = (bf16[296,128]{1,0:T(8,128)(2,1)S(1)}, bf16[296,128]{1,0:T(8,128)(2,1)S(1)}, u32[]{:S(2)}, u32[]{:S(2)}) collective-permute-start(bf16[296,128]{1,0:T(8,128)(2,1)S(1)} %get-tuple-element.35), channel_id=1, source_target_pairs={{0,8},{4,12},{8,0},{12,4},{16,24},{20,28},{24,16},{28,20},{1,9},{5... | collective-permute-start | bytes 227336 | tf_op jit(solution)/shard_map/ppermute | solution.py:335
  50.5 9.6 %collective-permute-start.12 = (bf16[296,128]{1,0:T(8,128)(2,1)S(1)}, bf16[296,128]{1,0:T(8,128)(2,1)S(1)}, u32[]{:S(2)}, u32[]{:S(2)}) collective-permute-start(bf16[296,128]{1,0:T(8,128)(2,1)S(1)} %get-tuple-element.36), channel_id=1, source_target_pairs={{0,28},{4,24},{8,20},{12,16},{16,12},{20,8},{24,4},{28,0},{1,29},{... | collective-permute-start | bytes 227336 | tf_op jit(solution)/shard_map/ppermute | solution.py:335
  53.3 9.6 %collective-permute-start.13 = (bf16[296,128]{1,0:T(8,128)(2,1)S(1)}, bf16[296,128]{1,0:T(8,128)(2,1)S(1)}, u32[]{:S(2)}, u32[]{:S(2)}) collective-permute-start(bf16[296,128]{1,0:T(8,128)(2,1)S(1)} %get-tuple-element.37), channel_id=1, source_target_pairs={{0,20},{4,16},{8,28},{12,24},{16,4},{20,0},{24,12},{28,8},{1,21},{... | collective-permute-start | bytes 227336 | tf_op jit(solution)/shard_map/ppermute | solution.py:335
  54.7 8.2 %collective-permute-start.14 = (bf16[296,128]{1,0:T(8,128)(2,1)S(1)}, bf16[296,128]{1,0:T(8,128)(2,1)S(1)}, u32[]{:S(2)}, u32[]{:S(2)}) collective-permute-start(bf16[296,128]{1,0:T(8,128)(2,1)S(1)} %get-tuple-element.38), channel_id=1, source_target_pairs={{0,12},{4,8},{8,4},{12,0},{16,28},{20,24},{24,20},{28,16},{1,13},{... | collective-permute-start | bytes 227336 | tf_op jit(solution)/shard_map/ppermute | solution.py:335
  59.1 4.6 %collective-permute-start.15 = (bf16[296,128]{1,0:T(8,128)(2,1)S(1)}, bf16[296,128]{1,0:T(8,128)(2,1)S(1)}, u32[]{:S(2)}, u32[]{:S(2)}) collective-permute-start(bf16[296,128]{1,0:T(8,128)(2,1)S(1)} %get-tuple-element.39), channel_id=1, source_target_pairs={{0,4},{4,0},{8,12},{12,8},{16,20},{20,16},{24,28},{28,24},{1,5},{5... | collective-permute-start | bytes 227336 | tf_op jit(solution)/shard_map/ppermute | solution.py:335
  63.8 3.3 %collective-permute-start.18 = (f32[4,32]{1,0:T(4,128)S(1)}, f32[4,32]{1,0:T(4,128)S(1)}, u32[]{:S(2)}, u32[]{:S(2)}) collective-permute-start(f32[4,32]{1,0:T(4,128)S(1)} %slice_add_fusion.own), channel_id=1, source_target_pairs={{0,3},{1,2},{2,1},{3,0},{4,7},{5,6},{6,5},{7,4},{8,11},{9,10},{10,... | collective-permute-start | bytes 1544 | tf_op jit(solution)/shard_map/ppermute | solution.py:335
  63.8 3.7 %collective-permute-start.17 = (f32[4,32]{1,0:T(4,128)S(1)}, f32[4,32]{1,0:T(4,128)S(1)}, u32[]{:S(2)}, u32[]{:S(2)}) collective-permute-start(f32[4,32]{1,0:T(4,128)S(1)} %slice_add_fusion.own), channel_id=1, source_target_pairs={{0,1},{1,0},{2,3},{3,2},{4,5},{5,4},{6,7},{7,6},{8,9},{9,8},{10,11... | collective-permute-start | bytes 1544 | tf_op jit(solution)/shard_map/ppermute | solution.py:335
  65.4 2.1 %collective-permute-start.16 = (f32[4,32]{1,0:T(4,128)S(1)}, f32[4,32]{1,0:T(4,128)S(1)}, u32[]{:S(2)}, u32[]{:S(2)}) collective-permute-start(f32[4,32]{1,0:T(4,128)S(1)} %slice_add_fusion.own), channel_id=1, source_target_pairs={{0,2},{2,0},{1,3},{3,1},{4,6},{6,4},{5,7},{7,5},{8,10},{10,8},{9,1... | collective-permute-start | bytes 1544 | tf_op jit(solution)/shard_map/ppermute | solution.py:335

commit v6 on v5

--- a/solution.py
+++ b/solution.py
@@ -172,18 +172,17 @@
 def build_right(blocks, k, m, cosine, sine, right, phases, spread):
     lane = lax.broadcasted_iota(jnp.int32, (96, 384), 1)
     build_phases(cosine, sine, (k * 2 + m) * 32, phases)
-    for side, (spin, block) in enumerate(blocks):
+    for spin, block in blocks:
         w = block.astype(F32)
         turns = [shift_lanes(w, 96 * by) for by in range(4)]
-        for part in range(4):
-            x = by_quarter(lane, *[turns[(k4 - part) % 4] for k4 in range(4)])
-            spread[side, part] = -x if part % 2 else x
-    for h in range(2):
-        cos, sin = phases[h, 0][None], phases[h, 1][None]
-        for side, (spin, _) in enumerate(blocks):
-            for low in range(2):
-                re = spread[side, low * 2].reshape(3, 32, 384)
-                im = spread[side, low * 2 + 1].reshape(3, 32, 384)
+        copies = [
+            by_quarter(lane, *[turns[(k4 - part) % 4] for k4 in range(4)]).reshape(3, 32, 384)
+            for part in range(4)
+        ]
+        for low in range(2):
+            re, im = copies[low * 2], -copies[low * 2 + 1]
+            for h in range(2):
+                cos, sin = phases[h, 0][None], phases[h, 1][None]
                 at = (spin + low) * 384 + (k % 2) * 192 + m * 96
                 rows = slice(at, at + 96)
                 right[h, rows, 0:384] = (cos * re + sin * im).reshape(96, 384).astype(BF16)
@@ -223,9 +222,14 @@
 def given_kernel(gammas, table, second, first, right, acc, out, left, base):
     build_base(first, second, base)
     build_left(base, gammas, table, left)
-    for n in range(3):
+    for n in range(2):
         at, part = product(left, right, lax.axis_index("core") ^ 1, n)
         out[:, at] = (acc[:, at] + part).astype(BF16)
+
+
+def rest_kernel(left, right, acc, out):
+    at, part = product(left, right, lax.axis_index("core") ^ 1, 2)
+    out[...] = (acc[:, at] + part).astype(BF16)
 
 
 def own_kernel(left, right, acc, out):
@@ -234,7 +238,7 @@
         out[:, at] = acc[:, at] + part
 
 
-def finish_kernel(own, got, *rest):
+def finish_kernel(own, got, got_rest, *rest):
     outs, pairs = rest[:8], rest[8]
     z, x, _ = here()
     low = lax.broadcasted_iota(jnp.int32, (96, 384), 1) < 192
@@ -242,8 +246,12 @@
     for k in range(4):
         (a, b), (c, d) = [
             [
-                own[pl.ds(at, 96), lanes] + got[pl.ds(at, 96), lanes].astype(F32)
-                for lanes in (slice(0, 384), slice(384, 768))
+                own[pl.ds(at, 96), :384] + got[pl.ds(at, 96), :384].astype(F32),
+                own[pl.ds(at, 96), 384:]
+                + jnp.concatenate(
+                    [got[pl.ds(at, 96), 384:].astype(F32), got_rest[pl.ds(at, 96), :].astype(F32)],
+                    axis=1,
+                ),
             ]
             for at in (pl.multiple_of(gs[k] * 192, 96), pl.multiple_of(gs[k] * 192 + 96, 96))
         ]
@@ -373,14 +381,17 @@
         given_kernel,
         [sols[3], sols[2], right, acc_other],
         scalars,
-        [jax.ShapeDtypeStruct((768, 768), BF16), jax.ShapeDtypeStruct((768, 1536), BF16)],
+        [jax.ShapeDtypeStruct((768, 512), BF16), jax.ShapeDtypeStruct((768, 1536), BF16)],
         [BASE],
     )
-    taken = swap(given, "core", 1)
+    given_rest = call(
+        rest_kernel, [left, right, acc_other], [], jax.ShapeDtypeStruct((768, 256), BF16)
+    )
+    taken = [swap(given, "core", 1), swap(given_rest, "core", 1)]
     own = call(own_kernel, [left, right, acc_own], [], total)
     sent = call(
         finish_kernel,
-        [own, taken],
+        [own, *taken],
         [],
         [jax.ShapeDtypeStruct((296, 128), BF16)] * 8,
         [pltpu.VMEM((32, 384), F32)],

time: 68.3 us -> 68.1 us (level)
  waiting for transfers between devices: 8.98 us -> 7.91 us
  starting transfers between devices: 27.8 us -> 28.5 us
    ppermute x19 -> x20, waiting for transfers between devices: 8.98 us -> 7.91 us  [swap(): lax.ppermute(x, axis, [(i, i ^ mask) for i in range(lax.axis_size(axis))])]
    ppermute x19 -> x20, starting transfers between devices: 27.8 us -> 28.5 us  [swap(): lax.ppermute(x, axis, [(i, i ^ mask) for i in range(lax.axis_size(axis))])]
    pallas_call x6 -> x7, Pallas kernels: 16 us -> 16.2 us  [call(): pl.pallas_call(kernel, out_shape=out_shape, in_specs=[SMEM] * len(scalars...]
  transfers between devices with their start and end apart: 19 -> 20, of which waited for: 7 -> 6; matrix products, arithmetic and copies ran while one was open for 0% -> 0% of each run, Pallas kernels for 17% -> 19%
where the time goes in v6:
time: 68.1 us; the launch traced here: 68 us
  starting transfers between devices  28.5 us (42%)
  Pallas kernels  16.9 us (25%)
  blocking collectives  12.7 us (19%)
  waiting for transfers between devices  7.91 us (12%)
  local copies, waits for them, and re-layouts  1.01 us (1%)
  between operations  0.81 us (1%)
    ppermute x20, starting transfers between devices, swap(): lax.ppermute(x, axis, [(i, i ^ mask) for i in range(lax.axis_size(axis))])  28.5 us
    pallas_call x7, Pallas kernels, call(): pl.pallas_call(kernel, out_shape=out_shape, in_specs=[SMEM] * len(scalars...  16.2 us
    all_gather x1, blocking collectives, fast_body(): eig_all = lax.all_gather(mine, ('x', 'mode')).reshape(2, 2, 3, 96, 384)  12.7 us
    ppermute x20, waiting for transfers between devices, swap(): lax.ppermute(x, axis, [(i, i ^ mask) for i in range(lax.axis_size(axis))])  7.91 us
  transfers between devices with their start and end apart: 20, of which 6 were waited for; matrix products, arithmetic and copies ran while one was open for 0% of the time, Pallas kernels for 19%

profile of v6, /device:TPU:0, one launch (start us, length us, event | category | flops | bytes accessed | tf_op | source)
XLA Modules:
  0.0 68.0 jit_solution(6214773895664049388)
XLA Ops:
  0.6 1.0 %copy-done.4 = bf16[2,32,12,192]{3,1,2,0:T(8,128)(2,1)S(1)} copy-done((bf16[2,32,12,192]{3,1,2,0:T(8,128)(2,1)S(1)}, bf16[2,32,12,192]{3,1,2,0:T(8,128)(2,1)}, u32[]{:S(2)}) %copy-start.4) | copy-done | bytes 294936
  1.9 3.0 %collective-permute-start = (bf16[96,768]{1,0:T(8,128)(2,1)S(1)}, bf16[96,768]{1,0:T(8,128)(2,1)S(1)}, u32[]{:S(2)}, u32[]{:S(2)}) collective-permute-start(bf16[96,768]{1,0:T(8,128)(2,1)S(1)} %get-tuple-element.22.after), channel_id=1, source_target_pairs={{0,4},{4,0},{1,5},{5,1},{2,6},{6,2},{3,7},{7,3},{8,12},{12,8},{9,1... | collective-permute-start | bytes 442376 | tf_op jit(solution)/shard_map/ppermute | solution.py:343
  4.9 0.5 shard_map.69
  5.4 1.6 %collective-permute-start.5 = (bf16[96,384]{1,0:T(8,128)(2,1)S(1)}, bf16[96,384]{1,0:T(8,128)(2,1)S(1)}, u32[]{:S(2)}, u32[]{:S(2)}) collective-permute-start(bf16[96,384]{1,0:T(8,128)(2,1)S(1)} %get-tuple-element.24), channel_id=1, source_target_pairs={{0,8},{8,0},{16,24},{24,16},{1,9},{9,1},{17,25},{25,17},{2,10},{10... | collective-permute-start | bytes 221192 | tf_op jit(solution)/shard_map/ppermute | solution.py:343
  7.0 2.6 %collective-permute-start.6 = (bf16[96,384]{1,0:T(8,128)(2,1)S(1)}, bf16[96,384]{1,0:T(8,128)(2,1)S(1)}, u32[]{:S(2)}, u32[]{:S(2)}) collective-permute-start(bf16[96,384]{1,0:T(8,128)(2,1)S(1)} %get-tuple-element.25), channel_id=1, source_target_pairs={{0,16},{8,24},{16,0},{24,8},{1,17},{9,25},{17,1},{25,9},{2,18},{10... | collective-permute-start | bytes 221192 | tf_op jit(solution)/shard_map/ppermute | solution.py:343
  9.6 0.2 collective-permute-start.7
  9.9 0.8 %collective-permute-start.3 = (bf16[2,96,768]{2,1,0:T(8,128)(2,1)S(1)}, bf16[2,96,768]{2,1,0:T(8,128)(2,1)S(1)}, u32[]{:S(2)}, u32[]{:S(2)}) collective-permute-start(bf16[2,96,768]{2,1,0:T(8,128)(2,1)S(1)} %pad_maximum_fusion.refs_0_), channel_id=1, source_target_pairs={{0,8},{8,0},{16,24},{24,16},{1,9},{9,1},{17,25},{25,17},{2,10},{10... | collective-permute-start | bytes 884744 | tf_op jit(solution)/shard_map/ppermute | solution.py:343
  10.6 3.5 %collective-permute-start.2 = (bf16[2,96,768]{2,1,0:T(8,128)(2,1)S(1)}, bf16[2,96,768]{2,1,0:T(8,128)(2,1)S(1)}, u32[]{:S(2)}, u32[]{:S(2)}) collective-permute-start(bf16[2,96,768]{2,1,0:T(8,128)(2,1)S(1)} %pad_maximum_fusion.refs_0_), channel_id=1, source_target_pairs={{0,16},{8,24},{16,0},{24,8},{1,17},{9,25},{17,1},{25,9},{2,18},{10... | collective-permute-start | bytes 884744 | tf_op jit(solution)/shard_map/ppermute | solution.py:343
  14.3 0.4 collective-permute-done.6
  14.8 1.0 %collective-permute-start.4 = (bf16[192,384]{1,0:T(8,128)(2,1)S(1)}, bf16[192,384]{1,0:T(8,128)(2,1)S(1)}, u32[]{:S(2)}, u32[]{:S(2)}) collective-permute-start(bf16[192,384]{1,0:T(8,128)(2,1)S(1)} %get-tuple-element.23.refs_2_), channel_id=1, source_target_pairs={{0,4},{4,0},{1,5},{5,1},{2,6},{6,2},{3,7},{7,3},{8,12},{12,8},{9,1... | collective-permute-start | bytes 442376 | tf_op jit(solution)/shard_map/ppermute | solution.py:343
  15.7 0.9 %collective-permute-done.7 = bf16[96,384]{1,0:T(8,128)(2,1)S(1)} collective-permute-done((bf16[96,384]{1,0:T(8,128)(2,1)S(1)}, bf16[96,384]{1,0:T(8,128)(2,1)S(1)}, u32[]{:S(2)}, u32[]{:S(2)}) %collective-permute-start.7) | collective-permute-done | bytes 73760 | tf_op jit(solution)/shard_map/ppermute | solution.py:343
  16.7 12.7 %all-gather = bf16[12,96,384]{2,1,0:T(8,128)(2,1)S(1)} all-gather(bf16[3,96,384]{2,1,0:T(8,128)(2,1)S(1)} %pad_maximum_fusion.1), channel_id=2, replica_groups=mesh['z'=4,'x'=2,'core'=2,'mode'=2] {'x','mode'}, dimensions={0}, use_global_device_ids=true | all-gather | bytes 1105920 | tf_op jit(solution)/shard_map/all_gather | solution.py:364
  29.4 8.0 %shard_map.70 = (f32[768,768]{1,0:T(8,128)S(1)}, f32[768,768]{1,0:T(8,128)S(1)}, bf16[2,1536,768]{2,1,0:T(8,128)(2,1)S(1)}) custom-call(s32[4]{0:T(128)S(1)} %copy-done.2, s32[128]{0:T(128)S(1)} %copy-done.3, s32[3,8]{1,0:T(4,128)S(1)} %bitcast.18, bf16[2,96,768]{2,1,0:T(8,128)(2,1)S(1)} %pad_maximum_fusion.refs_0_, ...), custom_call_target="tpu_custom_call" | custom-call | tf_op jit(solution)/shard_map/pallas_call | solution.py:301
  37.4 2.4 %shard_map.71 = (bf16[768,512]{1,0:T(8,128)(2,1)S(1)}, bf16[768,1536]{1,0:T(8,128)(2,1)S(1)}) custom-call(s32[4]{0:T(128)S(1)} %copy-done.2, s32[128]{0:T(128)S(1)} %copy-done.3, bf16[2,96,768]{2,1,0:T(8,128)(2,1)S(1)} %collective-permute-done.1.second, bf16[2,96,768]{2,1,0:T(8,128)(2,1)S(1)} %collective-permute-done.2.first, ...), custom_call_target="tpu_custom_call" | custom-call | tf_op jit(solution)/shard_map/pallas_call | solution.py:301
  39.9 0.8 %shard_map.73 = bf16[768,256]{1,0:T(8,128)(2,1)S(1)} custom-call(bf16[768,1536]{1,0:T(8,128)(2,1)S(1)} %get-tuple-element.29.left, bf16[2,1536,768]{2,1,0:T(8,128)(2,1)S(1)} %get-tuple-element.27.right, f32[768,768]{1,0:T(8,128)S(1)} %get-tuple-element.28.acc), custom_call_target="tpu_custom_call" | custom-call | tf_op jit(solution)/shard_map/pallas_call | solution.py:301
  40.7 0.6 collective-permute-start.9
  41.3 2.0 %shard_map.72.own = f32[768,768]{1,0:T(8,128)S(1)} custom-call(bf16[768,1536]{1,0:T(8,128)(2,1)S(1)} %get-tuple-element.29.left, bf16[2,1536,768]{2,1,0:T(8,128)(2,1)S(1)} %get-tuple-element.27.right, f32[768,768]{1,0:T(8,128)S(1)} %get-tuple-element.30.acc), custom_call_target="tpu_custom_call" | custom-call | tf_op jit(solution)/shard_map/pallas_call | solution.py:301
  43.3 0.9 %shard_map.74 = (bf16[296,128]{1,0:T(8,128)(2,1)S(1)}, bf16[296,128]{1,0:T(8,128)(2,1)S(1)}, bf16[296,128]{1,0:T(8,128)(2,1)S(1)}, bf16[296,128]{1,0:T(8,128)(2,...) custom-call(f32[768,768]{1,0:T(8,128)S(1)} %shard_map.72.own, ...), custom_call_target="tpu_custom_call" | custom-call | tf_op jit(solution)/shard_map/pallas_call | solution.py:301
  44.2 2.6 %collective-permute-start.10 = (bf16[296,128]{1,0:T(8,128)(2,1)S(1)}, bf16[296,128]{1,0:T(8,128)(2,1)S(1)}, u32[]{:S(2)}, u32[]{:S(2)}) collective-permute-start(bf16[296,128]{1,0:T(8,128)(2,1)S(1)} %get-tuple-element.33), channel_id=1, source_target_pairs={{0,24},{4,28},{8,16},{12,20},{16,8},{20,12},{24,0},{28,4},{1,25},{... | collective-permute-start | bytes 227336 | tf_op jit(solution)/shard_map/ppermute | solution.py:343
  46.9 3.4 %collective-permute-start.11 = (bf16[296,128]{1,0:T(8,128)(2,1)S(1)}, bf16[296,128]{1,0:T(8,128)(2,1)S(1)}, u32[]{:S(2)}, u32[]{:S(2)}) collective-permute-start(bf16[296,128]{1,0:T(8,128)(2,1)S(1)} %get-tuple-element.34), channel_id=1, source_target_pairs={{0,16},{4,20},{8,24},{12,28},{16,0},{20,4},{24,8},{28,12},{1,17},{... | collective-permute-start | bytes 227336 | tf_op jit(solution)/shard_map/ppermute | solution.py:343
  50.4 2.8 %collective-permute-start.13 = (bf16[296,128]{1,0:T(8,128)(2,1)S(1)}, bf16[296,128]{1,0:T(8,128)(2,1)S(1)}, u32[]{:S(2)}, u32[]{:S(2)}) collective-permute-start(bf16[296,128]{1,0:T(8,128)(2,1)S(1)} %get-tuple-element.36), channel_id=1, source_target_pairs={{0,28},{4,24},{8,20},{12,16},{16,12},{20,8},{24,4},{28,0},{1,29},{... | collective-permute-start | bytes 227336 | tf_op jit(solution)/shard_map/ppermute | solution.py:343
  53.2 1.4 %collective-permute-start.14 = (bf16[296,128]{1,0:T(8,128)(2,1)S(1)}, bf16[296,128]{1,0:T(8,128)(2,1)S(1)}, u32[]{:S(2)}, u32[]{:S(2)}) collective-permute-start(bf16[296,128]{1,0:T(8,128)(2,1)S(1)} %get-tuple-element.37), channel_id=1, source_target_pairs={{0,20},{4,16},{8,28},{12,24},{16,4},{20,0},{24,12},{28,8},{1,21},{... | collective-permute-start | bytes 227336 | tf_op jit(solution)/shard_map/ppermute | solution.py:343
  54.7 1.5 %collective-permute-start.15 = (bf16[296,128]{1,0:T(8,128)(2,1)S(1)}, bf16[296,128]{1,0:T(8,128)(2,1)S(1)}, u32[]{:S(2)}, u32[]{:S(2)}) collective-permute-start(bf16[296,128]{1,0:T(8,128)(2,1)S(1)} %get-tuple-element.38), channel_id=1, source_target_pairs={{0,12},{4,8},{8,4},{12,0},{16,28},{20,24},{24,20},{28,16},{1,13},{... | collective-permute-start | bytes 227336 | tf_op jit(solution)/shard_map/ppermute | solution.py:343
  56.1 2.7 %collective-permute-done.11.refs_2_ = bf16[296,128]{1,0:T(8,128)(2,1)S(1)} collective-permute-done((bf16[296,128]{1,0:T(8,128)(2,1)S(1)}, bf16[296,128]{1,0:T(8,128)(2,1)S(1)}, u32[]{:S(2)}, u32[]{:S(2)}) %collective-permute-start.11) | collective-permute-done | bytes 75808 | tf_op jit(solution)/shard_map/ppermute | solution.py:343
  58.9 1.2 %collective-permute-start.16 = (bf16[296,128]{1,0:T(8,128)(2,1)S(1)}, bf16[296,128]{1,0:T(8,128)(2,1)S(1)}, u32[]{:S(2)}, u32[]{:S(2)}) collective-permute-start(bf16[296,128]{1,0:T(8,128)(2,1)S(1)} %get-tuple-element.39), channel_id=1, source_target_pairs={{0,4},{4,0},{8,12},{12,8},{16,20},{20,16},{24,28},{28,24},{1,5},{5... | collective-permute-start | bytes 227336 | tf_op jit(solution)/shard_map/ppermute | solution.py:343
  60.1 2.7 %collective-permute-done.14.refs_5_ = bf16[296,128]{1,0:T(8,128)(2,1)S(1)} collective-permute-done((bf16[296,128]{1,0:T(8,128)(2,1)S(1)}, bf16[296,128]{1,0:T(8,128)(2,1)S(1)}, u32[]{:S(2)}, u32[]{:S(2)}) %collective-permute-start.14) | collective-permute-done | bytes 75808 | tf_op jit(solution)/shard_map/ppermute | solution.py:343
  62.7 0.8 %collective-permute-done.16.refs_7_ = bf16[296,128]{1,0:T(8,128)(2,1)S(1)} collective-permute-done((bf16[296,128]{1,0:T(8,128)(2,1)S(1)}, bf16[296,128]{1,0:T(8,128)(2,1)S(1)}, u32[]{:S(2)}, u32[]{:S(2)}) %collective-permute-start.16) | collective-permute-done | bytes 75808 | tf_op jit(solution)/shard_map/ppermute | solution.py:343
  63.6 1.6 %collective-permute-start.18 = (f32[4,32]{1,0:T(4,128)S(1)}, f32[4,32]{1,0:T(4,128)S(1)}, u32[]{:S(2)}, u32[]{:S(2)}) collective-permute-start(f32[4,32]{1,0:T(4,128)S(1)} %slice_add_fusion.own), channel_id=1, source_target_pairs={{0,1},{1,0},{2,3},{3,2},{4,5},{5,4},{6,7},{7,6},{8,9},{9,8},{10,11... | collective-permute-start | bytes 1544 | tf_op jit(solution)/shard_map/ppermute | solution.py:343
  65.2 0.3 collective-permute-start.17
  65.5 1.4 %shard_map.75 = f32[2,192,768]{2,1,0:T(8,128)} custom-call(bf16[296,128]{1,0:T(8,128)(2,1)S(1)} %get-tuple-element.32.refs_0_, bf16[296,128]{1,0:T(8,128)(2,1)S(1)} %collective-permute-done.10.refs_1_, bf16[296,128]{1,0:T(8,128)(2,1)S(1)} %collective-permute-done.11.refs_2_, bf16[296,128]{1,0:T(8,128)(2,1)S(1)} %collective-permute-done.12.refs_3_, ...), custom_call_target="tpu_custom_call" | custom-call | tf_op jit(solution)/shard_map/pallas_call | solution.py:301
  66.9 0.4 collective-permute-done.18.own_mode
  67.3 0.7 %shard_map.76 = f32[4,4,2,8]{3,2,1,0:T(2,128)} custom-call(f32[4,32]{1,0:T(4,128)S(1)} %slice_add_fusion.own, f32[4,32]{1,0:T(4,128)S(1)} %collective-permute-done.17.core, f32[4,32]{1,0:T(4,128)S(1)} %collective-permute-done.18.own_mode, f32[4,32]{1,0:T(4,128)S(1)} %collective-permute-done.19.core_mode), custom_call_target="tpu_custom_call" | custom-call | tf_op jit(solution)/shard_map/pallas_call | solution.py:301
  (32 shorter events, 0.8 us)
Async XLA Ops:
  0.6 1.0 %copy-start.4 = (bf16[2,32,12,192]{3,1,2,0:T(8,128)(2,1)S(1)}, bf16[2,32,12,192]{3,1,2,0:T(8,128)(2,1)}, u32[]{:S(2)}) copy-start(bf16[2,32,12,192]{3,1,2,0:T(8,128)(2,1)} %param.6) | copy-start | bytes 884740
  1.6 3.2 %copy-start = (bf16[2,32,12,384]{3,1,2,0:T(8,128)(2,1)S(1)}, bf16[2,32,12,384]{3,1,2,0:T(8,128)(2,1)}, u32[]{:S(2)}) copy-start(bf16[2,32,12,384]{3,1,2,0:T(8,128)(2,1)} %param.5) | copy-start | bytes 1769476
  1.8 27.5 %copy-start.1 = (s32[8,3]{0,1:T(4,128)S(1)}, s32[8,3]{0,1:T(4,128)}, u32[]{:S(2)}) copy-start(s32[8,3]{0,1:T(4,128)} %param.7) | copy-start | bytes 292
  1.8 27.5 %copy-start.2 = (s32[4]{0:T(128)S(1)}, s32[4]{0:T(128)}, u32[]{:S(2)}) copy-start(s32[4]{0:T(128)} %gammas.3) | copy-start | bytes 52
  1.9 27.5 %copy-start.3 = (s32[128]{0:T(128)S(1)}, s32[128]{0:T(128)}, u32[]{:S(2)}) copy-start(s32[128]{0:T(128)} %constant.2.clone.table) | copy-start | bytes 1540
  1.9 8.0 %collective-permute-start = (bf16[96,768]{1,0:T(8,128)(2,1)S(1)}, bf16[96,768]{1,0:T(8,128)(2,1)S(1)}, u32[]{:S(2)}, u32[]{:S(2)}) collective-permute-start(bf16[96,768]{1,0:T(8,128)(2,1)S(1)} %get-tuple-element.22.after), channel_id=1, source_target_pairs={{0,4},{4,0},{1,5},{5,1},{2,6},{6,2},{3,7},{7,3},{8,12},{12,8},{9,1... | collective-permute-start | bytes 442376 | tf_op jit(solution)/shard_map/ppermute | solution.py:343
  5.4 8.7 %collective-permute-start.5 = (bf16[96,384]{1,0:T(8,128)(2,1)S(1)}, bf16[96,384]{1,0:T(8,128)(2,1)S(1)}, u32[]{:S(2)}, u32[]{:S(2)}) collective-permute-start(bf16[96,384]{1,0:T(8,128)(2,1)S(1)} %get-tuple-element.24), channel_id=1, source_target_pairs={{0,8},{8,0},{16,24},{24,16},{1,9},{9,1},{17,25},{25,17},{2,10},{10... | collective-permute-start | bytes 221192 | tf_op jit(solution)/shard_map/ppermute | solution.py:343
  7.0 7.7 %collective-permute-start.6 = (bf16[96,384]{1,0:T(8,128)(2,1)S(1)}, bf16[96,384]{1,0:T(8,128)(2,1)S(1)}, u32[]{:S(2)}, u32[]{:S(2)}) collective-permute-start(bf16[96,384]{1,0:T(8,128)(2,1)S(1)} %get-tuple-element.25), channel_id=1, source_target_pairs={{0,16},{8,24},{16,0},{24,8},{1,17},{9,25},{17,1},{25,9},{2,18},{10... | collective-permute-start | bytes 221192 | tf_op jit(solution)/shard_map/ppermute | solution.py:343
  9.6 7.0 %collective-permute-start.7 = (bf16[96,384]{1,0:T(8,128)(2,1)S(1)}, bf16[96,384]{1,0:T(8,128)(2,1)S(1)}, u32[]{:S(2)}, u32[]{:S(2)}) collective-permute-start(bf16[96,384]{1,0:T(8,128)(2,1)S(1)} %get-tuple-element.26), channel_id=1, source_target_pairs={{0,24},{8,16},{16,8},{24,0},{1,25},{9,17},{17,9},{25,1},{2,26},{10... | collective-permute-start | bytes 221192 | tf_op jit(solution)/shard_map/ppermute | solution.py:343
  9.9 19.5 %collective-permute-start.3 = (bf16[2,96,768]{2,1,0:T(8,128)(2,1)S(1)}, bf16[2,96,768]{2,1,0:T(8,128)(2,1)S(1)}, u32[]{:S(2)}, u32[]{:S(2)}) collective-permute-start(bf16[2,96,768]{2,1,0:T(8,128)(2,1)S(1)} %pad_maximum_fusion.refs_0_), channel_id=1, source_target_pairs={{0,8},{8,0},{16,24},{24,16},{1,9},{9,1},{17,25},{25,17},{2,10},{10... | collective-permute-start | bytes 884744 | tf_op jit(solution)/shard_map/ppermute | solution.py:343
  10.6 26.7 %collective-permute-start.2 = (bf16[2,96,768]{2,1,0:T(8,128)(2,1)S(1)}, bf16[2,96,768]{2,1,0:T(8,128)(2,1)S(1)}, u32[]{:S(2)}, u32[]{:S(2)}) collective-permute-start(bf16[2,96,768]{2,1,0:T(8,128)(2,1)S(1)} %pad_maximum_fusion.refs_0_), channel_id=1, source_target_pairs={{0,16},{8,24},{16,0},{24,8},{1,17},{9,25},{17,1},{25,9},{2,18},{10... | collective-permute-start | bytes 884744 | tf_op jit(solution)/shard_map/ppermute | solution.py:343
  14.1 23.3 %collective-permute-start.1 = (bf16[2,96,768]{2,1,0:T(8,128)(2,1)S(1)}, bf16[2,96,768]{2,1,0:T(8,128)(2,1)S(1)}, u32[]{:S(2)}, u32[]{:S(2)}) collective-permute-start(bf16[2,96,768]{2,1,0:T(8,128)(2,1)S(1)} %pad_maximum_fusion.refs_0_), channel_id=1, source_target_pairs={{0,24},{8,16},{16,8},{24,0},{1,25},{9,17},{17,9},{25,1},{2,26},{10... | collective-permute-start | bytes 884744 | tf_op jit(solution)/shard_map/ppermute | solution.py:343
  14.8 14.6 %collective-permute-start.4 = (bf16[192,384]{1,0:T(8,128)(2,1)S(1)}, bf16[192,384]{1,0:T(8,128)(2,1)S(1)}, u32[]{:S(2)}, u32[]{:S(2)}) collective-permute-start(bf16[192,384]{1,0:T(8,128)(2,1)S(1)} %get-tuple-element.23.refs_2_), channel_id=1, source_target_pairs={{0,4},{4,0},{1,5},{5,1},{2,6},{6,2},{3,7},{7,3},{8,12},{12,8},{9,1... | collective-permute-start | bytes 442376 | tf_op jit(solution)/shard_map/ppermute | solution.py:343
  39.8 3.5 %collective-permute-start.8 = (bf16[768,512]{1,0:T(8,128)(2,1)S(1)}, bf16[768,512]{1,0:T(8,128)(2,1)S(1)}, u32[]{:S(2)}, u32[]{:S(2)}) collective-permute-start(bf16[768,512]{1,0:T(8,128)(2,1)S(1)} %get-tuple-element.31), channel_id=1, source_target_pairs={{0,2},{2,0},{1,3},{3,1},{4,6},{6,4},{5,7},{7,5},{8,10},{10,8},{9,1... | collective-permute-start | bytes 2359304 | tf_op jit(solution)/shard_map/ppermute | solution.py:343
  40.7 2.6 %collective-permute-start.9 = (bf16[768,256]{1,0:T(8,128)(2,1)S(1)}, bf16[768,256]{1,0:T(8,128)(2,1)S(1)}, u32[]{:S(2)}, u32[]{:S(2)}) collective-permute-start(bf16[768,256]{1,0:T(8,128)(2,1)S(1)} %shard_map.73), channel_id=1, source_target_pairs={{0,2},{2,0},{1,3},{3,1},{4,6},{6,4},{5,7},{7,5},{8,10},{10,8},{9,1... | collective-permute-start | bytes 1179656 | tf_op jit(solution)/shard_map/ppermute | solution.py:343
  44.2 10.4 %collective-permute-start.10 = (bf16[296,128]{1,0:T(8,128)(2,1)S(1)}, bf16[296,128]{1,0:T(8,128)(2,1)S(1)}, u32[]{:S(2)}, u32[]{:S(2)}) collective-permute-start(bf16[296,128]{1,0:T(8,128)(2,1)S(1)} %get-tuple-element.33), channel_id=1, source_target_pairs={{0,24},{4,28},{8,16},{12,20},{16,8},{20,12},{24,0},{28,4},{1,25},{... | collective-permute-start | bytes 227336 | tf_op jit(solution)/shard_map/ppermute | solution.py:343
  46.9 12.0 %collective-permute-start.11 = (bf16[296,128]{1,0:T(8,128)(2,1)S(1)}, bf16[296,128]{1,0:T(8,128)(2,1)S(1)}, u32[]{:S(2)}, u32[]{:S(2)}) collective-permute-start(bf16[296,128]{1,0:T(8,128)(2,1)S(1)} %get-tuple-element.34), channel_id=1, source_target_pairs={{0,16},{4,20},{8,24},{12,28},{16,0},{20,4},{24,8},{28,12},{1,17},{... | collective-permute-start | bytes 227336 | tf_op jit(solution)/shard_map/ppermute | solution.py:343
  50.3 9.8 %collective-permute-start.12 = (bf16[296,128]{1,0:T(8,128)(2,1)S(1)}, bf16[296,128]{1,0:T(8,128)(2,1)S(1)}, u32[]{:S(2)}, u32[]{:S(2)}) collective-permute-start(bf16[296,128]{1,0:T(8,128)(2,1)S(1)} %get-tuple-element.35), channel_id=1, source_target_pairs={{0,8},{4,12},{8,0},{12,4},{16,24},{20,28},{24,16},{28,20},{1,9},{5... | collective-permute-start | bytes 227336 | tf_op jit(solution)/shard_map/ppermute | solution.py:343
  50.4 9.7 %collective-permute-start.13 = (bf16[296,128]{1,0:T(8,128)(2,1)S(1)}, bf16[296,128]{1,0:T(8,128)(2,1)S(1)}, u32[]{:S(2)}, u32[]{:S(2)}) collective-permute-start(bf16[296,128]{1,0:T(8,128)(2,1)S(1)} %get-tuple-element.36), channel_id=1, source_target_pairs={{0,28},{4,24},{8,20},{12,16},{16,12},{20,8},{24,4},{28,0},{1,29},{... | collective-permute-start | bytes 227336 | tf_op jit(solution)/shard_map/ppermute | solution.py:343
  53.2 9.5 %collective-permute-start.14 = (bf16[296,128]{1,0:T(8,128)(2,1)S(1)}, bf16[296,128]{1,0:T(8,128)(2,1)S(1)}, u32[]{:S(2)}, u32[]{:S(2)}) collective-permute-start(bf16[296,128]{1,0:T(8,128)(2,1)S(1)} %get-tuple-element.37), channel_id=1, source_target_pairs={{0,20},{4,16},{8,28},{12,24},{16,4},{20,0},{24,12},{28,8},{1,21},{... | collective-permute-start | bytes 227336 | tf_op jit(solution)/shard_map/ppermute | solution.py:343
  54.7 8.1 %collective-permute-start.15 = (bf16[296,128]{1,0:T(8,128)(2,1)S(1)}, bf16[296,128]{1,0:T(8,128)(2,1)S(1)}, u32[]{:S(2)}, u32[]{:S(2)}) collective-permute-start(bf16[296,128]{1,0:T(8,128)(2,1)S(1)} %get-tuple-element.38), channel_id=1, source_target_pairs={{0,12},{4,8},{8,4},{12,0},{16,28},{20,24},{24,20},{28,16},{1,13},{... | collective-permute-start | bytes 227336 | tf_op jit(solution)/shard_map/ppermute | solution.py:343
  58.9 4.6 %collective-permute-start.16 = (bf16[296,128]{1,0:T(8,128)(2,1)S(1)}, bf16[296,128]{1,0:T(8,128)(2,1)S(1)}, u32[]{:S(2)}, u32[]{:S(2)}) collective-permute-start(bf16[296,128]{1,0:T(8,128)(2,1)S(1)} %get-tuple-element.39), channel_id=1, source_target_pairs={{0,4},{4,0},{8,12},{12,8},{16,20},{20,16},{24,28},{28,24},{1,5},{5... | collective-permute-start | bytes 227336 | tf_op jit(solution)/shard_map/ppermute | solution.py:343
  63.6 3.3 %collective-permute-start.19 = (f32[4,32]{1,0:T(4,128)S(1)}, f32[4,32]{1,0:T(4,128)S(1)}, u32[]{:S(2)}, u32[]{:S(2)}) collective-permute-start(f32[4,32]{1,0:T(4,128)S(1)} %slice_add_fusion.own), channel_id=1, source_target_pairs={{0,3},{1,2},{2,1},{3,0},{4,7},{5,6},{6,5},{7,4},{8,11},{9,10},{10,... | collective-permute-start | bytes 1544 | tf_op jit(solution)/shard_map/ppermute | solution.py:343
  63.6 3.7 %collective-permute-start.18 = (f32[4,32]{1,0:T(4,128)S(1)}, f32[4,32]{1,0:T(4,128)S(1)}, u32[]{:S(2)}, u32[]{:S(2)}) collective-permute-start(f32[4,32]{1,0:T(4,128)S(1)} %slice_add_fusion.own), channel_id=1, source_target_pairs={{0,1},{1,0},{2,3},{3,2},{4,5},{5,4},{6,7},{7,6},{8,9},{9,8},{10,11... | collective-permute-start | bytes 1544 | tf_op jit(solution)/shard_map/ppermute | solution.py:343
  65.2 2.1 %collective-permute-start.17 = (f32[4,32]{1,0:T(4,128)S(1)}, f32[4,32]{1,0:T(4,128)S(1)}, u32[]{:S(2)}, u32[]{:S(2)}) collective-permute-start(f32[4,32]{1,0:T(4,128)S(1)} %slice_add_fusion.own), channel_id=1, source_target_pairs={{0,2},{2,0},{1,3},{3,1},{4,6},{6,4},{5,7},{7,5},{8,10},{10,8},{9,1... | collective-permute-start | bytes 1544 | tf_op jit(solution)/shard_map/ppermute | solution.py:343

commit v7 on v6

--- a/solution.py
+++ b/solution.py
@@ -18,7 +18,7 @@
 F32 = jnp.float32
 
 
-ORDER = (6, 4, 2, 7, 5, 3, 1)
+ORDER = (6, 2, 4, 7, 3, 5, 1)
 COST = pl.CostEstimate(flops=2_000_000_000, bytes_accessed=8_000_000, transcendentals=0)
 
 

time: 68.1 us -> 67.9 us (level)
  transfers between devices with their start and end apart: 20 -> 20, of which waited for: 6 -> 5; matrix products, arithmetic and copies ran while one was open for 0% -> 0% of each run, Pallas kernels for 19% -> 19%
where the time goes in v7:
time: 67.9 us; the launch traced here: 67.8 us
  starting transfers between devices  28.3 us (42%)
  Pallas kernels  16.9 us (25%)
  blocking collectives  12.7 us (19%)
  waiting for transfers between devices  7.9 us (12%)
  local copies, waits for them, and re-layouts  1.01 us (1%)
  between operations  0.81 us (1%)
    ppermute x20, starting transfers between devices, swap(): lax.ppermute(x, axis, [(i, i ^ mask) for i in range(lax.axis_size(axis))])  28.3 us
    pallas_call x7, Pallas kernels, call(): pl.pallas_call(kernel, out_shape=out_shape, in_specs=[SMEM] * len(scalars...  16.2 us
    all_gather x1, blocking collectives, fast_body(): eig_all = lax.all_gather(mine, ('x', 'mode')).reshape(2, 2, 3, 96, 384)  12.7 us
    ppermute x20, waiting for transfers between devices, swap(): lax.ppermute(x, axis, [(i, i ^ mask) for i in range(lax.axis_size(axis))])  7.9 us
  transfers between devices with their start and end apart: 20, of which 5 were waited for; matrix products, arithmetic and copies ran while one was open for 0% of the time, Pallas kernels for 19%

profile of v7, /device:TPU:0, one launch (start us, length us, event | category | flops | bytes accessed | tf_op | source)
XLA Modules:
  0.0 67.8 jit_solution(7107330617421424268)
XLA Ops:
  0.6 1.0 %copy-done.4 = bf16[2,32,12,192]{3,1,2,0:T(8,128)(2,1)S(1)} copy-done((bf16[2,32,12,192]{3,1,2,0:T(8,128)(2,1)S(1)}, bf16[2,32,12,192]{3,1,2,0:T(8,128)(2,1)}, u32[]{:S(2)}) %copy-start.4) | copy-done | bytes 294936
  1.9 3.0 %collective-permute-start = (bf16[96,768]{1,0:T(8,128)(2,1)S(1)}, bf16[96,768]{1,0:T(8,128)(2,1)S(1)}, u32[]{:S(2)}, u32[]{:S(2)}) collective-permute-start(bf16[96,768]{1,0:T(8,128)(2,1)S(1)} %get-tuple-element.22.after), channel_id=1, source_target_pairs={{0,4},{4,0},{1,5},{5,1},{2,6},{6,2},{3,7},{7,3},{8,12},{12,8},{9,1... | collective-permute-start | bytes 442376 | tf_op jit(solution)/shard_map/ppermute | solution.py:343
  4.9 0.5 shard_map.69
  5.4 1.6 %collective-permute-start.5 = (bf16[96,384]{1,0:T(8,128)(2,1)S(1)}, bf16[96,384]{1,0:T(8,128)(2,1)S(1)}, u32[]{:S(2)}, u32[]{:S(2)}) collective-permute-start(bf16[96,384]{1,0:T(8,128)(2,1)S(1)} %get-tuple-element.24), channel_id=1, source_target_pairs={{0,8},{8,0},{16,24},{24,16},{1,9},{9,1},{17,25},{25,17},{2,10},{10... | collective-permute-start | bytes 221192 | tf_op jit(solution)/shard_map/ppermute | solution.py:343
  7.0 2.6 %collective-permute-start.6 = (bf16[96,384]{1,0:T(8,128)(2,1)S(1)}, bf16[96,384]{1,0:T(8,128)(2,1)S(1)}, u32[]{:S(2)}, u32[]{:S(2)}) collective-permute-start(bf16[96,384]{1,0:T(8,128)(2,1)S(1)} %get-tuple-element.25), channel_id=1, source_target_pairs={{0,16},{8,24},{16,0},{24,8},{1,17},{9,25},{17,1},{25,9},{2,18},{10... | collective-permute-start | bytes 221192 | tf_op jit(solution)/shard_map/ppermute | solution.py:343
  9.6 0.2 collective-permute-start.7
  9.9 0.8 %collective-permute-start.3 = (bf16[2,96,768]{2,1,0:T(8,128)(2,1)S(1)}, bf16[2,96,768]{2,1,0:T(8,128)(2,1)S(1)}, u32[]{:S(2)}, u32[]{:S(2)}) collective-permute-start(bf16[2,96,768]{2,1,0:T(8,128)(2,1)S(1)} %pad_maximum_fusion.refs_0_), channel_id=1, source_target_pairs={{0,8},{8,0},{16,24},{24,16},{1,9},{9,1},{17,25},{25,17},{2,10},{10... | collective-permute-start | bytes 884744 | tf_op jit(solution)/shard_map/ppermute | solution.py:343
  10.6 3.5 %collective-permute-start.2 = (bf16[2,96,768]{2,1,0:T(8,128)(2,1)S(1)}, bf16[2,96,768]{2,1,0:T(8,128)(2,1)S(1)}, u32[]{:S(2)}, u32[]{:S(2)}) collective-permute-start(bf16[2,96,768]{2,1,0:T(8,128)(2,1)S(1)} %pad_maximum_fusion.refs_0_), channel_id=1, source_target_pairs={{0,16},{8,24},{16,0},{24,8},{1,17},{9,25},{17,1},{25,9},{2,18},{10... | collective-permute-start | bytes 884744 | tf_op jit(solution)/shard_map/ppermute | solution.py:343
  14.1 0.2 collective-permute-start.1
  14.3 0.4 collective-permute-done.6
  14.8 1.0 %collective-permute-start.4 = (bf16[192,384]{1,0:T(8,128)(2,1)S(1)}, bf16[192,384]{1,0:T(8,128)(2,1)S(1)}, u32[]{:S(2)}, u32[]{:S(2)}) collective-permute-start(bf16[192,384]{1,0:T(8,128)(2,1)S(1)} %get-tuple-element.23.refs_2_), channel_id=1, source_target_pairs={{0,4},{4,0},{1,5},{5,1},{2,6},{6,2},{3,7},{7,3},{8,12},{12,8},{9,1... | collective-permute-start | bytes 442376 | tf_op jit(solution)/shard_map/ppermute | solution.py:343
  15.7 0.9 %collective-permute-done.7 = bf16[96,384]{1,0:T(8,128)(2,1)S(1)} collective-permute-done((bf16[96,384]{1,0:T(8,128)(2,1)S(1)}, bf16[96,384]{1,0:T(8,128)(2,1)S(1)}, u32[]{:S(2)}, u32[]{:S(2)}) %collective-permute-start.7) | collective-permute-done | bytes 73760 | tf_op jit(solution)/shard_map/ppermute | solution.py:343
  16.7 12.7 %all-gather = bf16[12,96,384]{2,1,0:T(8,128)(2,1)S(1)} all-gather(bf16[3,96,384]{2,1,0:T(8,128)(2,1)S(1)} %pad_maximum_fusion.1), channel_id=2, replica_groups=mesh['z'=4,'x'=2,'core'=2,'mode'=2] {'x','mode'}, dimensions={0}, use_global_device_ids=true | all-gather | bytes 1105920 | tf_op jit(solution)/shard_map/all_gather | solution.py:364
  29.4 8.0 %shard_map.70 = (f32[768,768]{1,0:T(8,128)S(1)}, f32[768,768]{1,0:T(8,128)S(1)}, bf16[2,1536,768]{2,1,0:T(8,128)(2,1)S(1)}) custom-call(s32[4]{0:T(128)S(1)} %copy-done.2, s32[128]{0:T(128)S(1)} %copy-done.3, s32[3,8]{1,0:T(4,128)S(1)} %bitcast.18, bf16[2,96,768]{2,1,0:T(8,128)(2,1)S(1)} %pad_maximum_fusion.refs_0_, ...), custom_call_target="tpu_custom_call" | custom-call | tf_op jit(solution)/shard_map/pallas_call | solution.py:301
  37.4 2.4 %shard_map.71 = (bf16[768,512]{1,0:T(8,128)(2,1)S(1)}, bf16[768,1536]{1,0:T(8,128)(2,1)S(1)}) custom-call(s32[4]{0:T(128)S(1)} %copy-done.2, s32[128]{0:T(128)S(1)} %copy-done.3, bf16[2,96,768]{2,1,0:T(8,128)(2,1)S(1)} %collective-permute-done.1.second, bf16[2,96,768]{2,1,0:T(8,128)(2,1)S(1)} %collective-permute-done.2.first, ...), custom_call_target="tpu_custom_call" | custom-call | tf_op jit(solution)/shard_map/pallas_call | solution.py:301
  39.9 0.8 %shard_map.73 = bf16[768,256]{1,0:T(8,128)(2,1)S(1)} custom-call(bf16[768,1536]{1,0:T(8,128)(2,1)S(1)} %get-tuple-element.29.left, bf16[2,1536,768]{2,1,0:T(8,128)(2,1)S(1)} %get-tuple-element.27.right, f32[768,768]{1,0:T(8,128)S(1)} %get-tuple-element.28.acc), custom_call_target="tpu_custom_call" | custom-call | tf_op jit(solution)/shard_map/pallas_call | solution.py:301
  40.7 0.6 collective-permute-start.9
  41.3 2.0 %shard_map.72.own = f32[768,768]{1,0:T(8,128)S(1)} custom-call(bf16[768,1536]{1,0:T(8,128)(2,1)S(1)} %get-tuple-element.29.left, bf16[2,1536,768]{2,1,0:T(8,128)(2,1)S(1)} %get-tuple-element.27.right, f32[768,768]{1,0:T(8,128)S(1)} %get-tuple-element.30.acc), custom_call_target="tpu_custom_call" | custom-call | tf_op jit(solution)/shard_map/pallas_call | solution.py:301
  43.3 0.9 %shard_map.74 = (bf16[296,128]{1,0:T(8,128)(2,1)S(1)}, bf16[296,128]{1,0:T(8,128)(2,1)S(1)}, bf16[296,128]{1,0:T(8,128)(2,1)S(1)}, bf16[296,128]{1,0:T(8,128)(2,...) custom-call(f32[768,768]{1,0:T(8,128)S(1)} %shard_map.72.own, ...), custom_call_target="tpu_custom_call" | custom-call | tf_op jit(solution)/shard_map/pallas_call | solution.py:301
  44.2 2.7 %collective-permute-start.10 = (bf16[296,128]{1,0:T(8,128)(2,1)S(1)}, bf16[296,128]{1,0:T(8,128)(2,1)S(1)}, u32[]{:S(2)}, u32[]{:S(2)}) collective-permute-start(bf16[296,128]{1,0:T(8,128)(2,1)S(1)} %get-tuple-element.33), channel_id=1, source_target_pairs={{0,24},{4,28},{8,16},{12,20},{16,8},{20,12},{24,0},{28,4},{1,25},{... | collective-permute-start | bytes 227336 | tf_op jit(solution)/shard_map/ppermute | solution.py:343
  46.9 3.5 %collective-permute-start.11 = (bf16[296,128]{1,0:T(8,128)(2,1)S(1)}, bf16[296,128]{1,0:T(8,128)(2,1)S(1)}, u32[]{:S(2)}, u32[]{:S(2)}) collective-permute-start(bf16[296,128]{1,0:T(8,128)(2,1)S(1)} %get-tuple-element.34), channel_id=1, source_target_pairs={{0,8},{4,12},{8,0},{12,4},{16,24},{20,28},{24,16},{28,20},{1,9},{5... | collective-permute-start | bytes 227336 | tf_op jit(solution)/shard_map/ppermute | solution.py:343
  50.4 2.8 %collective-permute-start.13 = (bf16[296,128]{1,0:T(8,128)(2,1)S(1)}, bf16[296,128]{1,0:T(8,128)(2,1)S(1)}, u32[]{:S(2)}, u32[]{:S(2)}) collective-permute-start(bf16[296,128]{1,0:T(8,128)(2,1)S(1)} %get-tuple-element.36), channel_id=1, source_target_pairs={{0,28},{4,24},{8,20},{12,16},{16,12},{20,8},{24,4},{28,0},{1,29},{... | collective-permute-start | bytes 227336 | tf_op jit(solution)/shard_map/ppermute | solution.py:343
  53.2 1.6 %collective-permute-start.14 = (bf16[296,128]{1,0:T(8,128)(2,1)S(1)}, bf16[296,128]{1,0:T(8,128)(2,1)S(1)}, u32[]{:S(2)}, u32[]{:S(2)}) collective-permute-start(bf16[296,128]{1,0:T(8,128)(2,1)S(1)} %get-tuple-element.37), channel_id=1, source_target_pairs={{0,12},{4,8},{8,4},{12,0},{16,28},{20,24},{24,20},{28,16},{1,13},{... | collective-permute-start | bytes 227336 | tf_op jit(solution)/shard_map/ppermute | solution.py:343
  54.8 1.4 %collective-permute-start.15 = (bf16[296,128]{1,0:T(8,128)(2,1)S(1)}, bf16[296,128]{1,0:T(8,128)(2,1)S(1)}, u32[]{:S(2)}, u32[]{:S(2)}) collective-permute-start(bf16[296,128]{1,0:T(8,128)(2,1)S(1)} %get-tuple-element.38), channel_id=1, source_target_pairs={{0,20},{4,16},{8,28},{12,24},{16,4},{20,0},{24,12},{28,8},{1,21},{... | collective-permute-start | bytes 227336 | tf_op jit(solution)/shard_map/ppermute | solution.py:343
  56.2 1.0 %collective-permute-start.16 = (bf16[296,128]{1,0:T(8,128)(2,1)S(1)}, bf16[296,128]{1,0:T(8,128)(2,1)S(1)}, u32[]{:S(2)}, u32[]{:S(2)}) collective-permute-start(bf16[296,128]{1,0:T(8,128)(2,1)S(1)} %get-tuple-element.39), channel_id=1, source_target_pairs={{0,4},{4,0},{8,12},{12,8},{16,20},{20,16},{24,28},{28,24},{1,5},{5... | collective-permute-start | bytes 227336 | tf_op jit(solution)/shard_map/ppermute | solution.py:343
  57.1 2.6 %collective-permute-done.12.refs_3_ = bf16[296,128]{1,0:T(8,128)(2,1)S(1)} collective-permute-done((bf16[296,128]{1,0:T(8,128)(2,1)S(1)}, bf16[296,128]{1,0:T(8,128)(2,1)S(1)}, u32[]{:S(2)}, u32[]{:S(2)}) %collective-permute-start.12) | collective-permute-done | bytes 75808 | tf_op jit(solution)/shard_map/ppermute | solution.py:343
  59.7 3.6 %collective-permute-done.15.refs_6_ = bf16[296,128]{1,0:T(8,128)(2,1)S(1)} collective-permute-done((bf16[296,128]{1,0:T(8,128)(2,1)S(1)}, bf16[296,128]{1,0:T(8,128)(2,1)S(1)}, u32[]{:S(2)}, u32[]{:S(2)}) %collective-permute-start.15) | collective-permute-done | bytes 75808 | tf_op jit(solution)/shard_map/ppermute | solution.py:343
  63.4 1.6 %collective-permute-start.18 = (f32[4,32]{1,0:T(4,128)S(1)}, f32[4,32]{1,0:T(4,128)S(1)}, u32[]{:S(2)}, u32[]{:S(2)}) collective-permute-start(f32[4,32]{1,0:T(4,128)S(1)} %slice_add_fusion.own), channel_id=1, source_target_pairs={{0,1},{1,0},{2,3},{3,2},{4,5},{5,4},{6,7},{7,6},{8,9},{9,8},{10,11... | collective-permute-start | bytes 1544 | tf_op jit(solution)/shard_map/ppermute | solution.py:343
  65.0 0.3 collective-permute-start.17
  65.3 1.4 %shard_map.75 = f32[2,192,768]{2,1,0:T(8,128)} custom-call(bf16[296,128]{1,0:T(8,128)(2,1)S(1)} %get-tuple-element.32.refs_0_, bf16[296,128]{1,0:T(8,128)(2,1)S(1)} %collective-permute-done.10.refs_1_, bf16[296,128]{1,0:T(8,128)(2,1)S(1)} %collective-permute-done.11.refs_2_, bf16[296,128]{1,0:T(8,128)(2,1)S(1)} %collective-permute-done.12.refs_3_, ...), custom_call_target="tpu_custom_call" | custom-call | tf_op jit(solution)/shard_map/pallas_call | solution.py:301
  66.7 0.4 collective-permute-done.18.own_mode
  67.1 0.7 %shard_map.76 = f32[4,4,2,8]{3,2,1,0:T(2,128)} custom-call(f32[4,32]{1,0:T(4,128)S(1)} %slice_add_fusion.own, f32[4,32]{1,0:T(4,128)S(1)} %collective-permute-done.17.core, f32[4,32]{1,0:T(4,128)S(1)} %collective-permute-done.18.own_mode, f32[4,32]{1,0:T(4,128)S(1)} %collective-permute-done.19.core_mode), custom_call_target="tpu_custom_call" | custom-call | tf_op jit(solution)/shard_map/pallas_call | solution.py:301
  (32 shorter events, 0.5 us)
Async XLA Ops:
  0.6 1.0 %copy-start.4 = (bf16[2,32,12,192]{3,1,2,0:T(8,128)(2,1)S(1)}, bf16[2,32,12,192]{3,1,2,0:T(8,128)(2,1)}, u32[]{:S(2)}) copy-start(bf16[2,32,12,192]{3,1,2,0:T(8,128)(2,1)} %param.6) | copy-start | bytes 884740
  1.6 3.2 %copy-start = (bf16[2,32,12,384]{3,1,2,0:T(8,128)(2,1)S(1)}, bf16[2,32,12,384]{3,1,2,0:T(8,128)(2,1)}, u32[]{:S(2)}) copy-start(bf16[2,32,12,384]{3,1,2,0:T(8,128)(2,1)} %param.5) | copy-start | bytes 1769476
  1.8 27.5 %copy-start.1 = (s32[8,3]{0,1:T(4,128)S(1)}, s32[8,3]{0,1:T(4,128)}, u32[]{:S(2)}) copy-start(s32[8,3]{0,1:T(4,128)} %param.7) | copy-start | bytes 292
  1.8 27.5 %copy-start.2 = (s32[4]{0:T(128)S(1)}, s32[4]{0:T(128)}, u32[]{:S(2)}) copy-start(s32[4]{0:T(128)} %gammas.3) | copy-start | bytes 52
  1.9 27.5 %copy-start.3 = (s32[128]{0:T(128)S(1)}, s32[128]{0:T(128)}, u32[]{:S(2)}) copy-start(s32[128]{0:T(128)} %constant.2.clone.table) | copy-start | bytes 1540
  1.9 8.0 %collective-permute-start = (bf16[96,768]{1,0:T(8,128)(2,1)S(1)}, bf16[96,768]{1,0:T(8,128)(2,1)S(1)}, u32[]{:S(2)}, u32[]{:S(2)}) collective-permute-start(bf16[96,768]{1,0:T(8,128)(2,1)S(1)} %get-tuple-element.22.after), channel_id=1, source_target_pairs={{0,4},{4,0},{1,5},{5,1},{2,6},{6,2},{3,7},{7,3},{8,12},{12,8},{9,1... | collective-permute-start | bytes 442376 | tf_op jit(solution)/shard_map/ppermute | solution.py:343
  5.4 8.7 %collective-permute-start.5 = (bf16[96,384]{1,0:T(8,128)(2,1)S(1)}, bf16[96,384]{1,0:T(8,128)(2,1)S(1)}, u32[]{:S(2)}, u32[]{:S(2)}) collective-permute-start(bf16[96,384]{1,0:T(8,128)(2,1)S(1)} %get-tuple-element.24), channel_id=1, source_target_pairs={{0,8},{8,0},{16,24},{24,16},{1,9},{9,1},{17,25},{25,17},{2,10},{10... | collective-permute-start | bytes 221192 | tf_op jit(solution)/shard_map/ppermute | solution.py:343
  7.0 7.7 %collective-permute-start.6 = (bf16[96,384]{1,0:T(8,128)(2,1)S(1)}, bf16[96,384]{1,0:T(8,128)(2,1)S(1)}, u32[]{:S(2)}, u32[]{:S(2)}) collective-permute-start(bf16[96,384]{1,0:T(8,128)(2,1)S(1)} %get-tuple-element.25), channel_id=1, source_target_pairs={{0,16},{8,24},{16,0},{24,8},{1,17},{9,25},{17,1},{25,9},{2,18},{10... | collective-permute-start | bytes 221192 | tf_op jit(solution)/shard_map/ppermute | solution.py:343
  9.6 7.0 %collective-permute-start.7 = (bf16[96,384]{1,0:T(8,128)(2,1)S(1)}, bf16[96,384]{1,0:T(8,128)(2,1)S(1)}, u32[]{:S(2)}, u32[]{:S(2)}) collective-permute-start(bf16[96,384]{1,0:T(8,128)(2,1)S(1)} %get-tuple-element.26), channel_id=1, source_target_pairs={{0,24},{8,16},{16,8},{24,0},{1,25},{9,17},{17,9},{25,1},{2,26},{10... | collective-permute-start | bytes 221192 | tf_op jit(solution)/shard_map/ppermute | solution.py:343
  9.9 19.5 %collective-permute-start.3 = (bf16[2,96,768]{2,1,0:T(8,128)(2,1)S(1)}, bf16[2,96,768]{2,1,0:T(8,128)(2,1)S(1)}, u32[]{:S(2)}, u32[]{:S(2)}) collective-permute-start(bf16[2,96,768]{2,1,0:T(8,128)(2,1)S(1)} %pad_maximum_fusion.refs_0_), channel_id=1, source_target_pairs={{0,8},{8,0},{16,24},{24,16},{1,9},{9,1},{17,25},{25,17},{2,10},{10... | collective-permute-start | bytes 884744 | tf_op jit(solution)/shard_map/ppermute | solution.py:343
  10.6 26.7 %collective-permute-start.2 = (bf16[2,96,768]{2,1,0:T(8,128)(2,1)S(1)}, bf16[2,96,768]{2,1,0:T(8,128)(2,1)S(1)}, u32[]{:S(2)}, u32[]{:S(2)}) collective-permute-start(bf16[2,96,768]{2,1,0:T(8,128)(2,1)S(1)} %pad_maximum_fusion.refs_0_), channel_id=1, source_target_pairs={{0,16},{8,24},{16,0},{24,8},{1,17},{9,25},{17,1},{25,9},{2,18},{10... | collective-permute-start | bytes 884744 | tf_op jit(solution)/shard_map/ppermute | solution.py:343
  14.1 23.3 %collective-permute-start.1 = (bf16[2,96,768]{2,1,0:T(8,128)(2,1)S(1)}, bf16[2,96,768]{2,1,0:T(8,128)(2,1)S(1)}, u32[]{:S(2)}, u32[]{:S(2)}) collective-permute-start(bf16[2,96,768]{2,1,0:T(8,128)(2,1)S(1)} %pad_maximum_fusion.refs_0_), channel_id=1, source_target_pairs={{0,24},{8,16},{16,8},{24,0},{1,25},{9,17},{17,9},{25,1},{2,26},{10... | collective-permute-start | bytes 884744 | tf_op jit(solution)/shard_map/ppermute | solution.py:343
  14.8 14.6 %collective-permute-start.4 = (bf16[192,384]{1,0:T(8,128)(2,1)S(1)}, bf16[192,384]{1,0:T(8,128)(2,1)S(1)}, u32[]{:S(2)}, u32[]{:S(2)}) collective-permute-start(bf16[192,384]{1,0:T(8,128)(2,1)S(1)} %get-tuple-element.23.refs_2_), channel_id=1, source_target_pairs={{0,4},{4,0},{1,5},{5,1},{2,6},{6,2},{3,7},{7,3},{8,12},{12,8},{9,1... | collective-permute-start | bytes 442376 | tf_op jit(solution)/shard_map/ppermute | solution.py:343
  39.9 3.5 %collective-permute-start.8 = (bf16[768,512]{1,0:T(8,128)(2,1)S(1)}, bf16[768,512]{1,0:T(8,128)(2,1)S(1)}, u32[]{:S(2)}, u32[]{:S(2)}) collective-permute-start(bf16[768,512]{1,0:T(8,128)(2,1)S(1)} %get-tuple-element.31), channel_id=1, source_target_pairs={{0,2},{2,0},{1,3},{3,1},{4,6},{6,4},{5,7},{7,5},{8,10},{10,8},{9,1... | collective-permute-start | bytes 2359304 | tf_op jit(solution)/shard_map/ppermute | solution.py:343
  40.7 2.6 %collective-permute-start.9 = (bf16[768,256]{1,0:T(8,128)(2,1)S(1)}, bf16[768,256]{1,0:T(8,128)(2,1)S(1)}, u32[]{:S(2)}, u32[]{:S(2)}) collective-permute-start(bf16[768,256]{1,0:T(8,128)(2,1)S(1)} %shard_map.73), channel_id=1, source_target_pairs={{0,2},{2,0},{1,3},{3,1},{4,6},{6,4},{5,7},{7,5},{8,10},{10,8},{9,1... | collective-permute-start | bytes 1179656 | tf_op jit(solution)/shard_map/ppermute | solution.py:343
  44.2 10.5 %collective-permute-start.10 = (bf16[296,128]{1,0:T(8,128)(2,1)S(1)}, bf16[296,128]{1,0:T(8,128)(2,1)S(1)}, u32[]{:S(2)}, u32[]{:S(2)}) collective-permute-start(bf16[296,128]{1,0:T(8,128)(2,1)S(1)} %get-tuple-element.33), channel_id=1, source_target_pairs={{0,24},{4,28},{8,16},{12,20},{16,8},{20,12},{24,0},{28,4},{1,25},{... | collective-permute-start | bytes 227336 | tf_op jit(solution)/shard_map/ppermute | solution.py:343
  46.9 9.3 %collective-permute-start.11 = (bf16[296,128]{1,0:T(8,128)(2,1)S(1)}, bf16[296,128]{1,0:T(8,128)(2,1)S(1)}, u32[]{:S(2)}, u32[]{:S(2)}) collective-permute-start(bf16[296,128]{1,0:T(8,128)(2,1)S(1)} %get-tuple-element.34), channel_id=1, source_target_pairs={{0,8},{4,12},{8,0},{12,4},{16,24},{20,28},{24,16},{28,20},{1,9},{5... | collective-permute-start | bytes 227336 | tf_op jit(solution)/shard_map/ppermute | solution.py:343
  50.4 9.3 %collective-permute-start.12 = (bf16[296,128]{1,0:T(8,128)(2,1)S(1)}, bf16[296,128]{1,0:T(8,128)(2,1)S(1)}, u32[]{:S(2)}, u32[]{:S(2)}) collective-permute-start(bf16[296,128]{1,0:T(8,128)(2,1)S(1)} %get-tuple-element.35), channel_id=1, source_target_pairs={{0,16},{4,20},{8,24},{12,28},{16,0},{20,4},{24,8},{28,12},{1,17},{... | collective-permute-start | bytes 227336 | tf_op jit(solution)/shard_map/ppermute | solution.py:343
  50.4 9.3 %collective-permute-start.13 = (bf16[296,128]{1,0:T(8,128)(2,1)S(1)}, bf16[296,128]{1,0:T(8,128)(2,1)S(1)}, u32[]{:S(2)}, u32[]{:S(2)}) collective-permute-start(bf16[296,128]{1,0:T(8,128)(2,1)S(1)} %get-tuple-element.36), channel_id=1, source_target_pairs={{0,28},{4,24},{8,20},{12,16},{16,12},{20,8},{24,4},{28,0},{1,29},{... | collective-permute-start | bytes 227336 | tf_op jit(solution)/shard_map/ppermute | solution.py:343
  53.2 6.5 %collective-permute-start.14 = (bf16[296,128]{1,0:T(8,128)(2,1)S(1)}, bf16[296,128]{1,0:T(8,128)(2,1)S(1)}, u32[]{:S(2)}, u32[]{:S(2)}) collective-permute-start(bf16[296,128]{1,0:T(8,128)(2,1)S(1)} %get-tuple-element.37), channel_id=1, source_target_pairs={{0,12},{4,8},{8,4},{12,0},{16,28},{20,24},{24,20},{28,16},{1,13},{... | collective-permute-start | bytes 227336 | tf_op jit(solution)/shard_map/ppermute | solution.py:343
  54.8 8.5 %collective-permute-start.15 = (bf16[296,128]{1,0:T(8,128)(2,1)S(1)}, bf16[296,128]{1,0:T(8,128)(2,1)S(1)}, u32[]{:S(2)}, u32[]{:S(2)}) collective-permute-start(bf16[296,128]{1,0:T(8,128)(2,1)S(1)} %get-tuple-element.38), channel_id=1, source_target_pairs={{0,20},{4,16},{8,28},{12,24},{16,4},{20,0},{24,12},{28,8},{1,21},{... | collective-permute-start | bytes 227336 | tf_op jit(solution)/shard_map/ppermute | solution.py:343
  56.2 7.2 %collective-permute-start.16 = (bf16[296,128]{1,0:T(8,128)(2,1)S(1)}, bf16[296,128]{1,0:T(8,128)(2,1)S(1)}, u32[]{:S(2)}, u32[]{:S(2)}) collective-permute-start(bf16[296,128]{1,0:T(8,128)(2,1)S(1)} %get-tuple-element.39), channel_id=1, source_target_pairs={{0,4},{4,0},{8,12},{12,8},{16,20},{20,16},{24,28},{28,24},{1,5},{5... | collective-permute-start | bytes 227336 | tf_op jit(solution)/shard_map/ppermute | solution.py:343
  63.4 3.3 %collective-permute-start.19 = (f32[4,32]{1,0:T(4,128)S(1)}, f32[4,32]{1,0:T(4,128)S(1)}, u32[]{:S(2)}, u32[]{:S(2)}) collective-permute-start(f32[4,32]{1,0:T(4,128)S(1)} %slice_add_fusion.own), channel_id=1, source_target_pairs={{0,3},{1,2},{2,1},{3,0},{4,7},{5,6},{6,5},{7,4},{8,11},{9,10},{10,... | collective-permute-start | bytes 1544 | tf_op jit(solution)/shard_map/ppermute | solution.py:343
  63.4 3.7 %collective-permute-start.18 = (f32[4,32]{1,0:T(4,128)S(1)}, f32[4,32]{1,0:T(4,128)S(1)}, u32[]{:S(2)}, u32[]{:S(2)}) collective-permute-start(f32[4,32]{1,0:T(4,128)S(1)} %slice_add_fusion.own), channel_id=1, source_target_pairs={{0,1},{1,0},{2,3},{3,2},{4,5},{5,4},{6,7},{7,6},{8,9},{9,8},{10,11... | collective-permute-start | bytes 1544 | tf_op jit(solution)/shard_map/ppermute | solution.py:343
  65.0 2.1 %collective-permute-start.17 = (f32[4,32]{1,0:T(4,128)S(1)}, f32[4,32]{1,0:T(4,128)S(1)}, u32[]{:S(2)}, u32[]{:S(2)}) collective-permute-start(f32[4,32]{1,0:T(4,128)S(1)} %slice_add_fusion.own), channel_id=1, source_target_pairs={{0,2},{2,0},{1,3},{3,1},{4,6},{6,4},{5,7},{7,5},{8,10},{10,8},{9,1... | collective-permute-start | bytes 1544 | tf_op jit(solution)/shard_map/ppermute | solution.py:343
